TPU v7x, 32 devices: a whole 2x2x4 slice. The times are simulated.
32 devices in a mesh: grp: 4 (over z), dev: 8 (over y, x, core).
Axes of the slice: x: 2, y: 2, z: 4, core: 2. Of those that a mesh axis runs over, the one named last changes fastest.
Arguments:
- orbitals: bfloat16 [64, 48, 2304], P(('grp', 'dev')), may hold values from -6 to 6
- offsets: int32 [64, 3], P(('grp', 'dev')), may hold values from 0 to 23
- pick: int32 [4, 8, 4], P('grp'), may hold values from 0 to 1
- pair_local: int32 [4, 8, 2], P('grp', 'dev'), may hold values from 0 to 1
- pair_source: int32 [4, 8, 2], P('grp', 'dev'), may hold values from 0 to 3, as said below
- pair_count: int32 [4, 8, 1], P('grp', 'dev'), may hold values from 1 to 2, as said below
Outputs:
- exchange_action: float32 [64, 110592], P('grp', 'dev')
Inputs may be any that keep to these rules, and one draw needn't show every extreme that they name: pair_source[g, d, p] is never g; the two slots of one device's list name different groups. Only the first pair_count[g, d, 0] slots of a device's lists are pairs; some device lists exactly 2.
All inputs are finite; a program needn't handle non-finite values.
Results may differ from a plain program's by a relative error of at most 0.002.
Values may be sent and summed in bfloat16 or wider, within the bound.
No kernel may reach another device: no remote copies, remote signals or barrier semaphores. Data moves between devices by JAX's collectives and lax.ppermute only.
A program may use at most 64 MiB of HBM per device.

v0:
```python
import math

import jax
import jax.numpy as jnp
from jax import lax
from jax.sharding import PartitionSpec as P


def tables(box_side):
    freq = jnp.arange(box_side, dtype=jnp.int32)
    angle_step = math.pi / (box_side + 1)
    phase = (freq[:, None] + 1) * (freq[None, :] + 1) % (2 * (box_side + 1))
    sine_table = math.sqrt(2.0 / (box_side + 1)) * jnp.sin(angle_step * phase.astype(jnp.float32))
    modes = 2.0 - 2.0 * jnp.cos(angle_step * (freq.astype(jnp.float32) + 1.0))
    eigen_sum = modes[:, None, None] + modes[None, :, None] + modes[None, None, :]
    return (sine_table, eigen_sum.reshape(box_side, box_side * box_side))


def turn(matrix, a_field, box_side):
    product = jnp.dot(
        matrix, a_field, preferred_element_type=jnp.float32, precision=lax.Precision.HIGHEST
    )
    return (
        product.reshape(box_side, box_side, box_side)
        .transpose(1, 2, 0)
        .reshape(box_side, box_side * box_side)
    )


def shift_box(a_field, offset_gap, direction, box_side):
    margin = box_side // 2
    cube = a_field.reshape(box_side, box_side, box_side)
    padded = jnp.pad(cube, margin)
    starts = [
        (margin + direction * offset_gap[which_axis]).astype(jnp.int32) for which_axis in range(3)
    ]
    piece = lax.dynamic_slice(padded, starts, (box_side, box_side, box_side))
    return piece.reshape(box_side, box_side * box_side)


def pair_terms(phi_i, phi_j, offset_gap, sine_table, eigen_sum):
    box_side = phi_i.shape[0]
    moved = shift_box(phi_j, offset_gap, 1, box_side)
    moved_wide = moved.astype(jnp.float32)
    own_wide = phi_i.astype(jnp.float32)
    spectrum = own_wide * moved_wide
    for repeat in range(3):
        spectrum = turn(sine_table, spectrum, box_side)
    spectrum = spectrum / eigen_sum
    for repeat in range(3):
        spectrum = turn(sine_table, spectrum, box_side)
    own_term = spectrum * moved_wide
    backward = shift_box(spectrum * own_wide, offset_gap, -1, box_side)
    return (own_term, backward)


def body(orbitals, offsets, pick, pair_local, pair_source, pair_count):
    box_side = orbitals.shape[1]
    box_cells = box_side * box_side * box_side
    orb_count = orbitals.shape[0]
    slot_total = pair_local.shape[2]
    group_count = lax.axis_size("grp")
    own_member = lax.axis_index("dev")
    group_pick = pick[0]
    my_pick = lax.dynamic_index_in_dim(group_pick, own_member, 0, keepdims=False)
    outgoing = jnp.take(orbitals, my_pick, axis=0)
    outgoing_offs = jnp.take(offsets, my_pick, axis=0)
    boxes, box_offs = (
        lax.all_to_all(outgoing, "grp", split_axis=0, concat_axis=0, tiled=True),
        lax.all_to_all(outgoing_offs, "grp", split_axis=0, concat_axis=0, tiled=True),
    )
    sine_table, eigen_sum = tables(box_side)
    listed = pair_count[0, 0, 0]
    own_slots = pair_local[0, 0]
    src_slots = pair_source[0, 0]

    def one_pair(pair_index, state_pair):
        own_sum, returned = state_pair
        own_slot = own_slots[pair_index]
        src_slot = src_slots[pair_index]
        phi_i = lax.dynamic_index_in_dim(orbitals, own_slot, 0, keepdims=False)
        phi_j = lax.dynamic_index_in_dim(boxes, src_slot, 0, keepdims=False)
        offset_gap = lax.dynamic_index_in_dim(
            offsets, own_slot, 0, keepdims=False
        ) - lax.dynamic_index_in_dim(box_offs, src_slot, 0, keepdims=False)
        own_term, backward = pair_terms(phi_i, phi_j, offset_gap, sine_table, eigen_sum)
        is_live = (pair_index < listed).astype(jnp.float32)
        return (
            own_sum.at[own_slot].add(is_live * own_term),
            returned.at[src_slot].add(is_live * backward),
        )

    start = (
        jnp.zeros((orb_count, box_side, box_side * box_side), jnp.float32),
        jnp.zeros((group_count, box_side, box_side * box_side), jnp.float32),
    )
    own_sum, returned = lax.fori_loop(0, slot_total, one_pair, start)
    partial_value = returned.astype(jnp.bfloat16)
    orb_range = jnp.arange(orb_count, dtype=jnp.int32)
    back_parts = lax.all_to_all(partial_value, "grp", split_axis=0, concat_axis=0, tiled=True)
    chooser = (my_pick[:, None] == orb_range[None, :]).astype(jnp.bfloat16)
    gathered = jnp.einsum(
        "ga,gc->ac",
        chooser,
        back_parts.reshape(group_count, box_cells),
        preferred_element_type=jnp.float32,
    )
    whole = own_sum.reshape(orb_count, box_cells) + gathered
    return lax.all_to_all(whole, "dev", split_axis=1, concat_axis=0, tiled=True)


def solution(mesh):
    return jax.shard_map(
        body,
        mesh=mesh,
        in_specs=(
            P(("grp", "dev"), None, None),
            P(("grp", "dev"), None),
            P("grp", None, None),
            P("grp", "dev", None),
            P("grp", "dev", None),
            P("grp", "dev", None),
        ),
        out_specs=P("grp", "dev"),
        check_vma=False,
    )
```

profile of v0, /device:TPU:0, one launch (start us, length us, event | category | flops | bytes accessed | tf_op | source)
XLA Modules:
  0.0 173.6 jit_solution(9082989290054967600)
XLA Ops:
  1.5 1.2 gather_fusion.1
  3.4 6.3 %all-to-all-start.1 = ((s32[4,1,3]{2,1,0:T(1,128)}), s32[4,1,3]{2,1,0:T(1,128)S(1)}, u32[]{:S(2)}, u32[]{:S(2)}) async-start(s32[4,1,3]{2,1,0:T(1,128)} %bitcast.5), calls=%async_computation.1 | async-start | bytes 4096 | tf_op jit(solution)/shard_map/all_to_all | solution.py:70
  9.7 1.6 gather_fusion
  11.3 1.1 broadcast_select_fusion
  12.4 2.7 %all-to-all-done.1 = s32[4,1,3]{2,1,0:T(1,128)S(1)} async-done(((s32[4,1,3]{2,1,0:T(1,128)}), s32[4,1,3]{2,1,0:T(1,128)S(1)}, u32[]{:S(2)}, u32[]{:S(2)}) %all-to-all-start.1) | async-done | bytes 80 | tf_op jit(solution)/shard_map/all_to_all | solution.py:70
  15.1 3.5 %all-to-all-start = ((bf16[4,48,2304]{2,1,0:T(8,128)(2,1)}), bf16[4,48,2304]{2,1,0:T(8,128)(2,1)S(1)}, u32[]{:S(2)}, u32[]{:S(2)}) async-start(bf16[4,48,2304]{2,1,0:T(8,128)(2,1)} %broadcast_select_fusion), calls=%async_computation | async-start | bytes 1769472 | tf_op jit(solution)/shard_map/all_to_all | solution.py:69
  20.0 19.8 %all-to-all-done = bf16[4,48,2304]{2,1,0:T(8,128)(2,1)S(1)} async-done(((bf16[4,48,2304]{2,1,0:T(8,128)(2,1)}), bf16[4,48,2304]{2,1,0:T(8,128)(2,1)S(1)}, u32[]{:S(2)}, u32[]{:S(2)}) %all-to-all-start) | async-done | bytes 884768 | tf_op jit(solution)/shard_map/all_to_all | solution.py:69
  39.8 1.4 broadcast_in_dim.36
  41.2 1.0 broadcast_in_dim.35
  42.2 83.6 %while.22 = (s32[]{:T(128)}, f32[2,48,2304]{2,1,0:T(8,128)}, f32[4,48,2304]{2,1,0:T(8,128)}, s32[2]{0:T(128)S(1)}, s32[]{:T(128)}, /*index=5*/bf16[2,48,2304]{2,...) while((s32[]{:T(128)}, f32[2,48,2304]{2,1,0:T(8,128)}, ...), condition=%wide.region_3.4_spmd.clone.clone, body=%wide.region_0.0_spmd.clone.clone.sunk | while | flops 384003168 | bytes 42491336 | solution.py:97
  52.7 2.0 %fusion.84 = f32[48,48,48]{2,1,0:T(8,128)S(1)} fusion(s32[]{:T(128)S(6)} %select_n.239, s32[]{:T(128)S(6)} %select_n.240, s32[]{:T(128)S(6)} %select_n.241, bf16[48,48,48]{2,1,0:T(8,128)(2,1)S(1)} %reshape.611), kind=kLoop, calls=%fused_computation.16.clone.2 | loop fusion | flops 110592 | bytes 663564 | tf_op jit(solution)/shard_map/while/body/eval_jaxpr/convert_element_type | solution.py:44
  59.9 1.1 add.647
  61.5 1.5 convolution_bitcast_fusion.15
  66.6 1.8 %reshape.618 = f32[48,48,48]{2,1,0:T(8,128)} reshape(f32[1,48,2304]{2,1,0:T(8,128)S(1)} %dynamic-slice_convert_fusion.3) | data formatting | bytes 884736 | tf_op jit(solution)/shard_map/while/body/eval_jaxpr/convert_element_type | solution.py:45
  69.0 4.2 %fusion.85 = (f32[48,48,48]{2,1,0:T(8,128)}, f32[48,48,48]{2,1,0:T(8,128)S(1)}) fusion(f32[48,48,48]{2,1,0:T(8,128)S(1)} %bitcast.142, f32[48,48,48]{2,1,0:T(8,128)} %reshape.618, s32[]{:T(128)S(6)} %select_n.239, s32[]{:T(128)S(6)} %select_n.240, s32[]{:T(128)S(6)} %select_n.241, bf16[48,48,48]{2,1,0:T(8,128)(2,1)S(1)} %reshape.611, ...), kind=kLoop, calls=%fused_computation.80.clone.1 | loop fusion | flops 442368 | bytes 1990672 | tf_op jit(solution)/shard_map/while/body/eval_jaxpr/mul | solution.py:53
  75.2 2.0 %fusion.86 = f32[48,48,48]{2,1,0:T(8,128)S(1)} fusion(s32[]{:T(128)S(6)} %select_n.242, s32[]{:T(128)S(6)} %select_n.243, s32[]{:T(128)S(6)} %select_n.244, f32[48,48,48]{2,1,0:T(8,128)} %get-tuple-element.580, f32[]{:T(128)S(6)} %convert_element_type.171), kind=kLoop, calls=%fused_computation.12.clone.1 | loop fusion | flops 110592 | bytes 884752 | tf_op jit(solution)/shard_map/while/body/eval_jaxpr/mul | solution.py:90
  79.7 3.2 %fusion.87 = (f32[2,48,2304]{2,1,0:T(8,128)S(1)}, f32[4,48,2304]{2,1,0:T(8,128)}) fusion(f32[2,48,2304]{2,1,0:T(8,128)S(1)} %copy-done.2, s32[]{:T(128)} %select_n.237, f32[1,48,2304]{2,1,0:T(8,128)S(1)} %mul.479, pred[]{:T(512)} %and_reduce_fusion.4, f32[4,48,2304]{2,1,0:T(8,128)} %get-tuple-element.608, s32[]{:T(128)} %select_n.238, ...), kind=kLoop, calls=%fused_computation.17.clone.1 | loop fusion | flops 442368 | bytes 2656256 | tf_op jit(solution)/shard_map/while/body/eval_jaxpr/scatter-add | solution.py:89
  83.0 0.9 copy-done.3
  94.4 2.0 %fusion.84 = f32[48,48,48]{2,1,0:T(8,128)S(1)} fusion(s32[]{:T(128)S(6)} %select_n.239, s32[]{:T(128)S(6)} %select_n.240, s32[]{:T(128)S(6)} %select_n.241, bf16[48,48,48]{2,1,0:T(8,128)(2,1)S(1)} %reshape.611), kind=kLoop, calls=%fused_computation.16.clone.2 | loop fusion | flops 110592 | bytes 663564 | tf_op jit(solution)/shard_map/while/body/eval_jaxpr/convert_element_type | solution.py:44
  101.6 1.1 add.647
  103.3 1.5 convolution_bitcast_fusion.15
  108.3 1.8 %reshape.618 = f32[48,48,48]{2,1,0:T(8,128)} reshape(f32[1,48,2304]{2,1,0:T(8,128)S(1)} %dynamic-slice_convert_fusion.3) | data formatting | bytes 884736 | tf_op jit(solution)/shard_map/while/body/eval_jaxpr/convert_element_type | solution.py:45
  110.8 4.2 %fusion.85 = (f32[48,48,48]{2,1,0:T(8,128)}, f32[48,48,48]{2,1,0:T(8,128)S(1)}) fusion(f32[48,48,48]{2,1,0:T(8,128)S(1)} %bitcast.142, f32[48,48,48]{2,1,0:T(8,128)} %reshape.618, s32[]{:T(128)S(6)} %select_n.239, s32[]{:T(128)S(6)} %select_n.240, s32[]{:T(128)S(6)} %select_n.241, bf16[48,48,48]{2,1,0:T(8,128)(2,1)S(1)} %reshape.611, ...), kind=kLoop, calls=%fused_computation.80.clone.1 | loop fusion | flops 442368 | bytes 1990672 | tf_op jit(solution)/shard_map/while/body/eval_jaxpr/mul | solution.py:53
  116.9 2.1 %fusion.86 = f32[48,48,48]{2,1,0:T(8,128)S(1)} fusion(s32[]{:T(128)S(6)} %select_n.242, s32[]{:T(128)S(6)} %select_n.243, s32[]{:T(128)S(6)} %select_n.244, f32[48,48,48]{2,1,0:T(8,128)} %get-tuple-element.580, f32[]{:T(128)S(6)} %convert_element_type.171), kind=kLoop, calls=%fused_computation.12.clone.1 | loop fusion | flops 110592 | bytes 884752 | tf_op jit(solution)/shard_map/while/body/eval_jaxpr/mul | solution.py:90
  121.5 3.2 %fusion.87 = (f32[2,48,2304]{2,1,0:T(8,128)S(1)}, f32[4,48,2304]{2,1,0:T(8,128)}) fusion(f32[2,48,2304]{2,1,0:T(8,128)S(1)} %copy-done.2, s32[]{:T(128)} %select_n.237, f32[1,48,2304]{2,1,0:T(8,128)S(1)} %mul.479, pred[]{:T(512)} %and_reduce_fusion.4, f32[4,48,2304]{2,1,0:T(8,128)} %get-tuple-element.608, s32[]{:T(128)} %select_n.238, ...), kind=kLoop, calls=%fused_computation.17.clone.1 | loop fusion | flops 442368 | bytes 2656256 | tf_op jit(solution)/shard_map/while/body/eval_jaxpr/scatter-add | solution.py:89
  124.7 0.9 copy-done.3
  125.8 2.5 %convert_element_type.112 = bf16[4,48,2304]{2,1,0:T(8,128)(2,1)} convert(f32[4,48,2304]{2,1,0:T(8,128)} %get-tuple-element.681) | non-fusion elementwise | flops 442368 | bytes 2654208 | tf_op jit(solution)/shard_map/convert_element_type | solution.py:98
  128.3 3.6 %all-to-all-start.2 = ((bf16[4,48,2304]{2,1,0:T(8,128)(2,1)}), bf16[4,48,2304]{2,1,0:T(8,128)(2,1)S(1)}, u32[]{:S(2)}, u32[]{:S(2)}) async-start(bf16[4,48,2304]{2,1,0:T(8,128)(2,1)} %convert_element_type.112), calls=%async_computation.2 | async-start | bytes 1769472 | tf_op jit(solution)/shard_map/all_to_all | solution.py:100
  132.7 20.9 %all-to-all-done.2 = bf16[4,48,2304]{2,1,0:T(8,128)(2,1)S(1)} async-done(((bf16[4,48,2304]{2,1,0:T(8,128)(2,1)}), bf16[4,48,2304]{2,1,0:T(8,128)(2,1)S(1)}, u32[]{:S(2)}, u32[]{:S(2)}) %all-to-all-start.2) | async-done | bytes 884768 | tf_op jit(solution)/shard_map/all_to_all | solution.py:100
  154.1 0.9 convolution_add_fusion
  155.0 17.1 %all_to_all.38 = f32[2,8,13824]{2,0,1:T(2,128)S(1)} all-to-all(f32[2,8,13824]{2,0,1:T(2,128)S(1)} %bitcast.148), channel_id=1, replica_groups=mesh['grp'=4,'dev'=8] {'dev'}, dimensions={1} | all-to-all | bytes 1769472 | tf_op jit(solution)/shard_map/all_to_all | solution.py:109
  172.1 1.5 all_to_all.33
  (122 shorter events, 34.1 us)
Async XLA Ops:
  0.0 0.7 copy-start
  0.9 0.6 copy-start.12
  3.4 11.7 %all-to-all-start.1 = ((s32[4,1,3]{2,1,0:T(1,128)}), s32[4,1,3]{2,1,0:T(1,128)S(1)}, u32[]{:S(2)}, u32[]{:S(2)}) async-start(s32[4,1,3]{2,1,0:T(1,128)} %bitcast.5), calls=%async_computation.1 | async-start | bytes 4096 | tf_op jit(solution)/shard_map/all_to_all | solution.py:70
  15.1 24.7 %all-to-all-start = ((bf16[4,48,2304]{2,1,0:T(8,128)(2,1)}), bf16[4,48,2304]{2,1,0:T(8,128)(2,1)S(1)}, u32[]{:S(2)}, u32[]{:S(2)}) async-start(bf16[4,48,2304]{2,1,0:T(8,128)(2,1)} %broadcast_select_fusion), calls=%async_computation | async-start | bytes 1769472 | tf_op jit(solution)/shard_map/all_to_all | solution.py:69
  39.8 2.4 %copy-start.1 = (bf16[2,48,2304]{2,1,0:T(8,128)(2,1)S(1)}, bf16[2,48,2304]{2,1,0:T(8,128)(2,1)}, u32[]{:S(2)}) copy-start(bf16[2,48,2304]{2,1,0:T(8,128)(2,1)} %param.12) | copy-start | bytes 1327108
  39.8 2.4 %copy-start.7 = (s32[2,3]{1,0:T(2,128)S(1)}, s32[2,3]{1,0:T(2,128)}, u32[]{:S(2)}) copy-start(s32[2,3]{1,0:T(2,128)} %param.13) | copy-start | bytes 76
  39.8 2.4 %copy-start.8 = (s32[3]{0:T(128)S(1)}, s32[3]{0:T(128)}, u32[]{:S(2)}) copy-start(s32[3]{0:T(128)} %constant.277.clone.3) | copy-start | bytes 40
  39.8 2.4 %copy-start.14 = (s32[1,1,2]{2,1,0:T(1,128)S(1)}, s32[1,1,2]{2,1,0:T(1,128)}, u32[]{:S(2)}) copy-start(s32[1,1,2]{2,1,0:T(1,128)} %param.15) | copy-start | bytes 28
  39.8 2.4 %copy-start.16 = (s32[1,1,2]{2,1,0:T(1,128)S(1)}, s32[1,1,2]{2,1,0:T(1,128)}, u32[]{:S(2)}) copy-start(s32[1,1,2]{2,1,0:T(1,128)} %param.16) | copy-start | bytes 28
  42.2 9.6 %copy-start.10 = (s32[4,3]{1,0:T(4,128)}, s32[4,3]{1,0:T(4,128)S(1)}, u32[]{:S(2)}) copy-start(s32[4,3]{1,0:T(4,128)S(1)} %get-tuple-element.638) | copy-start | bytes 148 | tf_op jit(solution)/shard_map/while
  42.2 9.6 %copy-start.5 = (bf16[4,48,2304]{2,1,0:T(8,128)(2,1)}, bf16[4,48,2304]{2,1,0:T(8,128)(2,1)S(1)}, u32[]{:S(2)}) copy-start(bf16[4,48,2304]{2,1,0:T(8,128)(2,1)S(1)} %get-tuple-element.636) | copy-start | bytes 2654212 | tf_op jit(solution)/shard_map/while
  77.7 1.3 copy-start.9
  77.7 2.0 %copy-start.2 = (f32[2,48,2304]{2,1,0:T(8,128)S(1)}, f32[2,48,2304]{2,1,0:T(8,128)}, u32[]{:S(2)}) copy-start(f32[2,48,2304]{2,1,0:T(8,128)} %get-tuple-element.607) | copy-start | bytes 2654212 | tf_op jit(solution)/shard_map/while
  79.7 4.2 %copy-start.6 = (bf16[4,48,2304]{2,1,0:T(8,128)(2,1)S(1)}, bf16[4,48,2304]{2,1,0:T(8,128)(2,1)}, u32[]{:S(2)}) copy-start(bf16[4,48,2304]{2,1,0:T(8,128)(2,1)} %copy-done.5) | copy-start | bytes 2654212 | tf_op jit(solution)/shard_map/while
  79.7 4.2 %copy-start.11 = (s32[4,3]{1,0:T(4,128)S(1)}, s32[4,3]{1,0:T(4,128)}, u32[]{:S(2)}) copy-start(s32[4,3]{1,0:T(4,128)} %copy-done.10) | copy-start | bytes 148 | tf_op jit(solution)/shard_map/while
  79.7 4.2 %copy-start.15 = (s32[1,1,2]{2,1,0:T(1,128)S(1)}, s32[1,1,2]{2,1,0:T(1,128)}, u32[]{:S(2)}) copy-start(s32[1,1,2]{2,1,0:T(1,128)} %get-tuple-element.678) | copy-start | bytes 28 | tf_op jit(solution)/shard_map/while
  79.7 4.2 %copy-start.17 = (s32[1,1,2]{2,1,0:T(1,128)S(1)}, s32[1,1,2]{2,1,0:T(1,128)}, u32[]{:S(2)}) copy-start(s32[1,1,2]{2,1,0:T(1,128)} %get-tuple-element.703) | copy-start | bytes 28 | tf_op jit(solution)/shard_map/while
  83.0 0.9 copy-start.3
  83.9 9.6 %copy-start.10 = (s32[4,3]{1,0:T(4,128)}, s32[4,3]{1,0:T(4,128)S(1)}, u32[]{:S(2)}) copy-start(s32[4,3]{1,0:T(4,128)S(1)} %get-tuple-element.638) | copy-start | bytes 148 | tf_op jit(solution)/shard_map/while
  83.9 9.6 %copy-start.5 = (bf16[4,48,2304]{2,1,0:T(8,128)(2,1)}, bf16[4,48,2304]{2,1,0:T(8,128)(2,1)S(1)}, u32[]{:S(2)}) copy-start(bf16[4,48,2304]{2,1,0:T(8,128)(2,1)S(1)} %get-tuple-element.636) | copy-start | bytes 2654212 | tf_op jit(solution)/shard_map/while
  119.5 1.3 copy-start.9
  119.5 2.0 %copy-start.2 = (f32[2,48,2304]{2,1,0:T(8,128)S(1)}, f32[2,48,2304]{2,1,0:T(8,128)}, u32[]{:S(2)}) copy-start(f32[2,48,2304]{2,1,0:T(8,128)} %get-tuple-element.607) | copy-start | bytes 2654212 | tf_op jit(solution)/shard_map/while
  121.5 4.2 %copy-start.6 = (bf16[4,48,2304]{2,1,0:T(8,128)(2,1)S(1)}, bf16[4,48,2304]{2,1,0:T(8,128)(2,1)}, u32[]{:S(2)}) copy-start(bf16[4,48,2304]{2,1,0:T(8,128)(2,1)} %copy-done.5) | copy-start | bytes 2654212 | tf_op jit(solution)/shard_map/while
  121.5 4.2 %copy-start.11 = (s32[4,3]{1,0:T(4,128)S(1)}, s32[4,3]{1,0:T(4,128)}, u32[]{:S(2)}) copy-start(s32[4,3]{1,0:T(4,128)} %copy-done.10) | copy-start | bytes 148 | tf_op jit(solution)/shard_map/while
  121.5 4.2 %copy-start.15 = (s32[1,1,2]{2,1,0:T(1,128)S(1)}, s32[1,1,2]{2,1,0:T(1,128)}, u32[]{:S(2)}) copy-start(s32[1,1,2]{2,1,0:T(1,128)} %get-tuple-element.678) | copy-start | bytes 28 | tf_op jit(solution)/shard_map/while
  121.5 4.2 %copy-start.17 = (s32[1,1,2]{2,1,0:T(1,128)S(1)}, s32[1,1,2]{2,1,0:T(1,128)}, u32[]{:S(2)}) copy-start(s32[1,1,2]{2,1,0:T(1,128)} %get-tuple-element.703) | copy-start | bytes 28 | tf_op jit(solution)/shard_map/while
  124.7 0.9 copy-start.3
  128.3 3.6 %copy-start.4 = (f32[2,48,2304]{2,1,0:T(8,128)S(1)}, f32[2,48,2304]{2,1,0:T(8,128)}, u32[]{:S(2)}) copy-start(f32[2,48,2304]{2,1,0:T(8,128)} %get-tuple-element.680) | copy-start | bytes 2654212
  128.3 25.3 %all-to-all-start.2 = ((bf16[4,48,2304]{2,1,0:T(8,128)(2,1)}), bf16[4,48,2304]{2,1,0:T(8,128)(2,1)S(1)}, u32[]{:S(2)}, u32[]{:S(2)}) async-start(bf16[4,48,2304]{2,1,0:T(8,128)(2,1)} %convert_element_type.112), calls=%async_computation.2 | async-start | bytes 1769472 | tf_op jit(solution)/shard_map/all_to_all | solution.py:100
  132.7 21.4 %copy-start.13 = (s32[4]{0:T(128)S(1)}, s32[4]{0:T(128)}, u32[]{:S(2)}) copy-start(s32[4]{0:T(128)} %copy-done.12) | copy-start | bytes 52
where the time goes:
time: 175 us; the launch traced here: 174 us
  waiting for transfers between devices  43.4 us (25%)
  local copies, waits for them, and re-layouts  37 us (21%)
  other arithmetic  30.9 us (18%)
  loops' own time  20.8 us (12%)
  blocking collectives  17.1 us (10%)
  starting transfers between devices  13.5 us (8%)
  matrix products  10.8 us (6%)
    all_to_all x1, waiting for transfers between devices, body(): lax.all_to_all(partial_value, 'grp', split_axis=0, concat_axis=0, tiled=T...  20.9 us
    another operation x1, loops' own time, body(): own_sum, returned = lax.fori_loop(0, slot_total, one_pair, start)  20.8 us
    all_to_all x1, waiting for transfers between devices, body(): lax.all_to_all(outgoing, 'grp', split_axis=0, concat_axis=0, tiled=True)  19.8 us
    all_to_all x1, blocking collectives, body(): return lax.all_to_all(whole, 'dev', split_axis=1, concat_axis=0, tiled=True)  17.1 us
    dot_general x12, matrix products, turn(): jnp.dot(matrix, a_field, preferred_element_type=jnp.float32, precision=la...  9.94 us
    mul x2, other arithmetic, pair_terms(): backward = shift_box(spectrum * own_wide, offset_gap, -1, box_side)  8.44 us
    scatter-add x2, other arithmetic, one_pair(): own_sum.at[own_slot].add(is_live * own_term)  6.48 us
    all_to_all x1, starting transfers between devices, body(): lax.all_to_all(outgoing_offs, 'grp', split_axis=0, concat_axis=0, tiled=T...  6.32 us
  transfers between devices with their start and end apart: 3, of which 3 were waited for; matrix products, arithmetic and copies ran while one was open for 3% of the time, Pallas kernels for 0%

commit v1 on v0

v1 whole, which is shorter than its diff:
```python
import functools
import math

import numpy as np

import jax
import jax.numpy as jnp
from jax import lax
from jax.experimental import pallas as pl
from jax.experimental.pallas import tpu as pltpu
from jax.sharding import PartitionSpec as P

LANES = 128
HALF = 64
f32 = jnp.float32
bf16 = jnp.bfloat16


def np_tables(n):
    freq = np.arange(n)
    step = math.pi / (n + 1)
    sine = math.sqrt(2.0 / (n + 1)) * np.sin(step * ((freq[:, None] + 1) * (freq[None, :] + 1) % (2 * (n + 1))))
    sine = sine.astype(np.float32)
    high = sine.astype(jnp.bfloat16)
    low = (sine - high.astype(np.float32)).astype(jnp.bfloat16)

    def two(block):
        out = np.zeros((LANES, LANES), jnp.bfloat16)
        out[:n, :n] = block
        out[HALF : HALF + n, HALF : HALF + n] = block
        return out

    lane_side = np.block([[two(high), two(low)], [two(high), two(low)]])
    row_side = np.concatenate([high, high, low, low], axis=1)
    modes = (2.0 - 2.0 * np.cos(step * (freq + 1.0))).astype(np.float32)
    base = np.ones((n, LANES), np.float32)
    outer = np.ones((n // 2, LANES), np.float32)
    for half in range(2):
        at = half * HALF
        base[:, at : at + n] = modes[:, None] + modes[None, :]
        outer[:, at : at + HALF] = modes[half * (n // 2) : (half + 1) * (n // 2), None]
    return lane_side, row_side, base, outer


def split(x):
    high = x.astype(bf16)
    return high, (x - high.astype(f32)).astype(bf16)


def lane_turn(x, lane_side):
    both = jnp.concatenate(split(x), axis=1)
    out = jnp.dot(both, lane_side, preferred_element_type=f32)
    return out[:, :LANES] + out[:, LANES:]


def row_turn(tiles, row_side):
    columns = []
    for tile in tiles:
        high, low = split(tile)
        columns.append(jnp.concatenate([high, low, high, low], axis=0))
    out = jnp.dot(row_side, jnp.concatenate(columns, axis=1), preferred_element_type=f32)
    return out[:, :LANES], out[:, LANES:]


def pair_kernel(sizes, step, first, last, *refs):
    n, orbs, slots, groups = sizes
    half = n // 2
    cells_tile = half * n // LANES
    wide = n + 2 * half
    chunk = 6 if half % 6 == 0 else 2
    meta, where_am_i, own = refs[:3]
    others = refs[3 : 3 + orbs]
    lane_ref, row_ref, base_ref, outer_ref = refs[3 + orbs : 7 + orbs]
    rest = list(refs[7 + orbs :])
    total_in = None if first else rest.pop(0)
    total_out = None if last else rest.pop(0)
    out = rest.pop(0) if last else None
    total = rest.pop(0) if last else total_out
    dense_i, dense_j, held_i, held_j, moved, field, other = rest

    lane = lax.broadcasted_iota(jnp.int32, (n, LANES), 1)
    row = lax.broadcasted_iota(jnp.int32, (n, LANES), 0)
    left = lane < HALF
    left_half = left[:half]
    if first:
        total[...] = jnp.zeros_like(total)
    else:
        total[...] = total_in[...]

    at_source = 3 * orbs + slots
    at_count = at_source + slots
    at_pick = at_count + 1
    me = where_am_i[0]
    them = lax.rem(me + groups - step, groups)

    def unpack(dense, put):
        for yo in range(half):
            start = yo * n % LANES
            first_tile = yo * n // LANES
            halves = []
            for h in range(2):
                t = (first_tile + h * cells_tile) * LANES
                piece = dense[:, t : t + LANES].astype(f32)
                if start + n > LANES:
                    after = dense[:, t + LANES : t + 2 * LANES].astype(f32)
                    piece = jnp.where(lane >= start, piece, after)
                amount = (h * HALF - start) % LANES
                halves.append(pltpu.roll(piece, amount, 1) if amount else piece)
            put(yo, jnp.where(left, halves[0], halves[1]))

    def shifted(gap, use):
        gap_x, gap_y, gap_z = gap
        z_at = lax.rem(lane, HALF)
        inside = (
            (z_at < n)
            & (z_at + gap_z >= 0)
            & (z_at + gap_z < n)
            & (row + gap_x >= 0)
            & (row + gap_x < n)
        )
        for yo in range(half):
            s = gap_y + yo
            under = s < 0
            over = s >= half
            src = s + jnp.where(under, half, 0) - jnp.where(over, half, 0)
            tile = held_j[pl.ds(src * wide + half + gap_x, n), :]
            amount = (2 * LANES - gap_z + jnp.where(under | over, HALF, 0)) % LANES
            tile = pltpu.roll(tile, amount, 1)
            low_lane = jnp.where(under, HALF, 0)
            high_lane = jnp.where(over, HALF, LANES)
            good = inside & (lane >= low_lane) & (lane < high_lane)
            use(yo, jnp.where(good, tile, 0.0))

    def swapped(ref, at):
        a = ref[pl.ds(at, half, stride=n), :]
        b = ref[pl.ds(at + half, half, stride=n), :]
        top = jnp.where(left_half, a, pltpu.roll(b, HALF, 1))
        bottom = jnp.where(left_half, pltpu.roll(a, HALF, 1), b)
        return jnp.concatenate([top, bottom], axis=0)

    def task(which, carry):
        lister = jnp.where(which == 0, me, them)
        source = jnp.where(which == 0, them, me)
        listed = meta[lister, at_count]
        i_at = jnp.int32(0)
        found = jnp.int32(0)
        for p in range(slots):
            hit = (meta[lister, at_source + p] == source) & (p < listed)
            i_at = jnp.where(hit, meta[lister, 3 * orbs + p], i_at)
            found = jnp.where(hit, 1, found)
        j_at = meta[source, at_pick + lister]
        gap = [meta[lister, i_at * 3 + k] - meta[source, j_at * 3 + k] for k in range(3)]

        @pl.when(found == 1)
        def _():
            @pl.when(which == 0)
            def _():
                dense_i[...] = own[i_at]
                for q in range(orbs):
                    @pl.when(j_at == q)
                    def _():
                        dense_j[...] = others[q][...]

            @pl.when(which == 1)
            def _():
                dense_j[...] = own[j_at]
                for q in range(orbs):
                    @pl.when(i_at == q)
                    def _():
                        dense_i[...] = others[q][...]

            def put_i(yo, tile):
                held_i[yo * n : (yo + 1) * n, :] = tile

            def put_j(yo, tile):
                held_j[yo * wide + half : yo * wide + half + n, :] = tile

            unpack(dense_i, put_i)
            unpack(dense_j, put_j)

            def use_moved(yo, tile):
                moved[yo * n : (yo + 1) * n, :] = tile

            shifted(gap, use_moved)
            lane_side = lane_ref[...]
            row_side = row_ref[...]
            rows = chunk * n
            for c in range(half // chunk):
                here = slice(c * rows, (c + 1) * rows)
                spectrum = lane_turn(held_i[here, :] * moved[here, :], lane_side)
                for q in range(0, chunk, 2):
                    pair = row_turn([spectrum[(q + k) * n : (q + k + 1) * n] for k in range(2)], row_side)
                    for k in range(2):
                        at = c * rows + (q + k) * n
                        field[at : at + n, :] = pair[k]
            for xo in range(0, half, 2):
                pair = row_turn([swapped(field, xo + k) for k in range(2)], row_side)
                pair = [pair[k] / (base_ref[...] + outer_ref[xo + k : xo + k + 1, :]) for k in range(2)]
                pair = row_turn(pair, row_side)
                for k in range(2):
                    other[(xo + k) * n : (xo + k + 1) * n, :] = pair[k]
            for c in range(half // chunk):
                tiles = []
                for q in range(0, chunk, 2):
                    tiles += row_turn([swapped(other, c * chunk + q + k) for k in range(2)], row_side)
                field[c * rows : (c + 1) * rows, :] = lane_turn(jnp.concatenate(tiles, axis=0), lane_side)

            @pl.when(which == 0)
            def _():
                for yo in range(half):
                    here = slice(yo * n, (yo + 1) * n)
                    there = pl.ds(i_at * (half * n) + yo * n, n)
                    total[there, :] += field[here, :] * moved[here, :]

            @pl.when(which == 1)
            def _():
                for yo in range(half):
                    here = slice(yo * n, (yo + 1) * n)
                    put_j(yo, (field[here, :] * held_i[here, :]).astype(bf16).astype(f32))

                def add_back(yo, tile):
                    there = pl.ds(j_at * (half * n) + yo * n, n)
                    total[there, :] += tile

                shifted([-k for k in gap], add_back)

        return carry

    lax.fori_loop(0, 2, task, 0)

    if last:
        for a in range(orbs):
            current = {}
            for yo in range(half):
                start = yo * n % LANES
                first_tile = yo * n // LANES
                tile = total[a * half * n + yo * n : a * half * n + (yo + 1) * n, :]
                for h in range(2):
                    t = first_tile + h * cells_tile
                    amount = (start - h * HALF) % LANES
                    piece = pltpu.roll(tile, amount, 1) if amount else tile
                    current[t] = jnp.where(lane >= start, piece, current[t]) if t in current else piece
                    if start + n >= LANES:
                        out[a, :, t * LANES : (t + 1) * LANES] = current.pop(t).astype(bf16)
                        if start + n > LANES:
                            current[t + 1] = piece


def pair_step(step, first, last, meta, where_am_i, own, others, tables, total):
    orbs, n, plane = own.shape
    groups = meta.shape[0]
    half = n // 2
    slots = (meta.shape[1] - 3 * orbs - 1 - groups) // 2
    vmem = pl.BlockSpec(memory_space=pltpu.VMEM)
    smem = pl.BlockSpec(memory_space=pltpu.SMEM)
    operands = [meta, where_am_i, own, *others, *tables]
    specs = [smem, smem] + [vmem] * (1 + orbs + len(tables))
    if not first:
        operands.append(total)
        specs.append(vmem)
    held = jax.ShapeDtypeStruct((orbs * half * n, LANES), f32)
    rows = half * n
    scratch = [
        pltpu.VMEM((n, plane), bf16),
        pltpu.VMEM((n, plane), bf16),
        pltpu.VMEM((rows, LANES), f32),
        pltpu.VMEM((half * (n + 2 * half), LANES), f32),
        pltpu.VMEM((rows, LANES), f32),
        pltpu.VMEM((rows, LANES), f32),
        pltpu.VMEM((rows, LANES), f32),
    ]
    if last:
        scratch.insert(0, pltpu.VMEM(held.shape, f32))
    return pl.pallas_call(
        functools.partial(pair_kernel, (n, orbs, slots, groups), step, first, last),
        out_shape=jax.ShapeDtypeStruct(own.shape, bf16) if last else held,
        in_specs=specs,
        out_specs=vmem,
        scratch_shapes=scratch,
        compiler_params=pltpu.CompilerParams(vmem_limit_bytes=32 << 20),
        cost_estimate=pl.CostEstimate(flops=2 * 12 * 3 * n**4, bytes_accessed=4 * n**3 * 4, transcendentals=0),
        name=f"pairs_{step}",
    )(*operands)


def body(orbitals, offsets, pick, pair_local, pair_source, pair_count):
    orbs, n, plane = orbitals.shape
    groups = lax.axis_size("grp")
    me = lax.axis_index("grp").astype(jnp.int32)
    member = lax.axis_index("dev")
    my_pick = lax.dynamic_slice_in_dim(pick[0], member, 1, 0)[0]
    mine = jnp.concatenate(
        [offsets.reshape(-1), pair_local[0, 0], pair_source[0, 0], pair_count[0, 0], my_pick]
    ).astype(jnp.int32)
    ring = [(g, (g + 1) % groups) for g in range(groups)]
    held = [orbitals[q] for q in range(orbs)]
    tables = [jnp.asarray(t) for t in np_tables(n)]
    meta = None
    total = None
    for step in range(1, groups):
        held = [lax.ppermute(h, "grp", ring) for h in held]
        if meta is None:
            meta = lax.all_to_all(
                jnp.broadcast_to(mine[None, :], (groups, mine.shape[0])), "grp", 0, 0, tiled=True
            )
        total = pair_step(
            step, step == 1, step == groups - 1, meta, me.reshape(1), orbitals, held, tables, total
        )
    whole = total.reshape(orbs, n * plane)
    return lax.all_to_all(whole, "dev", split_axis=1, concat_axis=0, tiled=True).astype(f32)


def solution(mesh):
    return jax.shard_map(
        body,
        mesh=mesh,
        in_specs=(
            P(("grp", "dev"), None, None),
            P(("grp", "dev"), None),
            P("grp", None, None),
            P("grp", "dev", None),
            P("grp", "dev", None),
            P("grp", "dev", None),
        ),
        out_specs=P("grp", "dev"),
        check_vma=False,
    )
```

time: 175 us -> 74.3 us (0.42)
  other arithmetic: 30.9 us -> 0.3 us
  local copies, waits for them, and re-layouts: 37 us -> 8.91 us
  loops' own time: 20.8 us -> 0 us
  waiting for transfers between devices: 43.4 us -> 27 us
  matrix products: 10.8 us -> 0 us
  Pallas kernels: 0 us -> 10 us
  starting transfers between devices: 13.5 us -> 9.81 us
    all_to_all x3 -> x1, waiting for transfers between devices: 43.4 us -> 5.47 us  [body(): lax.all_to_all(jnp.broadcast_to(mine[None, :], (groups, mine.shape[0])),...]
    ppermute x0 -> x6, waiting for transfers between devices: none -> 21.5 us  [body(): held = [lax.ppermute(h, 'grp', ring) for h in held]]
    another operation x1 -> x0, loops' own time: 20.8 us -> none  [body(): own_sum, returned = lax.fori_loop(0, slot_total, one_pair, start)]
    mul x4 -> x0, other arithmetic: 12.5 us -> none  [the longest x2 8.44 us: pair_terms(): backward = shift_box(spectrum * own_wide, offset_gap, -1, box_side)]
    dot_general x13 -> x0, matrix products: 10.8 us -> none  [the longest x12 9.94 us: turn(): jnp.dot(matrix, a_field, preferred_element_type=jnp.float32, precision=la...]
    reshape x24 -> x1, local copies, waits for them, and re-layouts: 11.1 us -> 0.76 us  [body(): offsets.reshape(-1)]
    pallas_call x0 -> x3, Pallas kernels: none -> 10 us  [pair_step(): pl.pallas_call(functools.partial(pair_kernel, (n, orbs, slots, groups), s...]
    all_to_all x3 -> x1, starting transfers between devices: 13.5 us -> 5.09 us  [body(): lax.all_to_all(jnp.broadcast_to(mine[None, :], (groups, mine.shape[0])),...]
  transfers between devices with their start and end apart: 3 -> 7, of which waited for: 3 -> 5; matrix products, arithmetic and copies ran while one was open for 3% -> 3% of each run, Pallas kernels for 0% -> 12%
where the time goes in v1:
time: 74.3 us; the launch traced here: 73.4 us
  waiting for transfers between devices  27 us (36%)
  blocking collectives  16.6 us (22%)
  Pallas kernels  10 us (13%)
  starting transfers between devices  9.81 us (13%)
  local copies, waits for them, and re-layouts  8.91 us (12%)
    ppermute x6, waiting for transfers between devices, body(): held = [lax.ppermute(h, 'grp', ring) for h in held]  21.5 us
    all_to_all x1, blocking collectives, body(): lax.all_to_all(whole, 'dev', split_axis=1, concat_axis=0, tiled=True)  16.6 us
    pallas_call x3, Pallas kernels, pair_step(): pl.pallas_call(functools.partial(pair_kernel, (n, orbs, slots, groups), s...  10 us
    all_to_all x1, waiting for transfers between devices, body(): lax.all_to_all(jnp.broadcast_to(mine[None, :], (groups, mine.shape[0])),...  5.47 us
    all_to_all x1, starting transfers between devices, body(): lax.all_to_all(jnp.broadcast_to(mine[None, :], (groups, mine.shape[0])),...  5.09 us
    ppermute x6, starting transfers between devices, body(): held = [lax.ppermute(h, 'grp', ring) for h in held]  4.72 us
    unnamed x12, local copies, waits for them, and re-layouts  3.09 us
    convert_element_type x1, local copies, waits for them, and re-layouts, body(): lax.all_to_all(whole, 'dev', split_axis=1, concat_axis=0, tiled=True)  1.52 us
  transfers between devices with their start and end apart: 7, of which 5 were waited for; matrix products, arithmetic and copies ran while one was open for 3% of the time, Pallas kernels for 12%

profile of v1, /device:TPU:0, one launch (start us, length us, event | category | flops | bytes accessed | tf_op | source)
XLA Modules:
  0.0 73.4 jit_solution(6472484155315409490)
XLA Ops:
  0.0 0.0 copy-start
  0.0 1.1 %slice_bitcast_fusion = (bf16[48,2304]{1,0:T(8,128)(2,1)S(1)}, bf16[48,2304]{1,0:T(8,128)(2,1)S(1)}) fusion(bf16[2,48,2304]{2,1,0:T(8,128)(2,1)} %refs_2_.5), kind=kLoop, calls=%fused_computation.1 | loop fusion | bytes 884736 | tf_op jit(solution)/shard_map/squeeze | solution.py:296
  1.1 3.1 %collective-permute-start = (bf16[48,2304]{1,0:T(8,128)(2,1)S(1)}, bf16[48,2304]{1,0:T(8,128)(2,1)S(1)}, u32[]{:S(2)}, u32[]{:S(2)}) collective-permute-start(bf16[48,2304]{1,0:T(8,128)(2,1)S(1)} %get-tuple-element.6), channel_id=1, source_target_pairs={{0,8},{8,16},{16,24},{24,0},{1,9},{9,17},{17,25},{25,1},{2,10},{10... | collective-permute-start | bytes 663560 | tf_op jit(solution)/shard_map/ppermute | solution.py:301
  4.2 1.6 %collective-permute-start.3 = (bf16[48,2304]{1,0:T(8,128)(2,1)S(1)}, bf16[48,2304]{1,0:T(8,128)(2,1)S(1)}, u32[]{:S(2)}, u32[]{:S(2)}) collective-permute-start(bf16[48,2304]{1,0:T(8,128)(2,1)S(1)} %get-tuple-element.5), channel_id=1, source_target_pairs={{0,8},{8,16},{16,24},{24,0},{1,9},{9,17},{17,25},{25,1},{2,10},{10... | collective-permute-start | bytes 663560 | tf_op jit(solution)/shard_map/ppermute | solution.py:301
  5.8 6.7 %collective-permute-done.refs_3_ = bf16[48,2304]{1,0:T(8,128)(2,1)S(1)} collective-permute-done((bf16[48,2304]{1,0:T(8,128)(2,1)S(1)}, bf16[48,2304]{1,0:T(8,128)(2,1)S(1)}, u32[]{:S(2)}, u32[]{:S(2)}) %collective-permute-start) | collective-permute-done | bytes 221216 | tf_op jit(solution)/shard_map/ppermute | solution.py:301
  12.5 0.0 collective-permute-start.1
  12.5 4.7 %collective-permute-done.3.refs_4_ = bf16[48,2304]{1,0:T(8,128)(2,1)S(1)} collective-permute-done((bf16[48,2304]{1,0:T(8,128)(2,1)S(1)}, bf16[48,2304]{1,0:T(8,128)(2,1)S(1)}, u32[]{:S(2)}, u32[]{:S(2)}) %collective-permute-start.3) | collective-permute-done | bytes 221216 | tf_op jit(solution)/shard_map/ppermute | solution.py:301
  17.2 0.0 collective-permute-start.4
  17.3 4.9 %collective-permute-done.1.refs_3_ = bf16[48,2304]{1,0:T(8,128)(2,1)S(1)} collective-permute-done((bf16[48,2304]{1,0:T(8,128)(2,1)S(1)}, bf16[48,2304]{1,0:T(8,128)(2,1)S(1)}, u32[]{:S(2)}, u32[]{:S(2)}) %collective-permute-start.1) | collective-permute-done | bytes 221216 | tf_op jit(solution)/shard_map/ppermute | solution.py:301
  22.1 0.0 collective-permute-start.2
  22.1 5.3 %collective-permute-done.4.refs_4_ = bf16[48,2304]{1,0:T(8,128)(2,1)S(1)} collective-permute-done((bf16[48,2304]{1,0:T(8,128)(2,1)S(1)}, bf16[48,2304]{1,0:T(8,128)(2,1)S(1)}, u32[]{:S(2)}, u32[]{:S(2)}) %collective-permute-start.4) | collective-permute-done | bytes 221216 | tf_op jit(solution)/shard_map/ppermute | solution.py:301
  27.4 0.0 collective-permute-start.5
  28.1 0.8 %reshape.23 = s32[6]{0:T(128)S(1)} reshape(s32[2,3]{1,0:T(2,128)} %param.11) | data formatting | bytes 48 | tf_op jit(solution)/shard_map/reshape | solution.py:293
  28.8 0.2 dynamic-slice_reduce_fusion
  29.0 0.7 %concatenate.3 = s32[15]{0:T(128)S(1)} concatenate(s32[6]{0:T(128)S(1)} %reshape.23, s32[2]{0:T(128)} %bitcast.15, s32[2]{0:T(128)} %bitcast.16, s32[1]{0:T(128)} %bitcast.11, s32[4]{0:T(128)S(1)} %dynamic-slice_reduce_fusion), dimensions={0} | concatenate | bytes 120 | tf_op jit(solution)/shard_map/concatenate | solution.py:292
  29.8 0.6 broadcast_in_dim.2
  30.3 5.1 %all-to-all-start = ((s32[4,1,15]{2,1,0:T(1,128)}), s32[4,1,15]{2,1,0:T(1,128)S(1)}, u32[]{:S(2)}, u32[]{:S(2)}) async-start(s32[4,1,15]{2,1,0:T(1,128)} %broadcast_in_dim.2), calls=%async_computation | async-start | bytes 4096 | tf_op jit(solution)/shard_map/all_to_all | solution.py:303
  35.4 5.5 %all-to-all-done = s32[4,1,15]{2,1,0:T(1,128)S(1)} async-done(((s32[4,1,15]{2,1,0:T(1,128)}), s32[4,1,15]{2,1,0:T(1,128)S(1)}, u32[]{:S(2)}, u32[]{:S(2)}) %all-to-all-start) | async-done | bytes 272 | tf_op jit(solution)/shard_map/all_to_all | solution.py:303
  40.9 0.9 %copy-done.2 = bf16[256,256]{1,0:T(8,128)(2,1)S(1)} copy-done((bf16[256,256]{1,0:T(8,128)(2,1)S(1)}, bf16[256,256]{1,0:T(8,128)(2,1)}, u32[]{:S(2)}) %copy-start.2) | copy-done | bytes 131096
  41.8 0.7 %copy-done.3 = bf16[48,192]{1,0:T(8,128)(2,1)S(1)} copy-done((bf16[48,192]{1,0:T(8,128)(2,1)S(1)}, bf16[48,192]{1,0:T(8,128)(2,1)}, u32[]{:S(2)}) %copy-start.3) | copy-done | bytes 18456
  42.5 0.7 %copy-done.4 = f32[48,128]{1,0:T(8,128)S(1)} copy-done((f32[48,128]{1,0:T(8,128)S(1)}, f32[48,128]{1,0:T(8,128)}, u32[]{:S(2)}) %copy-start.4) | copy-done | bytes 24600
  43.3 0.7 copy-done.5
  44.0 5.7 %pairs_1.1.refs_9_ = f32[2304,128]{1,0:T(8,128)S(1)} custom-call(s32[4,15]{1,0:T(4,128)S(1)} %bitcast.12, s32[1]{0:T(128)} %bitcast.4.refs_1_, bf16[2,48,2304]{2,1,0:T(8,128)(2,1)S(1)} %copy-done.1, bf16[48,2304]{1,0:T(8,128)(2,1)S(1)} %collective-permute-done.refs_3_, bf16[48,2304]{1,0:T(8,128)(2,1)S(1)} %collective-permute-done.3.refs_4_, ...), custom_call_target="tpu_custom_call" | custom-call | flops 382205952 | bytes 1769472 | tf_op jit(solution)/shard_map/pairs_1/pallas_call | solution.py:274
  49.7 3.3 %pairs_2.1.refs_9_ = f32[2304,128]{1,0:T(8,128)S(1)} custom-call(s32[4,15]{1,0:T(4,128)S(1)} %bitcast.13, s32[1]{0:T(128)} %bitcast.4.refs_1_, bf16[2,48,2304]{2,1,0:T(8,128)(2,1)S(1)} %copy-done.1, bf16[48,2304]{1,0:T(8,128)(2,1)S(1)} %collective-permute-done.1.refs_3_, bf16[48,2304]{1,0:T(8,128)(2,1)S(1)} %collective-permute-done.4.refs_4_, ...), custom_call_target="tpu_custom_call" | custom-call | flops 382205952 | bytes 1769472 | tf_op jit(solution)/shard_map/pairs_2/pallas_call | solution.py:274
  53.0 0.0 collective-permute-done.2.refs_3_
  53.0 0.0 collective-permute-done.5.refs_4_
  53.0 1.1 %pairs_3.1 = bf16[2,48,2304]{2,1,0:T(8,128)(2,1)S(1)} custom-call(s32[4,15]{1,0:T(4,128)S(1)} %bitcast.14, s32[1]{0:T(128)} %bitcast.4.refs_1_, bf16[2,48,2304]{2,1,0:T(8,128)(2,1)S(1)} %copy-done.1, bf16[48,2304]{1,0:T(8,128)(2,1)S(1)} %collective-permute-done.2.refs_3_, bf16[48,2304]{1,0:T(8,128)(2,1)S(1)} %collective-permute-done.5.refs_4_, ...), custom_call_target="tpu_custom_call" | custom-call | flops 382205952 | bytes 1769472 | tf_op jit(solution)/shard_map/pairs_3/pallas_call | solution.py:274
  54.1 0.6 all_to_all.17
  54.6 0.3 copy.12
  55.0 16.6 %all_to_all.21 = bf16[2,8,13824]{2,0,1:T(2,128)(2,1)S(1)} all-to-all(bf16[2,8,13824]{2,0,1:T(2,128)(2,1)S(1)} %copy.12), channel_id=1, replica_groups=mesh['grp'=4,'dev'=8] {'dev'}, dimensions={1} | all-to-all | bytes 884736 | tf_op jit(solution)/shard_map/all_to_all | solution.py:310
  71.6 0.3 convert_bitcast_fusion
  71.9 1.5 %reshape.25 = f32[16,13824]{1,0:T(8,128)} reshape(f32[8,2,13824]{2,1,0:T(2,128)S(1)} %convert_bitcast_fusion) | data formatting | bytes 1769472 | tf_op jit(solution)/shard_map/convert_element_type | solution.py:310
  (7 shorter events, 0.0 us)
Async XLA Ops:
  0.0 28.8 %copy-start = (s32[1,8,4]{1,2,0:T(4,128)S(1)}, s32[1,8,4]{1,2,0:T(4,128)}, u32[]{:S(2)}) copy-start(s32[1,8,4]{1,2,0:T(4,128)} %param.12) | copy-start | bytes 388
  0.0 40.9 %copy-start.1 = (bf16[2,48,2304]{2,1,0:T(8,128)(2,1)S(1)}, bf16[2,48,2304]{2,1,0:T(8,128)(2,1)}, u32[]{:S(2)}) copy-start(bf16[2,48,2304]{2,1,0:T(8,128)(2,1)} %refs_2_.5) | copy-start | bytes 1327108
  1.1 11.4 %collective-permute-start = (bf16[48,2304]{1,0:T(8,128)(2,1)S(1)}, bf16[48,2304]{1,0:T(8,128)(2,1)S(1)}, u32[]{:S(2)}, u32[]{:S(2)}) collective-permute-start(bf16[48,2304]{1,0:T(8,128)(2,1)S(1)} %get-tuple-element.6), channel_id=1, source_target_pairs={{0,8},{8,16},{16,24},{24,0},{1,9},{9,17},{17,25},{25,1},{2,10},{10... | collective-permute-start | bytes 663560 | tf_op jit(solution)/shard_map/ppermute | solution.py:301
  4.2 13.0 %collective-permute-start.3 = (bf16[48,2304]{1,0:T(8,128)(2,1)S(1)}, bf16[48,2304]{1,0:T(8,128)(2,1)S(1)}, u32[]{:S(2)}, u32[]{:S(2)}) collective-permute-start(bf16[48,2304]{1,0:T(8,128)(2,1)S(1)} %get-tuple-element.5), channel_id=1, source_target_pairs={{0,8},{8,16},{16,24},{24,0},{1,9},{9,17},{17,25},{25,1},{2,10},{10... | collective-permute-start | bytes 663560 | tf_op jit(solution)/shard_map/ppermute | solution.py:301
  12.5 9.6 %collective-permute-start.1 = (bf16[48,2304]{1,0:T(8,128)(2,1)S(1)}, bf16[48,2304]{1,0:T(8,128)(2,1)S(1)}, u32[]{:S(2)}, u32[]{:S(2)}) collective-permute-start(bf16[48,2304]{1,0:T(8,128)(2,1)S(1)} %collective-permute-done.refs_3_), channel_id=1, source_target_pairs={{0,8},{8,16},{16,24},{24,0},{1,9},{9,17},{17,25},{25,1},{2,10},{10... | collective-permute-start | bytes 663560 | tf_op jit(solution)/shard_map/ppermute | solution.py:301
  17.2 10.2 %collective-permute-start.4 = (bf16[48,2304]{1,0:T(8,128)(2,1)S(1)}, bf16[48,2304]{1,0:T(8,128)(2,1)S(1)}, u32[]{:S(2)}, u32[]{:S(2)}) collective-permute-start(bf16[48,2304]{1,0:T(8,128)(2,1)S(1)} %collective-permute-done.3.refs_4_), channel_id=1, source_target_pairs={{0,8},{8,16},{16,24},{24,0},{1,9},{9,17},{17,25},{25,1},{2,10},{10... | collective-permute-start | bytes 663560 | tf_op jit(solution)/shard_map/ppermute | solution.py:301
  22.1 30.8 %collective-permute-start.2 = (bf16[48,2304]{1,0:T(8,128)(2,1)S(1)}, bf16[48,2304]{1,0:T(8,128)(2,1)S(1)}, u32[]{:S(2)}, u32[]{:S(2)}) collective-permute-start(bf16[48,2304]{1,0:T(8,128)(2,1)S(1)} %collective-permute-done.1.refs_3_), channel_id=1, source_target_pairs={{0,8},{8,16},{16,24},{24,0},{1,9},{9,17},{17,25},{25,1},{2,10},{10... | collective-permute-start | bytes 663560 | tf_op jit(solution)/shard_map/ppermute | solution.py:301
  27.4 25.6 %collective-permute-start.5 = (bf16[48,2304]{1,0:T(8,128)(2,1)S(1)}, bf16[48,2304]{1,0:T(8,128)(2,1)S(1)}, u32[]{:S(2)}, u32[]{:S(2)}) collective-permute-start(bf16[48,2304]{1,0:T(8,128)(2,1)S(1)} %collective-permute-done.4.refs_4_), channel_id=1, source_target_pairs={{0,8},{8,16},{16,24},{24,0},{1,9},{9,17},{17,25},{25,1},{2,10},{10... | collective-permute-start | bytes 663560 | tf_op jit(solution)/shard_map/ppermute | solution.py:301
  30.3 10.6 %all-to-all-start = ((s32[4,1,15]{2,1,0:T(1,128)}), s32[4,1,15]{2,1,0:T(1,128)S(1)}, u32[]{:S(2)}, u32[]{:S(2)}) async-start(s32[4,1,15]{2,1,0:T(1,128)} %broadcast_in_dim.2), calls=%async_computation | async-start | bytes 4096 | tf_op jit(solution)/shard_map/all_to_all | solution.py:303
  40.9 0.9 %copy-start.2 = (bf16[256,256]{1,0:T(8,128)(2,1)S(1)}, bf16[256,256]{1,0:T(8,128)(2,1)}, u32[]{:S(2)}) copy-start(bf16[256,256]{1,0:T(8,128)(2,1)} %constant.21.clone.refs_5_) | copy-start | bytes 393220
  41.8 0.7 %copy-start.3 = (bf16[48,192]{1,0:T(8,128)(2,1)S(1)}, bf16[48,192]{1,0:T(8,128)(2,1)}, u32[]{:S(2)}) copy-start(bf16[48,192]{1,0:T(8,128)(2,1)} %constant.22.clone.refs_6_) | copy-start | bytes 55300
  42.5 0.7 %copy-start.4 = (f32[48,128]{1,0:T(8,128)S(1)}, f32[48,128]{1,0:T(8,128)}, u32[]{:S(2)}) copy-start(f32[48,128]{1,0:T(8,128)} %constant.23.clone.refs_7_) | copy-start | bytes 73732
  43.3 0.7 copy-start.5

commit v2 on v1

--- a/solution.py
+++ b/solution.py
@@ -39,7 +39,8 @@
         at = half * HALF
         base[:, at : at + n] = modes[:, None] + modes[None, :]
         outer[:, at : at + HALF] = modes[half * (n // 2) : (half + 1) * (n // 2), None]
-    return lane_side, row_side, base, outer
+    pad = np.zeros((n, 2 * LANES - 4 * n), jnp.bfloat16)
+    return np.concatenate([lane_side, np.concatenate([row_side, pad], axis=1)]), np.concatenate([base, outer])
 
 
 def split(x):
@@ -62,20 +63,23 @@
     return out[:, :LANES], out[:, LANES:]
 
 
-def pair_kernel(sizes, step, first, last, *refs):
-    n, orbs, slots, groups = sizes
+def pair_kernel(sizes, pieces, first, last, *refs):
+    n, orbs, slots = sizes
     half = n // 2
     cells_tile = half * n // LANES
     wide = n + 2 * half
     chunk = 6 if half % 6 == 0 else 2
-    meta, where_am_i, own = refs[:3]
+    mine, theirs, own = refs[:3]
     others = refs[3 : 3 + orbs]
-    lane_ref, row_ref, base_ref, outer_ref = refs[3 + orbs : 7 + orbs]
-    rest = list(refs[7 + orbs :])
+    sines, modes = refs[3 + orbs : 5 + orbs]
+    rest = list(refs[5 + orbs :])
     total_in = None if first else rest.pop(0)
-    total_out = None if last else rest.pop(0)
-    out = rest.pop(0) if last else None
-    total = rest.pop(0) if last else total_out
+    if last:
+        outs = [rest.pop(0) for _ in range(max(pieces, 1))]
+        total = rest.pop(0)
+        flat = rest.pop(0) if pieces else None
+    else:
+        total = rest.pop(0)
     dense_i, dense_j, held_i, held_j, moved, field, other = rest
 
     lane = lax.broadcasted_iota(jnp.int32, (n, LANES), 1)
@@ -89,9 +93,11 @@
 
     at_source = 3 * orbs + slots
     at_count = at_source + slots
-    at_pick = at_count + 1
-    me = where_am_i[0]
-    them = lax.rem(me + groups - step, groups)
+    at_group = at_count + 1
+    at_pick = at_group + 2
+    me = mine[0, at_group]
+    them = theirs[0, at_group]
+    member = mine[0, at_group + 1]
 
     def unpack(dense, put):
         for yo in range(half):
@@ -139,17 +145,25 @@
         return jnp.concatenate([top, bottom], axis=0)
 
     def task(which, carry):
-        lister = jnp.where(which == 0, me, them)
-        source = jnp.where(which == 0, them, me)
-        listed = meta[lister, at_count]
+        outgoing = which == 0
+
+        def lister(k):
+            return jnp.where(outgoing, mine[0, k], theirs[0, k])
+
+        def source(k):
+            return jnp.where(outgoing, theirs[0, k], mine[0, k])
+
+        lister_group = jnp.where(outgoing, me, them)
+        source_group = jnp.where(outgoing, them, me)
+        listed = lister(at_count)
         i_at = jnp.int32(0)
         found = jnp.int32(0)
         for p in range(slots):
-            hit = (meta[lister, at_source + p] == source) & (p < listed)
-            i_at = jnp.where(hit, meta[lister, 3 * orbs + p], i_at)
+            hit = (lister(at_source + p) == source_group) & (p < listed)
+            i_at = jnp.where(hit, lister(3 * orbs + p), i_at)
             found = jnp.where(hit, 1, found)
-        j_at = meta[source, at_pick + lister]
-        gap = [meta[lister, i_at * 3 + k] - meta[source, j_at * 3 + k] for k in range(3)]
+        j_at = source(at_pick + lister_group)
+        gap = [lister(i_at * 3 + k) - source(j_at * 3 + k) for k in range(3)]
 
         @pl.when(found == 1)
         def _():
@@ -182,8 +196,8 @@
                 moved[yo * n : (yo + 1) * n, :] = tile
 
             shifted(gap, use_moved)
-            lane_side = lane_ref[...]
-            row_side = row_ref[...]
+            lane_side = sines[: 2 * LANES, :]
+            row_side = sines[2 * LANES :, : 4 * n]
             rows = chunk * n
             for c in range(half // chunk):
                 here = slice(c * rows, (c + 1) * rows)
@@ -195,7 +209,7 @@
                         field[at : at + n, :] = pair[k]
             for xo in range(0, half, 2):
                 pair = row_turn([swapped(field, xo + k) for k in range(2)], row_side)
-                pair = [pair[k] / (base_ref[...] + outer_ref[xo + k : xo + k + 1, :]) for k in range(2)]
+                pair = [pair[k] / (modes[:n, :] + modes[n + xo + k : n + xo + k + 1, :]) for k in range(2)]
                 pair = row_turn(pair, row_side)
                 for k in range(2):
                     other[(xo + k) * n : (xo + k + 1) * n, :] = pair[k]
@@ -241,19 +255,33 @@
                     piece = pltpu.roll(tile, amount, 1) if amount else tile
                     current[t] = jnp.where(lane >= start, piece, current[t]) if t in current else piece
                     if start + n >= LANES:
-                        out[a, :, t * LANES : (t + 1) * LANES] = current.pop(t).astype(bf16)
+                        here = slice(t * LANES, (t + 1) * LANES)
+                        if pieces:
+                            flat[pl.ds(t * orbs * n + a, n, stride=orbs), :] = current.pop(t)
+                        else:
+                            outs[0][a, :, here] = current.pop(t).astype(bf16)
                         if start + n > LANES:
                             current[t + 1] = piece
-
-
-def pair_step(step, first, last, meta, where_am_i, own, others, tables, total):
+        depth = n // pieces * orbs if pieces else 0
+        tiles = n * n // LANES
+        for k in range(pieces):
+            at = jnp.bitwise_xor(member, k) * depth
+            for t in range(tiles):
+                outs[k][:, t * LANES : (t + 1) * LANES] = flat[pl.ds(t * orbs * n + at, 8), :].astype(bf16)
+            for t in range(tiles // 2):
+                tail = [flat[pl.ds((t + h * tiles // 2) * orbs * n + at + 8, 4), :] for h in range(2)]
+                tail_at = (tiles + t) * LANES
+                outs[k][:, tail_at : tail_at + LANES] = jnp.concatenate(tail, axis=0).astype(bf16)
+
+
+def pair_step(step, pieces, first, last, mine, theirs, own, others, tables, total):
     orbs, n, plane = own.shape
-    groups = meta.shape[0]
     half = n // 2
-    slots = (meta.shape[1] - 3 * orbs - 1 - groups) // 2
+    slots = pieces[1]
+    pieces = pieces[0] if last else 0
     vmem = pl.BlockSpec(memory_space=pltpu.VMEM)
     smem = pl.BlockSpec(memory_space=pltpu.SMEM)
-    operands = [meta, where_am_i, own, *others, *tables]
+    operands = [mine, theirs, own, *others, *tables]
     specs = [smem, smem] + [vmem] * (1 + orbs + len(tables))
     if not first:
         operands.append(total)
@@ -269,13 +297,18 @@
         pltpu.VMEM((rows, LANES), f32),
         pltpu.VMEM((rows, LANES), f32),
     ]
+    shapes = held
     if last:
+        shapes = jax.ShapeDtypeStruct(own.shape, bf16)
+        if pieces:
+            scratch.insert(0, pltpu.VMEM((orbs * n * plane // LANES, LANES), f32))
+            shapes = [jax.ShapeDtypeStruct((8, orbs * n * plane // pieces // 8), bf16)] * pieces
         scratch.insert(0, pltpu.VMEM(held.shape, f32))
     return pl.pallas_call(
-        functools.partial(pair_kernel, (n, orbs, slots, groups), step, first, last),
-        out_shape=jax.ShapeDtypeStruct(own.shape, bf16) if last else held,
+        functools.partial(pair_kernel, (n, orbs, slots), pieces, first, last),
+        out_shape=shapes,
         in_specs=specs,
-        out_specs=vmem,
+        out_specs=[vmem] * pieces if pieces else vmem,
         scratch_shapes=scratch,
         compiler_params=pltpu.CompilerParams(vmem_limit_bytes=32 << 20),
         cost_estimate=pl.CostEstimate(flops=2 * 12 * 3 * n**4, bytes_accessed=4 * n**3 * 4, transcendentals=0),
@@ -283,31 +316,88 @@
     )(*operands)
 
 
+def gather_kernel(n, orbs, member_ref, *refs):
+    devices = len(refs) - 3
+    out, rows, mixed = refs[devices:]
+    tiles = n * n // LANES
+    member = member_ref[0]
+    for k in range(devices):
+        at = pl.multiple_of(jnp.bitwise_xor(member, k) * 8, 8)
+        for t in range(tiles * 3 // 2):
+            rows[pl.ds(t * devices * 8 + at, 8), :] = refs[k][:, t * LANES : (t + 1) * LANES].astype(f32)
+    for x in range(n // devices):
+        for t in range(tiles):
+            here = slice((x * tiles + t) * LANES, (x * tiles + t + 1) * LANES)
+            at = (x * tiles + t) * orbs * devices
+            for a in range(orbs):
+                q = x * orbs + a
+                tile = t
+                if q >= 8:
+                    q += 4 * (t * 2 // tiles) - 8
+                    tile = tiles + t % (tiles // 2)
+                mixed[pl.ds(at + a, devices, stride=orbs), :] = rows[
+                    pl.ds(tile * devices * 8 + q, devices, stride=8), :
+                ]
+            out[:, here] = mixed[at : at + orbs * devices, :]
+
+
 def body(orbitals, offsets, pick, pair_local, pair_source, pair_count):
     orbs, n, plane = orbitals.shape
     groups = lax.axis_size("grp")
+    devices = lax.axis_size("dev")
     me = lax.axis_index("grp").astype(jnp.int32)
-    member = lax.axis_index("dev")
+    member = lax.axis_index("dev").astype(jnp.int32)
     my_pick = lax.dynamic_slice_in_dim(pick[0], member, 1, 0)[0]
     mine = jnp.concatenate(
-        [offsets.reshape(-1), pair_local[0, 0], pair_source[0, 0], pair_count[0, 0], my_pick]
-    ).astype(jnp.int32)
+        [
+            offsets.reshape(-1),
+            pair_local[0, 0],
+            pair_source[0, 0],
+            pair_count[0, 0],
+            me.reshape(1),
+            member.reshape(1),
+            my_pick,
+        ]
+    ).astype(jnp.int32)[None, :]
+    by_pieces = devices & (devices - 1) == 0 and n % devices == 0 and n // devices * orbs == 12
+    pieces = devices if by_pieces else 0
     ring = [(g, (g + 1) % groups) for g in range(groups)]
     held = [orbitals[q] for q in range(orbs)]
     tables = [jnp.asarray(t) for t in np_tables(n)]
-    meta = None
+    theirs = mine
     total = None
     for step in range(1, groups):
         held = [lax.ppermute(h, "grp", ring) for h in held]
-        if meta is None:
-            meta = lax.all_to_all(
-                jnp.broadcast_to(mine[None, :], (groups, mine.shape[0])), "grp", 0, 0, tiled=True
-            )
+        theirs = lax.ppermute(theirs, "grp", ring)
+        held[0], theirs, total = lax.optimization_barrier((held[0], theirs, total))
         total = pair_step(
-            step, step == 1, step == groups - 1, meta, me.reshape(1), orbitals, held, tables, total
+            step,
+            (pieces, pair_local.shape[2]),
+            step == 1,
+            step == groups - 1,
+            mine,
+            theirs,
+            orbitals,
+            held,
+            tables,
+            total,
         )
-    whole = total.reshape(orbs, n * plane)
-    return lax.all_to_all(whole, "dev", split_axis=1, concat_axis=0, tiled=True).astype(f32)
+    if not pieces:
+        whole = total.reshape(orbs, n * plane)
+        return lax.all_to_all(whole, "dev", split_axis=1, concat_axis=0, tiled=True).astype(f32)
+    arrived = [total[0]]
+    for k in range(1, devices):
+        arrived.append(lax.ppermute(total[k], "dev", [(d, d ^ k) for d in range(devices)]))
+    vmem = pl.BlockSpec(memory_space=pltpu.VMEM)
+    return pl.pallas_call(
+        functools.partial(gather_kernel, n, orbs),
+        out_shape=jax.ShapeDtypeStruct((orbs * devices, n * plane // devices), f32),
+        in_specs=[pl.BlockSpec(memory_space=pltpu.SMEM)] + [vmem] * devices,
+        out_specs=vmem,
+        scratch_shapes=[pltpu.VMEM((orbs * n * plane // LANES, LANES), f32)] * 2,
+        compiler_params=pltpu.CompilerParams(vmem_limit_bytes=32 << 20),
+        name="cells",
+    )(member.reshape(1), *arrived)
 
 
 def solution(mesh):

time: 74.3 us -> 58.5 us (0.79); the launches traced: 73.4 us -> 59.4 us
  blocking collectives: 16.6 us -> 0 us
  starting transfers between devices: 9.81 us -> 18.8 us
  local copies, waits for them, and re-layouts: 8.91 us -> 4.51 us
  waiting for transfers between devices: 27 us -> 23.9 us
  Pallas kernels: 10 us -> 11.5 us
    ppermute x0 -> x10, waiting for transfers between devices: none -> 23.9 us  [the longest x3 20.2 us: body(): theirs = lax.ppermute(theirs, 'grp', ring)]
    ppermute x6, waiting for transfers between devices: 21.5 us -> 0.02 us  [body(): held = [lax.ppermute(h, 'grp', ring) for h in held]]
    all_to_all x1 -> x0, blocking collectives: 16.6 us -> none  [body(): lax.all_to_all(whole, 'dev', split_axis=1, concat_axis=0, tiled=True)]
    ppermute x0 -> x10, starting transfers between devices: none -> 12.8 us  [the longest x7 8.96 us: body(): lax.ppermute(total[k], 'dev', [(d, d ^ k) for d in range(devices)])]
    all_to_all x1 -> x0, waiting for transfers between devices: 5.47 us -> none  [body(): lax.all_to_all(jnp.broadcast_to(mine[None, :], (groups, mine.shape[0])),...]
    all_to_all x1 -> x0, starting transfers between devices: 5.09 us -> none  [body(): lax.all_to_all(jnp.broadcast_to(mine[None, :], (groups, mine.shape[0])),...]
    convert_element_type x1 -> x0, local copies, waits for them, and re-layouts: 1.52 us -> none  [body(): lax.all_to_all(whole, 'dev', split_axis=1, concat_axis=0, tiled=True)]
    pallas_call x3 -> x4, Pallas kernels: 10 us -> 11.5 us  [the longest x3 10.2 us: pair_step(): pl.pallas_call(functools.partial(pair_kernel, (n, orbs, slots), pieces, f...]
  transfers between devices with their start and end apart: 7 -> 16, of which waited for: 5 -> 5; matrix products, arithmetic and copies ran while one was open for 3% -> 3% of each run, Pallas kernels for 12% -> 11%
where the time goes in v2:
time: 58.5 us; the launch traced here: 59.4 us
  waiting for transfers between devices  23.9 us (41%)
  starting transfers between devices  18.8 us (32%)
  Pallas kernels  11.5 us (20%)
  local copies, waits for them, and re-layouts  4.51 us (8%)
  between operations  0.72 us (1%)
    ppermute x3, waiting for transfers between devices, body(): theirs = lax.ppermute(theirs, 'grp', ring)  20.2 us
    pallas_call x3, Pallas kernels, pair_step(): pl.pallas_call(functools.partial(pair_kernel, (n, orbs, slots), pieces, f...  10.2 us
    ppermute x7, starting transfers between devices, body(): lax.ppermute(total[k], 'dev', [(d, d ^ k) for d in range(devices)])  8.96 us
    ppermute x6, starting transfers between devices, body(): held = [lax.ppermute(h, 'grp', ring) for h in held]  6 us
    ppermute x3, starting transfers between devices, body(): theirs = lax.ppermute(theirs, 'grp', ring)  3.84 us
    ppermute x7, waiting for transfers between devices, body(): lax.ppermute(total[k], 'dev', [(d, d ^ k) for d in range(devices)])  3.61 us
    unnamed x8, local copies, waits for them, and re-layouts  1.69 us
    pallas_call x1, Pallas kernels, body(): pl.pallas_call(functools.partial(gather_kernel, n, orbs), out_shape=jax.S...  1.3 us
  transfers between devices with their start and end apart: 16, of which 5 were waited for; matrix products, arithmetic and copies ran while one was open for 3% of the time, Pallas kernels for 11%

profile of v2, /device:TPU:0, one launch (start us, length us, event | category | flops | bytes accessed | tf_op | source)
XLA Modules:
  0.0 59.4 jit_solution(8474563083379697553)
XLA Ops:
  0.0 1.1 %slice_bitcast_fusion = (bf16[48,2304]{1,0:T(8,128)(2,1)S(1)}, bf16[48,2304]{1,0:T(8,128)(2,1)S(1)}) fusion(bf16[2,48,2304]{2,1,0:T(8,128)(2,1)} %refs_2_.5), kind=kLoop, calls=%fused_computation | loop fusion | bytes 884736 | tf_op jit(solution)/shard_map/squeeze | solution.py:365
  1.1 3.1 %collective-permute-start = (bf16[48,2304]{1,0:T(8,128)(2,1)S(1)}, bf16[48,2304]{1,0:T(8,128)(2,1)S(1)}, u32[]{:S(2)}, u32[]{:S(2)}) collective-permute-start(bf16[48,2304]{1,0:T(8,128)(2,1)S(1)} %get-tuple-element.38), channel_id=1, source_target_pairs={{0,8},{8,16},{16,24},{24,0},{1,9},{9,17},{17,25},{25,1},{2,10},{10... | collective-permute-start | bytes 663560 | tf_op jit(solution)/shard_map/ppermute | solution.py:370
  4.2 1.6 %collective-permute-start.4 = (bf16[48,2304]{1,0:T(8,128)(2,1)S(1)}, bf16[48,2304]{1,0:T(8,128)(2,1)S(1)}, u32[]{:S(2)}, u32[]{:S(2)}) collective-permute-start(bf16[48,2304]{1,0:T(8,128)(2,1)S(1)} %get-tuple-element.37), channel_id=1, source_target_pairs={{0,8},{8,16},{16,24},{24,0},{1,9},{9,17},{17,25},{25,1},{2,10},{10... | collective-permute-start | bytes 663560 | tf_op jit(solution)/shard_map/ppermute | solution.py:370
  6.4 0.8 %reshape.13 = s32[6]{0:T(128)S(1)} reshape(s32[2,3]{1,0:T(2,128)} %param.9) | data formatting | bytes 48 | tf_op jit(solution)/shard_map/reshape | solution.py:353
  7.2 0.2 dynamic-slice_reduce_fusion
  7.4 0.8 %concatenate.3 = s32[17]{0:T(128)S(1)} concatenate(s32[6]{0:T(128)S(1)} %reshape.13, s32[2]{0:T(128)} %bitcast.15, s32[2]{0:T(128)} %bitcast.16, s32[1]{0:T(128)} %bitcast.10, s32[1]{0:T(128)} %bitcast.4, s32[1]{0:T(128)} %bitcast.member_ref, s32[4]{0:T(128)S(1)} %dynamic-slice_reduce_fusion), dimensions={0} | concatenate | bytes 136 | tf_op jit(solution)/shard_map/concatenate | solution.py:351
  8.1 1.6 %collective-permute-start.1 = (s32[1,17]{1,0:T(1,128)S(1)}, s32[1,17]{1,0:T(1,128)S(1)}, u32[]{:S(2)}, u32[]{:S(2)}) collective-permute-start(s32[1,17]{1,0:T(1,128)S(1)} %bitcast.11), channel_id=1, source_target_pairs={{0,8},{8,16},{16,24},{24,0},{1,9},{9,17},{17,25},{25,1},{2,10},{10... | collective-permute-start | bytes 212 | tf_op jit(solution)/shard_map/ppermute | solution.py:371
  9.7 6.8 %collective-permute-done.1.refs_1_ = s32[1,17]{1,0:T(1,128)S(1)} collective-permute-done((s32[1,17]{1,0:T(1,128)S(1)}, s32[1,17]{1,0:T(1,128)S(1)}, u32[]{:S(2)}, u32[]{:S(2)}) %collective-permute-start.1) | collective-permute-done | bytes 100 | tf_op jit(solution)/shard_map/ppermute | solution.py:371
  16.5 0.0 collective-permute-start.2
  16.5 0.0 collective-permute-done.4.refs_4_
  16.5 1.3 %collective-permute-start.7 = (bf16[48,2304]{1,0:T(8,128)(2,1)S(1)}, bf16[48,2304]{1,0:T(8,128)(2,1)S(1)}, u32[]{:S(2)}, u32[]{:S(2)}) collective-permute-start(bf16[48,2304]{1,0:T(8,128)(2,1)S(1)} %collective-permute-done.4.refs_4_), channel_id=1, source_target_pairs={{0,8},{8,16},{16,24},{24,0},{1,9},{9,17},{17,25},{25,1},{2,10},{10... | collective-permute-start | bytes 663560 | tf_op jit(solution)/shard_map/ppermute | solution.py:370
  17.8 1.6 %collective-permute-start.3 = (s32[1,17]{1,0:T(1,128)S(1)}, s32[1,17]{1,0:T(1,128)S(1)}, u32[]{:S(2)}, u32[]{:S(2)}) collective-permute-start(s32[1,17]{1,0:T(1,128)S(1)} %collective-permute-done.1.refs_1_), channel_id=1, source_target_pairs={{0,8},{8,16},{16,24},{24,0},{1,9},{9,17},{17,25},{25,1},{2,10},{10... | collective-permute-start | bytes 212 | tf_op jit(solution)/shard_map/ppermute | solution.py:371
  19.4 0.9 %copy-done.2 = bf16[304,256]{1,0:T(8,128)(2,1)S(1)} copy-done((bf16[304,256]{1,0:T(8,128)(2,1)S(1)}, bf16[304,256]{1,0:T(8,128)(2,1)}, u32[]{:S(2)}) %copy-start.2) | copy-done | bytes 155672
  20.3 0.8 %copy-done.3 = f32[72,128]{1,0:T(8,128)S(1)} copy-done((f32[72,128]{1,0:T(8,128)S(1)}, f32[72,128]{1,0:T(8,128)}, u32[]{:S(2)}) %copy-start.3) | copy-done | bytes 36888
  21.0 3.2 %pairs_1.1.refs_7_ = f32[2304,128]{1,0:T(8,128)S(1)} custom-call(s32[1,17]{1,0:T(1,128)S(1)} %bitcast.12, s32[1,17]{1,0:T(1,128)S(1)} %collective-permute-done.1.refs_1_, bf16[2,48,2304]{2,1,0:T(8,128)(2,1)S(1)} %copy-done.1, bf16[48,2304]{1,0:T(8,128)(2,1)S(1)} %collective-permute-done.refs_3_, bf16[48,2304]{1,0:T(8,128)(2,1)S(1)} %collective-permute-done.4.refs_4_, ...), custom_call_target="tpu_custom_call" | custom-call | flops 382205952 | bytes 1769472 | tf_op jit(solution)/shard_map/pairs_1/pallas_call | solution.py:307
  24.3 5.3 %collective-permute-done.3.refs_1_ = s32[1,17]{1,0:T(1,128)S(1)} collective-permute-done((s32[1,17]{1,0:T(1,128)S(1)}, s32[1,17]{1,0:T(1,128)S(1)}, u32[]{:S(2)}, u32[]{:S(2)}) %collective-permute-start.3) | collective-permute-done | bytes 100 | tf_op jit(solution)/shard_map/ppermute | solution.py:371
  29.6 0.0 collective-permute-done.2.refs_3_
  29.6 0.1 collective-permute-start.8
  29.7 0.7 %collective-permute-start.6 = (s32[1,17]{1,0:T(1,128)S(1)}, s32[1,17]{1,0:T(1,128)S(1)}, u32[]{:S(2)}, u32[]{:S(2)}) collective-permute-start(s32[1,17]{1,0:T(1,128)S(1)} %collective-permute-done.3.refs_1_), channel_id=1, source_target_pairs={{0,8},{8,16},{16,24},{24,0},{1,9},{9,17},{17,25},{25,1},{2,10},{10... | collective-permute-start | bytes 212 | tf_op jit(solution)/shard_map/ppermute | solution.py:371
  30.4 3.3 %pairs_2.1.refs_7_ = f32[2304,128]{1,0:T(8,128)S(1)} custom-call(s32[1,17]{1,0:T(1,128)S(1)} %bitcast.13, s32[1,17]{1,0:T(1,128)S(1)} %collective-permute-done.3.refs_1_, bf16[2,48,2304]{2,1,0:T(8,128)(2,1)S(1)} %copy-done.1, bf16[48,2304]{1,0:T(8,128)(2,1)S(1)} %collective-permute-done.2.refs_3_, bf16[48,2304]{1,0:T(8,128)(2,1)S(1)} %collective-permute-done.7.refs_4_, ...), custom_call_target="tpu_custom_call" | custom-call | flops 382205952 | bytes 1769472 | tf_op jit(solution)/shard_map/pairs_2/pallas_call | solution.py:307
  33.7 8.1 %collective-permute-done.6.refs_1_ = s32[1,17]{1,0:T(1,128)S(1)} collective-permute-done((s32[1,17]{1,0:T(1,128)S(1)}, s32[1,17]{1,0:T(1,128)S(1)}, u32[]{:S(2)}, u32[]{:S(2)}) %collective-permute-start.6) | collective-permute-done | bytes 100 | tf_op jit(solution)/shard_map/ppermute | solution.py:371
  41.8 0.0 collective-permute-done.5.refs_3_
  41.8 3.7 %pairs_3.1 = (bf16[8,3456]{1,0:T(8,128)(2,1)S(1)}, bf16[8,3456]{1,0:T(8,128)(2,1)S(1)}, bf16[8,3456]{1,0:T(8,128)(2,1)S(1)}, bf16[8,3456]{1,0:T(8,128)(2,1)S(1)}...) custom-call(s32[1,17]{1,0:T(1,128)S(1)} %bitcast.14, ...), custom_call_target="tpu_custom_call" | custom-call | flops 382205952 | bytes 1769472 | tf_op jit(solution)/shard_map/pairs_3/pallas_call | solution.py:307
  45.5 1.3 %collective-permute-start.10 = (bf16[8,3456]{1,0:T(8,128)(2,1)S(1)}, bf16[8,3456]{1,0:T(8,128)(2,1)S(1)}, u32[]{:S(2)}, u32[]{:S(2)}) collective-permute-start(bf16[8,3456]{1,0:T(8,128)(2,1)S(1)} %get-tuple-element.31), channel_id=1, source_target_pairs={{0,2},{1,3},{2,0},{3,1},{4,6},{5,7},{6,4},{7,5},{8,10},{9,11},{10,... | collective-permute-start | bytes 165896 | tf_op jit(solution)/shard_map/ppermute | solution.py:390
  46.8 0.0 collective-permute-start.11
  46.8 3.9 %collective-permute-start.12 = (bf16[8,3456]{1,0:T(8,128)(2,1)S(1)}, bf16[8,3456]{1,0:T(8,128)(2,1)S(1)}, u32[]{:S(2)}, u32[]{:S(2)}) collective-permute-start(bf16[8,3456]{1,0:T(8,128)(2,1)S(1)} %get-tuple-element.33), channel_id=1, source_target_pairs={{0,4},{1,5},{2,6},{3,7},{4,0},{5,1},{6,2},{7,3},{8,12},{9,13},{10,... | collective-permute-start | bytes 165896 | tf_op jit(solution)/shard_map/ppermute | solution.py:390
  50.7 0.0 collective-permute-start.13
  50.7 2.9 %collective-permute-start.14 = (bf16[8,3456]{1,0:T(8,128)(2,1)S(1)}, bf16[8,3456]{1,0:T(8,128)(2,1)S(1)}, u32[]{:S(2)}, u32[]{:S(2)}) collective-permute-start(bf16[8,3456]{1,0:T(8,128)(2,1)S(1)} %get-tuple-element.35), channel_id=1, source_target_pairs={{0,6},{1,7},{2,4},{3,5},{4,2},{5,3},{6,0},{7,1},{8,14},{9,15},{10,... | collective-permute-start | bytes 165896 | tf_op jit(solution)/shard_map/ppermute | solution.py:390
  53.6 0.9 %collective-permute-start.9 = (bf16[8,3456]{1,0:T(8,128)(2,1)S(1)}, bf16[8,3456]{1,0:T(8,128)(2,1)S(1)}, u32[]{:S(2)}, u32[]{:S(2)}) collective-permute-start(bf16[8,3456]{1,0:T(8,128)(2,1)S(1)} %get-tuple-element.30), channel_id=1, source_target_pairs={{0,1},{1,0},{2,3},{3,2},{4,5},{5,4},{6,7},{7,6},{8,9},{9,8},{10,11... | collective-permute-start | bytes 165896 | tf_op jit(solution)/shard_map/ppermute | solution.py:390
  54.5 1.5 %collective-permute-done.13.refs_5_ = bf16[8,3456]{1,0:T(8,128)(2,1)S(1)} collective-permute-done((bf16[8,3456]{1,0:T(8,128)(2,1)S(1)}, bf16[8,3456]{1,0:T(8,128)(2,1)S(1)}, u32[]{:S(2)}, u32[]{:S(2)}) %collective-permute-start.13) | collective-permute-done | bytes 55328 | tf_op jit(solution)/shard_map/ppermute | solution.py:390
  56.0 2.1 %collective-permute-done.15.refs_7_ = bf16[8,3456]{1,0:T(8,128)(2,1)S(1)} collective-permute-done((bf16[8,3456]{1,0:T(8,128)(2,1)S(1)}, bf16[8,3456]{1,0:T(8,128)(2,1)S(1)}, u32[]{:S(2)}, u32[]{:S(2)}) %collective-permute-start.15) | collective-permute-done | bytes 55328 | tf_op jit(solution)/shard_map/ppermute | solution.py:390
  58.1 1.3 %cells.1 = f32[16,13824]{1,0:T(8,128)} custom-call(s32[1]{0:T(128)} %bitcast.member_ref, bf16[8,3456]{1,0:T(8,128)(2,1)S(1)} %get-tuple-element.29.refs_0_, bf16[8,3456]{1,0:T(8,128)(2,1)S(1)} %collective-permute-done.9.refs_1_, bf16[8,3456]{1,0:T(8,128)(2,1)S(1)} %collective-permute-done.10.refs_2_, bf16[8,3456]{1,0:T(8,128)(2,1)S(1)} %collective-permute-done.11.refs_3_, ...), custom_call_target="tpu_custom_call" | custom-call | tf_op jit(solution)/shard_map/cells/pallas_call | solution.py:392
  (16 shorter events, 0.0 us)
Async XLA Ops:
  0.0 7.2 %copy-start = (s32[1,8,4]{1,2,0:T(4,128)S(1)}, s32[1,8,4]{1,2,0:T(4,128)}, u32[]{:S(2)}) copy-start(s32[1,8,4]{1,2,0:T(4,128)} %param.10) | copy-start | bytes 388
  0.0 19.3 %copy-start.1 = (bf16[2,48,2304]{2,1,0:T(8,128)(2,1)S(1)}, bf16[2,48,2304]{2,1,0:T(8,128)(2,1)}, u32[]{:S(2)}) copy-start(bf16[2,48,2304]{2,1,0:T(8,128)(2,1)} %refs_2_.5) | copy-start | bytes 1327108
  1.1 15.3 %collective-permute-start = (bf16[48,2304]{1,0:T(8,128)(2,1)S(1)}, bf16[48,2304]{1,0:T(8,128)(2,1)S(1)}, u32[]{:S(2)}, u32[]{:S(2)}) collective-permute-start(bf16[48,2304]{1,0:T(8,128)(2,1)S(1)} %get-tuple-element.38), channel_id=1, source_target_pairs={{0,8},{8,16},{16,24},{24,0},{1,9},{9,17},{17,25},{25,1},{2,10},{10... | collective-permute-start | bytes 663560 | tf_op jit(solution)/shard_map/ppermute | solution.py:370
  4.2 12.3 %collective-permute-start.4 = (bf16[48,2304]{1,0:T(8,128)(2,1)S(1)}, bf16[48,2304]{1,0:T(8,128)(2,1)S(1)}, u32[]{:S(2)}, u32[]{:S(2)}) collective-permute-start(bf16[48,2304]{1,0:T(8,128)(2,1)S(1)} %get-tuple-element.37), channel_id=1, source_target_pairs={{0,8},{8,16},{16,24},{24,0},{1,9},{9,17},{17,25},{25,1},{2,10},{10... | collective-permute-start | bytes 663560 | tf_op jit(solution)/shard_map/ppermute | solution.py:370
  8.1 8.3 %collective-permute-start.1 = (s32[1,17]{1,0:T(1,128)S(1)}, s32[1,17]{1,0:T(1,128)S(1)}, u32[]{:S(2)}, u32[]{:S(2)}) collective-permute-start(s32[1,17]{1,0:T(1,128)S(1)} %bitcast.11), channel_id=1, source_target_pairs={{0,8},{8,16},{16,24},{24,0},{1,9},{9,17},{17,25},{25,1},{2,10},{10... | collective-permute-start | bytes 212 | tf_op jit(solution)/shard_map/ppermute | solution.py:371
  16.5 13.2 %collective-permute-start.2 = (bf16[48,2304]{1,0:T(8,128)(2,1)S(1)}, bf16[48,2304]{1,0:T(8,128)(2,1)S(1)}, u32[]{:S(2)}, u32[]{:S(2)}) collective-permute-start(bf16[48,2304]{1,0:T(8,128)(2,1)S(1)} %collective-permute-done.refs_3_), channel_id=1, source_target_pairs={{0,8},{8,16},{16,24},{24,0},{1,9},{9,17},{17,25},{25,1},{2,10},{10... | collective-permute-start | bytes 663560 | tf_op jit(solution)/shard_map/ppermute | solution.py:370
  16.5 13.2 %collective-permute-start.7 = (bf16[48,2304]{1,0:T(8,128)(2,1)S(1)}, bf16[48,2304]{1,0:T(8,128)(2,1)S(1)}, u32[]{:S(2)}, u32[]{:S(2)}) collective-permute-start(bf16[48,2304]{1,0:T(8,128)(2,1)S(1)} %collective-permute-done.4.refs_4_), channel_id=1, source_target_pairs={{0,8},{8,16},{16,24},{24,0},{1,9},{9,17},{17,25},{25,1},{2,10},{10... | collective-permute-start | bytes 663560 | tf_op jit(solution)/shard_map/ppermute | solution.py:370
  17.8 11.9 %collective-permute-start.3 = (s32[1,17]{1,0:T(1,128)S(1)}, s32[1,17]{1,0:T(1,128)S(1)}, u32[]{:S(2)}, u32[]{:S(2)}) collective-permute-start(s32[1,17]{1,0:T(1,128)S(1)} %collective-permute-done.1.refs_1_), channel_id=1, source_target_pairs={{0,8},{8,16},{16,24},{24,0},{1,9},{9,17},{17,25},{25,1},{2,10},{10... | collective-permute-start | bytes 212 | tf_op jit(solution)/shard_map/ppermute | solution.py:371
  19.4 0.9 %copy-start.2 = (bf16[304,256]{1,0:T(8,128)(2,1)S(1)}, bf16[304,256]{1,0:T(8,128)(2,1)}, u32[]{:S(2)}) copy-start(bf16[304,256]{1,0:T(8,128)(2,1)} %constant.17.clone.refs_5_) | copy-start | bytes 466948
  20.3 0.8 %copy-start.3 = (f32[72,128]{1,0:T(8,128)S(1)}, f32[72,128]{1,0:T(8,128)}, u32[]{:S(2)}) copy-start(f32[72,128]{1,0:T(8,128)} %constant.18.clone.refs_6_) | copy-start | bytes 110596
  29.6 12.2 %collective-permute-start.5 = (bf16[48,2304]{1,0:T(8,128)(2,1)S(1)}, bf16[48,2304]{1,0:T(8,128)(2,1)S(1)}, u32[]{:S(2)}, u32[]{:S(2)}) collective-permute-start(bf16[48,2304]{1,0:T(8,128)(2,1)S(1)} %collective-permute-done.2.refs_3_), channel_id=1, source_target_pairs={{0,8},{8,16},{16,24},{24,0},{1,9},{9,17},{17,25},{25,1},{2,10},{10... | collective-permute-start | bytes 663560 | tf_op jit(solution)/shard_map/ppermute | solution.py:370
  29.6 12.2 %collective-permute-start.8 = (bf16[48,2304]{1,0:T(8,128)(2,1)S(1)}, bf16[48,2304]{1,0:T(8,128)(2,1)S(1)}, u32[]{:S(2)}, u32[]{:S(2)}) collective-permute-start(bf16[48,2304]{1,0:T(8,128)(2,1)S(1)} %collective-permute-done.7.refs_4_), channel_id=1, source_target_pairs={{0,8},{8,16},{16,24},{24,0},{1,9},{9,17},{17,25},{25,1},{2,10},{10... | collective-permute-start | bytes 663560 | tf_op jit(solution)/shard_map/ppermute | solution.py:370
  29.7 12.1 %collective-permute-start.6 = (s32[1,17]{1,0:T(1,128)S(1)}, s32[1,17]{1,0:T(1,128)S(1)}, u32[]{:S(2)}, u32[]{:S(2)}) collective-permute-start(s32[1,17]{1,0:T(1,128)S(1)} %collective-permute-done.3.refs_1_), channel_id=1, source_target_pairs={{0,8},{8,16},{16,24},{24,0},{1,9},{9,17},{17,25},{25,1},{2,10},{10... | collective-permute-start | bytes 212 | tf_op jit(solution)/shard_map/ppermute | solution.py:371
  45.5 8.1 %collective-permute-start.10 = (bf16[8,3456]{1,0:T(8,128)(2,1)S(1)}, bf16[8,3456]{1,0:T(8,128)(2,1)S(1)}, u32[]{:S(2)}, u32[]{:S(2)}) collective-permute-start(bf16[8,3456]{1,0:T(8,128)(2,1)S(1)} %get-tuple-element.31), channel_id=1, source_target_pairs={{0,2},{1,3},{2,0},{3,1},{4,6},{5,7},{6,4},{7,5},{8,10},{9,11},{10,... | collective-permute-start | bytes 165896 | tf_op jit(solution)/shard_map/ppermute | solution.py:390
  46.8 6.8 %collective-permute-start.11 = (bf16[8,3456]{1,0:T(8,128)(2,1)S(1)}, bf16[8,3456]{1,0:T(8,128)(2,1)S(1)}, u32[]{:S(2)}, u32[]{:S(2)}) collective-permute-start(bf16[8,3456]{1,0:T(8,128)(2,1)S(1)} %get-tuple-element.32), channel_id=1, source_target_pairs={{0,3},{1,2},{2,1},{3,0},{4,7},{5,6},{6,5},{7,4},{8,11},{9,10},{10,... | collective-permute-start | bytes 165896 | tf_op jit(solution)/shard_map/ppermute | solution.py:390
  46.8 7.7 %collective-permute-start.12 = (bf16[8,3456]{1,0:T(8,128)(2,1)S(1)}, bf16[8,3456]{1,0:T(8,128)(2,1)S(1)}, u32[]{:S(2)}, u32[]{:S(2)}) collective-permute-start(bf16[8,3456]{1,0:T(8,128)(2,1)S(1)} %get-tuple-element.33), channel_id=1, source_target_pairs={{0,4},{1,5},{2,6},{3,7},{4,0},{5,1},{6,2},{7,3},{8,12},{9,13},{10,... | collective-permute-start | bytes 165896 | tf_op jit(solution)/shard_map/ppermute | solution.py:390
  50.7 5.3 %collective-permute-start.13 = (bf16[8,3456]{1,0:T(8,128)(2,1)S(1)}, bf16[8,3456]{1,0:T(8,128)(2,1)S(1)}, u32[]{:S(2)}, u32[]{:S(2)}) collective-permute-start(bf16[8,3456]{1,0:T(8,128)(2,1)S(1)} %get-tuple-element.34), channel_id=1, source_target_pairs={{0,5},{1,4},{2,7},{3,6},{4,1},{5,0},{6,3},{7,2},{8,13},{9,12},{10,... | collective-permute-start | bytes 165896 | tf_op jit(solution)/shard_map/ppermute | solution.py:390
  50.7 5.3 %collective-permute-start.14 = (bf16[8,3456]{1,0:T(8,128)(2,1)S(1)}, bf16[8,3456]{1,0:T(8,128)(2,1)S(1)}, u32[]{:S(2)}, u32[]{:S(2)}) collective-permute-start(bf16[8,3456]{1,0:T(8,128)(2,1)S(1)} %get-tuple-element.35), channel_id=1, source_target_pairs={{0,6},{1,7},{2,4},{3,5},{4,2},{5,3},{6,0},{7,1},{8,14},{9,15},{10,... | collective-permute-start | bytes 165896 | tf_op jit(solution)/shard_map/ppermute | solution.py:390
  53.6 4.5 %collective-permute-start.15 = (bf16[8,3456]{1,0:T(8,128)(2,1)S(1)}, bf16[8,3456]{1,0:T(8,128)(2,1)S(1)}, u32[]{:S(2)}, u32[]{:S(2)}) collective-permute-start(bf16[8,3456]{1,0:T(8,128)(2,1)S(1)} %get-tuple-element.36), channel_id=1, source_target_pairs={{0,7},{1,6},{2,5},{3,4},{4,3},{5,2},{6,1},{7,0},{8,15},{9,14},{10,... | collective-permute-start | bytes 165896 | tf_op jit(solution)/shard_map/ppermute | solution.py:390
  53.6 4.5 %collective-permute-start.9 = (bf16[8,3456]{1,0:T(8,128)(2,1)S(1)}, bf16[8,3456]{1,0:T(8,128)(2,1)S(1)}, u32[]{:S(2)}, u32[]{:S(2)}) collective-permute-start(bf16[8,3456]{1,0:T(8,128)(2,1)S(1)} %get-tuple-element.30), channel_id=1, source_target_pairs={{0,1},{1,0},{2,3},{3,2},{4,5},{5,4},{6,7},{7,6},{8,9},{9,8},{10,11... | collective-permute-start | bytes 165896 | tf_op jit(solution)/shard_map/ppermute | solution.py:390

commit v3 on v2

--- a/solution.py
+++ b/solution.py
@@ -12,6 +12,7 @@
 
 LANES = 128
 HALF = 64
+ROWS = 16
 f32 = jnp.float32
 bf16 = jnp.bfloat16
 
@@ -40,7 +41,10 @@
         base[:, at : at + n] = modes[:, None] + modes[None, :]
         outer[:, at : at + HALF] = modes[half * (n // 2) : (half + 1) * (n // 2), None]
     pad = np.zeros((n, 2 * LANES - 4 * n), jnp.bfloat16)
-    return np.concatenate([lane_side, np.concatenate([row_side, pad], axis=1)]), np.concatenate([base, outer])
+    sines = np.concatenate([lane_side, np.concatenate([row_side, pad], axis=1)]).astype(np.float32)
+    modes = np.concatenate([base, outer])
+    modes = np.pad(modes, ((0, len(sines) - len(modes)), (0, 0)))
+    return np.concatenate([sines, modes], axis=1)
 
 
 def split(x):
@@ -69,10 +73,10 @@
     cells_tile = half * n // LANES
     wide = n + 2 * half
     chunk = 6 if half % 6 == 0 else 2
-    mine, theirs, own = refs[:3]
-    others = refs[3 : 3 + orbs]
-    sines, modes = refs[3 + orbs : 5 + orbs]
-    rest = list(refs[5 + orbs :])
+    mine, own = refs[:2]
+    others = refs[2 : 2 + orbs]
+    table = refs[2 + orbs]
+    rest = list(refs[3 + orbs :])
     total_in = None if first else rest.pop(0)
     if last:
         outs = [rest.pop(0) for _ in range(max(pieces, 1))]
@@ -80,7 +84,17 @@
         flat = rest.pop(0) if pieces else None
     else:
         total = rest.pop(0)
-    dense_i, dense_j, held_i, held_j, moved, field, other = rest
+    dense_i, dense_j, held_i, held_j, moved, field, other, theirs = rest
+    lists = others[-1][:, n * n * n // ROWS :].astype(f32).astype(jnp.int32)
+    for k in range(mine.shape[1]):
+        theirs[0, k] = lists[0, k]
+
+    def fetch(dense, q):
+        if q < orbs - 1:
+            dense[...] = others[q][...]
+        else:
+            for r in range(n // ROWS):
+                dense[r * ROWS : (r + 1) * ROWS, :] = others[q][:, r * n * n : (r + 1) * n * n]
 
     lane = lax.broadcasted_iota(jnp.int32, (n, LANES), 1)
     row = lax.broadcasted_iota(jnp.int32, (n, LANES), 0)
@@ -173,7 +187,7 @@
                 for q in range(orbs):
                     @pl.when(j_at == q)
                     def _():
-                        dense_j[...] = others[q][...]
+                        fetch(dense_j, q)
 
             @pl.when(which == 1)
             def _():
@@ -181,7 +195,7 @@
                 for q in range(orbs):
                     @pl.when(i_at == q)
                     def _():
-                        dense_i[...] = others[q][...]
+                        fetch(dense_i, q)
 
             def put_i(yo, tile):
                 held_i[yo * n : (yo + 1) * n, :] = tile
@@ -196,8 +210,9 @@
                 moved[yo * n : (yo + 1) * n, :] = tile
 
             shifted(gap, use_moved)
-            lane_side = sines[: 2 * LANES, :]
-            row_side = sines[2 * LANES :, : 4 * n]
+            lane_side = table[: 2 * LANES, : 2 * LANES].astype(bf16)
+            row_side = table[2 * LANES :, : 4 * n].astype(bf16)
+            modes = table.at[:, 2 * LANES :]
             rows = chunk * n
             for c in range(half // chunk):
                 here = slice(c * rows, (c + 1) * rows)
@@ -274,15 +289,38 @@
                 outs[k][:, tail_at : tail_at + LANES] = jnp.concatenate(tail, axis=0).astype(bf16)
 
 
-def pair_step(step, pieces, first, last, mine, theirs, own, others, tables, total):
+def pack_kernel(groups, offsets, pick, pair_local, pair_source, pair_count, orbitals, *outs):
+    *plain, box, mine = outs
+    orbs, n, plane = orbitals.shape
+    group = lax.axis_index("grp").astype(jnp.int32)
+    member = lax.axis_index("dev").astype(jnp.int32)
+    slots = pair_local.shape[2]
+    numbers = [offsets[a, k] for a in range(orbs) for k in range(3)]
+    numbers += [pair_local[0, 0, p] for p in range(slots)]
+    numbers += [pair_source[0, 0, p] for p in range(slots)]
+    numbers += [pair_count[0, 0, 0], group, member]
+    numbers += [pick[0, g, member] for g in range(groups)]
+    lane = lax.broadcasted_iota(jnp.int32, (ROWS, LANES), 1)
+    row = jnp.zeros((ROWS, LANES), jnp.int32)
+    for k, number in enumerate(numbers):
+        mine[0, k] = number
+        row = jnp.where(lane == k, number, row)
+    for q in range(orbs - 1):
+        plain[q][...] = orbitals[q]
+    for r in range(n // ROWS):
+        box[:, r * plane : (r + 1) * plane] = orbitals[orbs - 1, r * ROWS : (r + 1) * ROWS, :]
+    box[:, n * plane // ROWS :] = row.astype(f32).astype(bf16)
+
+
+def pair_step(step, pieces, first, last, mine, own, others, table, total):
     orbs, n, plane = own.shape
     half = n // 2
     slots = pieces[1]
     pieces = pieces[0] if last else 0
     vmem = pl.BlockSpec(memory_space=pltpu.VMEM)
     smem = pl.BlockSpec(memory_space=pltpu.SMEM)
-    operands = [mine, theirs, own, *others, *tables]
-    specs = [smem, smem] + [vmem] * (1 + orbs + len(tables))
+    operands = [mine, own, *others, table]
+    specs = [smem] + [vmem] * (2 + orbs)
     if not first:
         operands.append(total)
         specs.append(vmem)
@@ -296,6 +334,7 @@
         pltpu.VMEM((rows, LANES), f32),
         pltpu.VMEM((rows, LANES), f32),
         pltpu.VMEM((rows, LANES), f32),
+        pltpu.SMEM(mine.shape, jnp.int32),
     ]
     shapes = held
     if last:
@@ -345,41 +384,40 @@
     orbs, n, plane = orbitals.shape
     groups = lax.axis_size("grp")
     devices = lax.axis_size("dev")
-    me = lax.axis_index("grp").astype(jnp.int32)
     member = lax.axis_index("dev").astype(jnp.int32)
-    my_pick = lax.dynamic_slice_in_dim(pick[0], member, 1, 0)[0]
-    mine = jnp.concatenate(
-        [
-            offsets.reshape(-1),
-            pair_local[0, 0],
-            pair_source[0, 0],
-            pair_count[0, 0],
-            me.reshape(1),
-            member.reshape(1),
-            my_pick,
-        ]
-    ).astype(jnp.int32)[None, :]
+    slots = pair_local.shape[2]
+    vmem = pl.BlockSpec(memory_space=pltpu.VMEM)
+    smem = pl.BlockSpec(memory_space=pltpu.SMEM)
+    table = jnp.asarray(np_tables(n))
+    numbers = 3 * orbs + 2 * slots + 3 + groups
+    *held, mine = pl.pallas_call(
+        functools.partial(pack_kernel, groups),
+        out_shape=[jax.ShapeDtypeStruct((n, plane), bf16)] * (orbs - 1)
+        + [
+            jax.ShapeDtypeStruct((ROWS, n * plane // ROWS + LANES), bf16),
+            jax.ShapeDtypeStruct((1, numbers), jnp.int32),
+        ],
+        in_specs=[smem] * 4 + [vmem] * 2,
+        out_specs=[vmem] * orbs + [smem],
+        name="pack",
+    )(offsets, pick.transpose(0, 2, 1), pair_local, pair_source, pair_count, orbitals)
     by_pieces = devices & (devices - 1) == 0 and n % devices == 0 and n // devices * orbs == 12
     pieces = devices if by_pieces else 0
     ring = [(g, (g + 1) % groups) for g in range(groups)]
-    held = [orbitals[q] for q in range(orbs)]
-    tables = [jnp.asarray(t) for t in np_tables(n)]
-    theirs = mine
     total = None
     for step in range(1, groups):
         held = [lax.ppermute(h, "grp", ring) for h in held]
-        theirs = lax.ppermute(theirs, "grp", ring)
-        held[0], theirs, total = lax.optimization_barrier((held[0], theirs, total))
+        for q in range(orbs):
+            held[q], _ = lax.optimization_barrier((held[q], total))
         total = pair_step(
             step,
-            (pieces, pair_local.shape[2]),
+            (pieces, slots),
             step == 1,
             step == groups - 1,
             mine,
-            theirs,
             orbitals,
             held,
-            tables,
+            table,
             total,
         )
     if not pieces:
@@ -388,11 +426,10 @@
     arrived = [total[0]]
     for k in range(1, devices):
         arrived.append(lax.ppermute(total[k], "dev", [(d, d ^ k) for d in range(devices)]))
-    vmem = pl.BlockSpec(memory_space=pltpu.VMEM)
     return pl.pallas_call(
         functools.partial(gather_kernel, n, orbs),
         out_shape=jax.ShapeDtypeStruct((orbs * devices, n * plane // devices), f32),
-        in_specs=[pl.BlockSpec(memory_space=pltpu.SMEM)] + [vmem] * devices,
+        in_specs=[smem] + [vmem] * devices,
         out_specs=vmem,
         scratch_shapes=[pltpu.VMEM((orbs * n * plane // LANES, LANES), f32)] * 2,
         compiler_params=pltpu.CompilerParams(vmem_limit_bytes=32 << 20),

time: 58.5 us -> 55.4 us (0.947); the launches traced: 59.4 us -> 54.9 us
  waiting for transfers between devices: 23.9 us -> 21.2 us
  Pallas kernels: 11.5 us -> 13.3 us
  local copies, waits for them, and re-layouts: 4.51 us -> 2.72 us
  starting transfers between devices: 18.8 us -> 17.1 us
    ppermute x3 -> x0, waiting for transfers between devices: 20.2 us -> none  [body(): theirs = lax.ppermute(theirs, 'grp', ring)]
    ppermute x6, waiting for transfers between devices: 0.02 us -> 18.1 us  [body(): held = [lax.ppermute(h, 'grp', ring) for h in held]]
    ppermute x3 -> x0, starting transfers between devices: 3.84 us -> none  [body(): theirs = lax.ppermute(theirs, 'grp', ring)]
    pallas_call x0 -> x1, Pallas kernels: none -> 1.82 us  [body(): pl.pallas_call(functools.partial(pack_kernel, groups), out_shape=[jax.Sha...]
    ppermute x6, starting transfers between devices: 6 us -> 7.68 us  [body(): held = [lax.ppermute(h, 'grp', ring) for h in held]]
    squeeze x1 -> x0, local copies, waits for them, and re-layouts: 1.13 us -> none  [body(): held = [orbitals[q] for q in range(orbs)]]
    unnamed x8 -> x6, local copies, waits for them, and re-layouts: 1.69 us -> 2.72 us
    reshape x1 -> x0, local copies, waits for them, and re-layouts: 0.76 us -> none  [body(): offsets.reshape(-1)]
  transfers between devices with their start and end apart: 16 -> 13, of which waited for: 5 -> 8; matrix products, arithmetic and copies ran while one was open for 3% -> 0% of each run, Pallas kernels for 11% -> 16%
where the time goes in v3:
time: 55.4 us; the launch traced here: 54.9 us
  waiting for transfers between devices  21.2 us (38%)
  starting transfers between devices  17.1 us (31%)
  Pallas kernels  13.3 us (24%)
  local copies, waits for them, and re-layouts  2.72 us (5%)
  between operations  0.72 us (1%)
    ppermute x6, waiting for transfers between devices, body(): held = [lax.ppermute(h, 'grp', ring) for h in held]  18.1 us
    pallas_call x3, Pallas kernels, pair_step(): pl.pallas_call(functools.partial(pair_kernel, (n, orbs, slots), pieces, f...  10.2 us
    ppermute x7, starting transfers between devices, body(): lax.ppermute(total[k], 'dev', [(d, d ^ k) for d in range(devices)])  9.39 us
    ppermute x6, starting transfers between devices, body(): held = [lax.ppermute(h, 'grp', ring) for h in held]  7.68 us
    ppermute x7, waiting for transfers between devices, body(): lax.ppermute(total[k], 'dev', [(d, d ^ k) for d in range(devices)])  3.06 us
    unnamed x6, local copies, waits for them, and re-layouts  2.72 us
    pallas_call x1, Pallas kernels, body(): pl.pallas_call(functools.partial(pack_kernel, groups), out_shape=[jax.Sha...  1.82 us
    pallas_call x1, Pallas kernels, body(): pl.pallas_call(functools.partial(gather_kernel, n, orbs), out_shape=jax.S...  1.3 us
  transfers between devices with their start and end apart: 13, of which 8 were waited for; matrix products, arithmetic and copies ran while one was open for 0% of the time, Pallas kernels for 16%

profile of v3, /device:TPU:0, one launch (start us, length us, event | category | flops | bytes accessed | tf_op | source)
XLA Modules:
  0.0 54.9 jit_solution(7824825229656716853)
XLA Ops:
  0.7 1.8 %pack.1 = (bf16[48,2304]{1,0:T(8,128)(2,1)}, bf16[16,7040]{1,0:T(8,128)(2,1)}, s32[1,17]{1,0:T(1,128)}) custom-call(s32[2,3]{1,0:T(2,128)} %offsets.1, s32[1,4,8]{2,1,0:T(4,128)} %bitcast.2, s32[1,1,2]{2,1,0:T(1,128)} %pair_local.1, s32[1,1,2]{2,1,0:T(1,128)} %pair_source.1, s32[1,1,1]{2,1,0:T(1,128)S(6)} %copy.8.pair_count, bf16[2,48,2304]{2,1,0:T(8,128)(2,1)} %refs_1_.5), custom_call_target="tpu_custom_call" | custom-call | tf_op jit(solution)/shard_map/pack/pallas_call | solution.py:393
  2.5 3.1 %collective-permute-start.2 = (bf16[16,7040]{1,0:T(8,128)(2,1)}, bf16[16,7040]{1,0:T(8,128)(2,1)S(1)}, u32[]{:S(2)}, u32[]{:S(2)}) collective-permute-start(bf16[16,7040]{1,0:T(8,128)(2,1)} %get-tuple-element.22), channel_id=1, source_target_pairs={{0,8},{8,16},{16,24},{24,0},{1,9},{9,17},{17,25},{25,1},{2,10},{10... | collective-permute-start | bytes 675848 | tf_op jit(solution)/shard_map/ppermute | solution.py:409
  5.6 1.6 %collective-permute-start = (bf16[48,2304]{1,0:T(8,128)(2,1)}, bf16[48,2304]{1,0:T(8,128)(2,1)S(1)}, u32[]{:S(2)}, u32[]{:S(2)}) collective-permute-start(bf16[48,2304]{1,0:T(8,128)(2,1)} %get-tuple-element.21), channel_id=1, source_target_pairs={{0,8},{8,16},{16,24},{24,0},{1,9},{9,17},{17,25},{25,1},{2,10},{10... | collective-permute-start | bytes 663560 | tf_op jit(solution)/shard_map/ppermute | solution.py:409
  7.1 7.0 %collective-permute-done.2.refs_3_ = bf16[16,7040]{1,0:T(8,128)(2,1)S(1)} collective-permute-done((bf16[16,7040]{1,0:T(8,128)(2,1)}, bf16[16,7040]{1,0:T(8,128)(2,1)S(1)}, u32[]{:S(2)}, u32[]{:S(2)}) %collective-permute-start.2) | collective-permute-done | bytes 225312 | tf_op jit(solution)/shard_map/ppermute | solution.py:409
  14.1 0.0 collective-permute-start.4
  14.2 4.7 %collective-permute-done.refs_2_ = bf16[48,2304]{1,0:T(8,128)(2,1)S(1)} collective-permute-done((bf16[48,2304]{1,0:T(8,128)(2,1)}, bf16[48,2304]{1,0:T(8,128)(2,1)S(1)}, u32[]{:S(2)}, u32[]{:S(2)}) %collective-permute-start) | collective-permute-done | bytes 221216 | tf_op jit(solution)/shard_map/ppermute | solution.py:409
  18.9 0.0 collective-permute-start.1
  18.9 1.0 %copy-done = bf16[2,48,2304]{2,1,0:T(8,128)(2,1)S(1)} copy-done((bf16[2,48,2304]{2,1,0:T(8,128)(2,1)S(1)}, bf16[2,48,2304]{2,1,0:T(8,128)(2,1)}, u32[]{:S(2)}) %copy-start) | copy-done | bytes 442392
  19.9 1.0 %copy-done.1 = f32[304,384]{1,0:T(8,128)S(1)} copy-done((f32[304,384]{1,0:T(8,128)S(1)}, f32[304,384]{1,0:T(8,128)}, u32[]{:S(2)}) %copy-start.1) | copy-done | bytes 466968
  20.9 0.7 %copy-done.2 = s32[1,17]{1,0:T(1,128)S(1)} copy-done((s32[1,17]{1,0:T(1,128)S(1)}, s32[1,17]{1,0:T(1,128)}, u32[]{:S(2)}) %copy-start.2) | copy-done | bytes 92
  21.6 5.7 %pairs_1.1.refs_5_ = f32[2304,128]{1,0:T(8,128)S(1)} custom-call(s32[1,17]{1,0:T(1,128)S(1)} %copy-done.2, bf16[2,48,2304]{2,1,0:T(8,128)(2,1)S(1)} %copy-done, bf16[48,2304]{1,0:T(8,128)(2,1)S(1)} %collective-permute-done.refs_2_, bf16[16,7040]{1,0:T(8,128)(2,1)S(1)} %collective-permute-done.2.refs_3_, f32[304,384]{1,0:T(8,128)S(1)} %copy-done.1), custom_call_target="tpu_custom_call" | custom-call | flops 382205952 | bytes 1769472 | tf_op jit(solution)/shard_map/pairs_1/pallas_call | solution.py:346
  27.3 0.0 collective-permute-done.4.refs_3_
  27.3 0.1 collective-permute-start.5
  27.4 0.2 collective-permute-done.1.refs_2_
  27.6 2.9 %collective-permute-start.3 = (bf16[48,2304]{1,0:T(8,128)(2,1)S(1)}, bf16[48,2304]{1,0:T(8,128)(2,1)S(1)}, u32[]{:S(2)}, u32[]{:S(2)}) collective-permute-start(bf16[48,2304]{1,0:T(8,128)(2,1)S(1)} %collective-permute-done.1.refs_2_), channel_id=1, source_target_pairs={{0,8},{8,16},{16,24},{24,0},{1,9},{9,17},{17,25},{25,1},{2,10},{10... | collective-permute-start | bytes 663560 | tf_op jit(solution)/shard_map/ppermute | solution.py:409
  30.5 3.1 %pairs_2.1.refs_5_ = f32[2304,128]{1,0:T(8,128)S(1)} custom-call(s32[1,17]{1,0:T(1,128)S(1)} %copy-done.2, bf16[2,48,2304]{2,1,0:T(8,128)(2,1)S(1)} %copy-done, bf16[48,2304]{1,0:T(8,128)(2,1)S(1)} %collective-permute-done.1.refs_2_, bf16[16,7040]{1,0:T(8,128)(2,1)S(1)} %collective-permute-done.4.refs_3_, f32[304,384]{1,0:T(8,128)S(1)} %copy-done.1, ...), custom_call_target="tpu_custom_call" | custom-call | flops 382205952 | bytes 1769472 | tf_op jit(solution)/shard_map/pairs_2/pallas_call | solution.py:346
  33.6 6.1 %collective-permute-done.3.refs_2_ = bf16[48,2304]{1,0:T(8,128)(2,1)S(1)} collective-permute-done((bf16[48,2304]{1,0:T(8,128)(2,1)S(1)}, bf16[48,2304]{1,0:T(8,128)(2,1)S(1)}, u32[]{:S(2)}, u32[]{:S(2)}) %collective-permute-start.3) | collective-permute-done | bytes 221216 | tf_op jit(solution)/shard_map/ppermute | solution.py:409
  39.8 0.0 collective-permute-done.5.refs_3_
  39.8 1.4 %pairs_3.1 = (bf16[8,3456]{1,0:T(8,128)(2,1)S(1)}, bf16[8,3456]{1,0:T(8,128)(2,1)S(1)}, bf16[8,3456]{1,0:T(8,128)(2,1)S(1)}, bf16[8,3456]{1,0:T(8,128)(2,1)S(1)}...) custom-call(s32[1,17]{1,0:T(1,128)S(1)} %copy-done.2, ...), custom_call_target="tpu_custom_call" | custom-call | flops 382205952 | bytes 1769472 | tf_op jit(solution)/shard_map/pairs_3/pallas_call | solution.py:346
  41.2 0.1 collective-permute-start.10
  41.3 5.2 %collective-permute-start.11 = (bf16[8,3456]{1,0:T(8,128)(2,1)S(1)}, bf16[8,3456]{1,0:T(8,128)(2,1)S(1)}, u32[]{:S(2)}, u32[]{:S(2)}) collective-permute-start(bf16[8,3456]{1,0:T(8,128)(2,1)S(1)} %get-tuple-element.33), channel_id=1, source_target_pairs={{0,6},{1,7},{2,4},{3,5},{4,2},{5,3},{6,0},{7,1},{8,14},{9,15},{10,... | collective-permute-start | bytes 165896 | tf_op jit(solution)/shard_map/ppermute | solution.py:428
  46.5 0.7 %collective-permute-start.12 = (bf16[8,3456]{1,0:T(8,128)(2,1)S(1)}, bf16[8,3456]{1,0:T(8,128)(2,1)S(1)}, u32[]{:S(2)}, u32[]{:S(2)}) collective-permute-start(bf16[8,3456]{1,0:T(8,128)(2,1)S(1)} %get-tuple-element.34), channel_id=1, source_target_pairs={{0,7},{1,6},{2,5},{3,4},{4,3},{5,2},{6,1},{7,0},{8,15},{9,14},{10,... | collective-permute-start | bytes 165896 | tf_op jit(solution)/shard_map/ppermute | solution.py:428
  47.2 0.0 collective-permute-start.6
  47.2 2.1 %collective-permute-start.7 = (bf16[8,3456]{1,0:T(8,128)(2,1)S(1)}, bf16[8,3456]{1,0:T(8,128)(2,1)S(1)}, u32[]{:S(2)}, u32[]{:S(2)}) collective-permute-start(bf16[8,3456]{1,0:T(8,128)(2,1)S(1)} %get-tuple-element.29), channel_id=1, source_target_pairs={{0,2},{1,3},{2,0},{3,1},{4,6},{5,7},{6,4},{7,5},{8,10},{9,11},{10,... | collective-permute-start | bytes 165896 | tf_op jit(solution)/shard_map/ppermute | solution.py:428
  49.3 0.1 collective-permute-start.8
  49.5 0.0 collective-permute-done.11.refs_6_
  49.5 1.1 %collective-permute-start.9 = (bf16[8,3456]{1,0:T(8,128)(2,1)S(1)}, bf16[8,3456]{1,0:T(8,128)(2,1)S(1)}, u32[]{:S(2)}, u32[]{:S(2)}) collective-permute-start(bf16[8,3456]{1,0:T(8,128)(2,1)S(1)} %get-tuple-element.31), channel_id=1, source_target_pairs={{0,4},{1,5},{2,6},{3,7},{4,0},{5,1},{6,2},{7,3},{8,12},{9,13},{10,... | collective-permute-start | bytes 165896 | tf_op jit(solution)/shard_map/ppermute | solution.py:428
  50.6 0.4 collective-permute-done.12.refs_7_
  51.0 1.6 %collective-permute-done.7.refs_2_ = bf16[8,3456]{1,0:T(8,128)(2,1)S(1)} collective-permute-done((bf16[8,3456]{1,0:T(8,128)(2,1)S(1)}, bf16[8,3456]{1,0:T(8,128)(2,1)S(1)}, u32[]{:S(2)}, u32[]{:S(2)}) %collective-permute-start.7) | collective-permute-done | bytes 55328 | tf_op jit(solution)/shard_map/ppermute | solution.py:428
  52.6 0.8 %collective-permute-done.8.refs_3_ = bf16[8,3456]{1,0:T(8,128)(2,1)S(1)} collective-permute-done((bf16[8,3456]{1,0:T(8,128)(2,1)S(1)}, bf16[8,3456]{1,0:T(8,128)(2,1)S(1)}, u32[]{:S(2)}, u32[]{:S(2)}) %collective-permute-start.8) | collective-permute-done | bytes 55328 | tf_op jit(solution)/shard_map/ppermute | solution.py:428
  53.4 0.3 collective-permute-done.9.refs_4_
  53.6 1.3 %cells.1 = f32[16,13824]{1,0:T(8,128)} custom-call(s32[1]{0:T(128)} %bitcast.member_ref, bf16[8,3456]{1,0:T(8,128)(2,1)S(1)} %get-tuple-element.27.refs_0_, bf16[8,3456]{1,0:T(8,128)(2,1)S(1)} %collective-permute-done.6.refs_1_, bf16[8,3456]{1,0:T(8,128)(2,1)S(1)} %collective-permute-done.7.refs_2_, bf16[8,3456]{1,0:T(8,128)(2,1)S(1)} %collective-permute-done.8.refs_3_, ...), custom_call_target="tpu_custom_call" | custom-call | tf_op jit(solution)/shard_map/cells/pallas_call | solution.py:429
  (5 shorter events, 0.0 us)
Async XLA Ops:
  2.5 11.7 %collective-permute-start.2 = (bf16[16,7040]{1,0:T(8,128)(2,1)}, bf16[16,7040]{1,0:T(8,128)(2,1)S(1)}, u32[]{:S(2)}, u32[]{:S(2)}) collective-permute-start(bf16[16,7040]{1,0:T(8,128)(2,1)} %get-tuple-element.22), channel_id=1, source_target_pairs={{0,8},{8,16},{16,24},{24,0},{1,9},{9,17},{17,25},{25,1},{2,10},{10... | collective-permute-start | bytes 675848 | tf_op jit(solution)/shard_map/ppermute | solution.py:409
  5.6 13.3 %collective-permute-start = (bf16[48,2304]{1,0:T(8,128)(2,1)}, bf16[48,2304]{1,0:T(8,128)(2,1)S(1)}, u32[]{:S(2)}, u32[]{:S(2)}) collective-permute-start(bf16[48,2304]{1,0:T(8,128)(2,1)} %get-tuple-element.21), channel_id=1, source_target_pairs={{0,8},{8,16},{16,24},{24,0},{1,9},{9,17},{17,25},{25,1},{2,10},{10... | collective-permute-start | bytes 663560 | tf_op jit(solution)/shard_map/ppermute | solution.py:409
  14.1 13.2 %collective-permute-start.4 = (bf16[16,7040]{1,0:T(8,128)(2,1)S(1)}, bf16[16,7040]{1,0:T(8,128)(2,1)S(1)}, u32[]{:S(2)}, u32[]{:S(2)}) collective-permute-start(bf16[16,7040]{1,0:T(8,128)(2,1)S(1)} %collective-permute-done.2.refs_3_), channel_id=1, source_target_pairs={{0,8},{8,16},{16,24},{24,0},{1,9},{9,17},{17,25},{25,1},{2,10},{10... | collective-permute-start | bytes 675848 | tf_op jit(solution)/shard_map/ppermute | solution.py:409
  18.9 8.7 %collective-permute-start.1 = (bf16[48,2304]{1,0:T(8,128)(2,1)S(1)}, bf16[48,2304]{1,0:T(8,128)(2,1)S(1)}, u32[]{:S(2)}, u32[]{:S(2)}) collective-permute-start(bf16[48,2304]{1,0:T(8,128)(2,1)S(1)} %collective-permute-done.refs_2_), channel_id=1, source_target_pairs={{0,8},{8,16},{16,24},{24,0},{1,9},{9,17},{17,25},{25,1},{2,10},{10... | collective-permute-start | bytes 663560 | tf_op jit(solution)/shard_map/ppermute | solution.py:409
  18.9 1.0 %copy-start = (bf16[2,48,2304]{2,1,0:T(8,128)(2,1)S(1)}, bf16[2,48,2304]{2,1,0:T(8,128)(2,1)}, u32[]{:S(2)}) copy-start(bf16[2,48,2304]{2,1,0:T(8,128)(2,1)} %refs_1_.5) | copy-start | bytes 1327108
  19.9 1.0 %copy-start.1 = (f32[304,384]{1,0:T(8,128)S(1)}, f32[304,384]{1,0:T(8,128)}, u32[]{:S(2)}) copy-start(f32[304,384]{1,0:T(8,128)} %constant.6.clone.refs_4_) | copy-start | bytes 1400836
  20.9 0.7 %copy-start.2 = (s32[1,17]{1,0:T(1,128)S(1)}, s32[1,17]{1,0:T(1,128)}, u32[]{:S(2)}) copy-start(s32[1,17]{1,0:T(1,128)} %get-tuple-element.20.refs_0_) | copy-start | bytes 208
  27.3 12.4 %collective-permute-start.5 = (bf16[16,7040]{1,0:T(8,128)(2,1)S(1)}, bf16[16,7040]{1,0:T(8,128)(2,1)S(1)}, u32[]{:S(2)}, u32[]{:S(2)}) collective-permute-start(bf16[16,7040]{1,0:T(8,128)(2,1)S(1)} %collective-permute-done.4.refs_3_), channel_id=1, source_target_pairs={{0,8},{8,16},{16,24},{24,0},{1,9},{9,17},{17,25},{25,1},{2,10},{10... | collective-permute-start | bytes 675848 | tf_op jit(solution)/shard_map/ppermute | solution.py:409
  27.6 12.1 %collective-permute-start.3 = (bf16[48,2304]{1,0:T(8,128)(2,1)S(1)}, bf16[48,2304]{1,0:T(8,128)(2,1)S(1)}, u32[]{:S(2)}, u32[]{:S(2)}) collective-permute-start(bf16[48,2304]{1,0:T(8,128)(2,1)S(1)} %collective-permute-done.1.refs_2_), channel_id=1, source_target_pairs={{0,8},{8,16},{16,24},{24,0},{1,9},{9,17},{17,25},{25,1},{2,10},{10... | collective-permute-start | bytes 663560 | tf_op jit(solution)/shard_map/ppermute | solution.py:409
  41.2 8.2 %collective-permute-start.10 = (bf16[8,3456]{1,0:T(8,128)(2,1)S(1)}, bf16[8,3456]{1,0:T(8,128)(2,1)S(1)}, u32[]{:S(2)}, u32[]{:S(2)}) collective-permute-start(bf16[8,3456]{1,0:T(8,128)(2,1)S(1)} %get-tuple-element.32), channel_id=1, source_target_pairs={{0,5},{1,4},{2,7},{3,6},{4,1},{5,0},{6,3},{7,2},{8,13},{9,12},{10,... | collective-permute-start | bytes 165896 | tf_op jit(solution)/shard_map/ppermute | solution.py:428
  41.3 8.2 %collective-permute-start.11 = (bf16[8,3456]{1,0:T(8,128)(2,1)S(1)}, bf16[8,3456]{1,0:T(8,128)(2,1)S(1)}, u32[]{:S(2)}, u32[]{:S(2)}) collective-permute-start(bf16[8,3456]{1,0:T(8,128)(2,1)S(1)} %get-tuple-element.33), channel_id=1, source_target_pairs={{0,6},{1,7},{2,4},{3,5},{4,2},{5,3},{6,0},{7,1},{8,14},{9,15},{10,... | collective-permute-start | bytes 165896 | tf_op jit(solution)/shard_map/ppermute | solution.py:428
  46.5 4.5 %collective-permute-start.12 = (bf16[8,3456]{1,0:T(8,128)(2,1)S(1)}, bf16[8,3456]{1,0:T(8,128)(2,1)S(1)}, u32[]{:S(2)}, u32[]{:S(2)}) collective-permute-start(bf16[8,3456]{1,0:T(8,128)(2,1)S(1)} %get-tuple-element.34), channel_id=1, source_target_pairs={{0,7},{1,6},{2,5},{3,4},{4,3},{5,2},{6,1},{7,0},{8,15},{9,14},{10,... | collective-permute-start | bytes 165896 | tf_op jit(solution)/shard_map/ppermute | solution.py:428
  47.2 3.8 %collective-permute-start.6 = (bf16[8,3456]{1,0:T(8,128)(2,1)S(1)}, bf16[8,3456]{1,0:T(8,128)(2,1)S(1)}, u32[]{:S(2)}, u32[]{:S(2)}) collective-permute-start(bf16[8,3456]{1,0:T(8,128)(2,1)S(1)} %get-tuple-element.28), channel_id=1, source_target_pairs={{0,1},{1,0},{2,3},{3,2},{4,5},{5,4},{6,7},{7,6},{8,9},{9,8},{10,11... | collective-permute-start | bytes 165896 | tf_op jit(solution)/shard_map/ppermute | solution.py:428
  47.2 5.3 %collective-permute-start.7 = (bf16[8,3456]{1,0:T(8,128)(2,1)S(1)}, bf16[8,3456]{1,0:T(8,128)(2,1)S(1)}, u32[]{:S(2)}, u32[]{:S(2)}) collective-permute-start(bf16[8,3456]{1,0:T(8,128)(2,1)S(1)} %get-tuple-element.29), channel_id=1, source_target_pairs={{0,2},{1,3},{2,0},{3,1},{4,6},{5,7},{6,4},{7,5},{8,10},{9,11},{10,... | collective-permute-start | bytes 165896 | tf_op jit(solution)/shard_map/ppermute | solution.py:428
  49.3 4.0 %collective-permute-start.8 = (bf16[8,3456]{1,0:T(8,128)(2,1)S(1)}, bf16[8,3456]{1,0:T(8,128)(2,1)S(1)}, u32[]{:S(2)}, u32[]{:S(2)}) collective-permute-start(bf16[8,3456]{1,0:T(8,128)(2,1)S(1)} %get-tuple-element.30), channel_id=1, source_target_pairs={{0,3},{1,2},{2,1},{3,0},{4,7},{5,6},{6,5},{7,4},{8,11},{9,10},{10,... | collective-permute-start | bytes 165896 | tf_op jit(solution)/shard_map/ppermute | solution.py:428
  49.5 4.2 %collective-permute-start.9 = (bf16[8,3456]{1,0:T(8,128)(2,1)S(1)}, bf16[8,3456]{1,0:T(8,128)(2,1)S(1)}, u32[]{:S(2)}, u32[]{:S(2)}) collective-permute-start(bf16[8,3456]{1,0:T(8,128)(2,1)S(1)} %get-tuple-element.31), channel_id=1, source_target_pairs={{0,4},{1,5},{2,6},{3,7},{4,0},{5,1},{6,2},{7,3},{8,12},{9,13},{10,... | collective-permute-start | bytes 165896 | tf_op jit(solution)/shard_map/ppermute | solution.py:428

commit v4 on v3

--- a/solution.py
+++ b/solution.py
@@ -32,7 +32,7 @@
         return out
 
     lane_side = np.block([[two(high), two(low)], [two(high), two(low)]])
-    row_side = np.concatenate([high, high, low, low], axis=1)
+    row_side = np.concatenate([high, high, low, 0 * low], axis=1)
     modes = (2.0 - 2.0 * np.cos(step * (freq + 1.0))).astype(np.float32)
     base = np.ones((n, LANES), np.float32)
     outer = np.ones((n // 2, LANES), np.float32)
@@ -62,34 +62,66 @@
     columns = []
     for tile in tiles:
         high, low = split(tile)
-        columns.append(jnp.concatenate([high, low, high, low], axis=0))
+        columns.append(jnp.concatenate([high, low, high], axis=0))
     out = jnp.dot(row_side, jnp.concatenate(columns, axis=1), preferred_element_type=f32)
     return out[:, :LANES], out[:, LANES:]
 
 
-def pair_kernel(sizes, pieces, first, last, *refs):
+def unpack(dense, put):
+    n = dense.shape[0]
+    half = n // 2
+    lane = lax.broadcasted_iota(jnp.int32, (n, LANES), 1)
+    for yo in range(half):
+        start = yo * n % LANES
+        halves = []
+        for h in range(2):
+            t = (yo * n // LANES + h * (half * n // LANES)) * LANES
+            piece = dense[:, t : t + LANES].astype(f32)
+            if start + n > LANES:
+                after = dense[:, t + LANES : t + 2 * LANES].astype(f32)
+                piece = jnp.where(lane >= start, piece, after)
+            amount = (h * HALF - start) % LANES
+            halves.append(pltpu.roll(piece, amount, 1) if amount else piece)
+        put(yo, jnp.where(lane < HALF, halves[0], halves[1]))
+
+
+def setup_kernel(own, table, mine, held, sines, modes, total):
+    orbs, n, _ = own.shape
+    half = n // 2
+    wide = n + 2 * half
+    for q in range(orbs):
+
+        def put(yo, tile, q=q):
+            at = (q * half + yo) * wide + half
+            held[at : at + n, :] = tile
+
+        unpack(own.at[q], put)
+    sines[...] = table[:, : 2 * LANES].astype(bf16)
+    modes[...] = table[: modes.shape[0], 2 * LANES :]
+    total[...] = jnp.zeros_like(total)
+
+
+def pair_kernel(sizes, pieces, tasks, last, *refs):
     n, orbs, slots = sizes
     half = n // 2
     cells_tile = half * n // LANES
     wide = n + 2 * half
-    chunk = 6 if half % 6 == 0 else 2
-    mine, own = refs[:2]
-    others = refs[2 : 2 + orbs]
-    table = refs[2 + orbs]
-    rest = list(refs[3 + orbs :])
-    total_in = None if first else rest.pop(0)
+    mine, own, sines, modes = refs[:4]
+    others = refs[4 : 4 + orbs]
+    total_in = refs[4 + orbs]
+    rest = list(refs[5 + orbs :])
     if last:
         outs = [rest.pop(0) for _ in range(max(pieces, 1))]
         total = rest.pop(0)
         flat = rest.pop(0) if pieces else None
     else:
         total = rest.pop(0)
-    dense_i, dense_j, held_i, held_j, moved, field, other, theirs = rest
+    dense, held, moved, field, other, theirs = rest
     lists = others[-1][:, n * n * n // ROWS :].astype(f32).astype(jnp.int32)
     for k in range(mine.shape[1]):
         theirs[0, k] = lists[0, k]
 
-    def fetch(dense, q):
+    def fetch(q):
         if q < orbs - 1:
             dense[...] = others[q][...]
         else:
@@ -98,37 +130,19 @@
 
     lane = lax.broadcasted_iota(jnp.int32, (n, LANES), 1)
     row = lax.broadcasted_iota(jnp.int32, (n, LANES), 0)
-    left = lane < HALF
-    left_half = left[:half]
-    if first:
-        total[...] = jnp.zeros_like(total)
-    else:
-        total[...] = total_in[...]
+    left_half = lane[:half] < HALF
+    total[...] = total_in[...]
 
     at_source = 3 * orbs + slots
     at_count = at_source + slots
     at_group = at_count + 1
     at_pick = at_group + 2
-    me = mine[0, at_group]
-    them = theirs[0, at_group]
     member = mine[0, at_group + 1]
 
-    def unpack(dense, put):
-        for yo in range(half):
-            start = yo * n % LANES
-            first_tile = yo * n // LANES
-            halves = []
-            for h in range(2):
-                t = (first_tile + h * cells_tile) * LANES
-                piece = dense[:, t : t + LANES].astype(f32)
-                if start + n > LANES:
-                    after = dense[:, t + LANES : t + 2 * LANES].astype(f32)
-                    piece = jnp.where(lane >= start, piece, after)
-                amount = (h * HALF - start) % LANES
-                halves.append(pltpu.roll(piece, amount, 1) if amount else piece)
-            put(yo, jnp.where(left, halves[0], halves[1]))
-
-    def shifted(gap, use):
+    def tile_at(base, yo):
+        return pl.ds(base + yo * wide + half, n)
+
+    def shifted(ref, base, gap, use):
         gap_x, gap_y, gap_z = gap
         z_at = lax.rem(lane, HALF)
         inside = (
@@ -143,7 +157,7 @@
             under = s < 0
             over = s >= half
             src = s + jnp.where(under, half, 0) - jnp.where(over, half, 0)
-            tile = held_j[pl.ds(src * wide + half + gap_x, n), :]
+            tile = ref[pl.ds(base + src * wide + half + gap_x, n), :]
             amount = (2 * LANES - gap_z + jnp.where(under | over, HALF, 0)) % LANES
             tile = pltpu.roll(tile, amount, 1)
             low_lane = jnp.where(under, HALF, 0)
@@ -158,104 +172,78 @@
         bottom = jnp.where(left_half, pltpu.roll(a, HALF, 1), b)
         return jnp.concatenate([top, bottom], axis=0)
 
-    def task(which, carry):
-        outgoing = which == 0
-
-        def lister(k):
-            return jnp.where(outgoing, mine[0, k], theirs[0, k])
-
-        def source(k):
-            return jnp.where(outgoing, theirs[0, k], mine[0, k])
-
-        lister_group = jnp.where(outgoing, me, them)
-        source_group = jnp.where(outgoing, them, me)
-        listed = lister(at_count)
+    def rows_of(ref, at):
+        return ref[at * n : (at + 1) * n, :]
+
+    def task(outgoing):
+        lister, source = (mine, theirs) if outgoing else (theirs, mine)
+        source_group = source[0, at_group]
+        listed = lister[0, at_count]
         i_at = jnp.int32(0)
         found = jnp.int32(0)
         for p in range(slots):
-            hit = (lister(at_source + p) == source_group) & (p < listed)
-            i_at = jnp.where(hit, lister(3 * orbs + p), i_at)
+            hit = (lister[0, at_source + p] == source_group) & (p < listed)
+            i_at = jnp.where(hit, lister[0, 3 * orbs + p], i_at)
             found = jnp.where(hit, 1, found)
-        j_at = source(at_pick + lister_group)
-        gap = [lister(i_at * 3 + k) - source(j_at * 3 + k) for k in range(3)]
+        j_at = source[0, at_pick + lister[0, at_group]]
+        gap = [lister[0, i_at * 3 + k] - source[0, j_at * 3 + k] for k in range(3)]
+        own_at, other_at = (i_at, j_at) if outgoing else (j_at, i_at)
+        base = own_at * (half * wide)
+        box_i, base_i, box_j, base_j = (own, base, held, 0) if outgoing else (held, 0, own, base)
 
         @pl.when(found == 1)
         def _():
-            @pl.when(which == 0)
-            def _():
-                dense_i[...] = own[i_at]
-                for q in range(orbs):
-                    @pl.when(j_at == q)
-                    def _():
-                        fetch(dense_j, q)
-
-            @pl.when(which == 1)
-            def _():
-                dense_j[...] = own[j_at]
-                for q in range(orbs):
-                    @pl.when(i_at == q)
-                    def _():
-                        fetch(dense_i, q)
-
-            def put_i(yo, tile):
-                held_i[yo * n : (yo + 1) * n, :] = tile
-
-            def put_j(yo, tile):
-                held_j[yo * wide + half : yo * wide + half + n, :] = tile
-
-            unpack(dense_i, put_i)
-            unpack(dense_j, put_j)
+            for q in range(orbs):
+                @pl.when(other_at == q)
+                def _():
+                    fetch(q)
+
+            def put(yo, tile):
+                held[tile_at(0, yo), :] = tile
+
+            unpack(dense, put)
 
             def use_moved(yo, tile):
                 moved[yo * n : (yo + 1) * n, :] = tile
-
-            shifted(gap, use_moved)
-            lane_side = table[: 2 * LANES, : 2 * LANES].astype(bf16)
-            row_side = table[2 * LANES :, : 4 * n].astype(bf16)
-            modes = table.at[:, 2 * LANES :]
-            rows = chunk * n
-            for c in range(half // chunk):
-                here = slice(c * rows, (c + 1) * rows)
-                spectrum = lane_turn(held_i[here, :] * moved[here, :], lane_side)
-                for q in range(0, chunk, 2):
-                    pair = row_turn([spectrum[(q + k) * n : (q + k + 1) * n] for k in range(2)], row_side)
-                    for k in range(2):
-                        at = c * rows + (q + k) * n
-                        field[at : at + n, :] = pair[k]
-            for xo in range(0, half, 2):
-                pair = row_turn([swapped(field, xo + k) for k in range(2)], row_side)
-                pair = [pair[k] / (modes[:n, :] + modes[n + xo + k : n + xo + k + 1, :]) for k in range(2)]
+                field[yo * n : (yo + 1) * n, :] = box_i[tile_at(base_i, yo), :] * tile
+
+            shifted(box_j, base_j, gap, use_moved)
+            lane_side = sines[: 2 * LANES, :]
+            row_side = sines[2 * LANES :, : 3 * n]
+            other[...] = lane_turn(field[...], lane_side)
+            for at in range(0, half, 2):
+                pair = row_turn([rows_of(other, at + k) for k in range(2)], row_side)
+                for k in range(2):
+                    field[(at + k) * n : (at + k + 1) * n, :] = pair[k]
+            for at in range(0, half, 2):
+                pair = row_turn([swapped(field, at + k) for k in range(2)], row_side)
+                pair = [pair[k] / (modes[:n, :] + modes[n + at + k : n + at + k + 1, :]) for k in range(2)]
                 pair = row_turn(pair, row_side)
                 for k in range(2):
-                    other[(xo + k) * n : (xo + k + 1) * n, :] = pair[k]
-            for c in range(half // chunk):
-                tiles = []
-                for q in range(0, chunk, 2):
-                    tiles += row_turn([swapped(other, c * chunk + q + k) for k in range(2)], row_side)
-                field[c * rows : (c + 1) * rows, :] = lane_turn(jnp.concatenate(tiles, axis=0), lane_side)
-
-            @pl.when(which == 0)
-            def _():
+                    other[(at + k) * n : (at + k + 1) * n, :] = pair[k]
+            for at in range(0, half, 2):
+                pair = row_turn([swapped(other, at + k) for k in range(2)], row_side)
+                for k in range(2):
+                    field[(at + k) * n : (at + k + 1) * n, :] = pair[k]
+            field[...] = lane_turn(field[...], lane_side)
+
+            if outgoing:
                 for yo in range(half):
-                    here = slice(yo * n, (yo + 1) * n)
-                    there = pl.ds(i_at * (half * n) + yo * n, n)
-                    total[there, :] += field[here, :] * moved[here, :]
-
-            @pl.when(which == 1)
-            def _():
+                    there = pl.ds(own_at * (half * n) + yo * n, n)
+                    total[there, :] += rows_of(field, yo) * rows_of(moved, yo)
+            else:
                 for yo in range(half):
-                    here = slice(yo * n, (yo + 1) * n)
-                    put_j(yo, (field[here, :] * held_i[here, :]).astype(bf16).astype(f32))
+                    term = rows_of(field, yo) * held[tile_at(0, yo), :]
+                    held[tile_at(0, yo), :] = term.astype(bf16).astype(f32)
 
                 def add_back(yo, tile):
-                    there = pl.ds(j_at * (half * n) + yo * n, n)
+                    there = pl.ds(own_at * (half * n) + yo * n, n)
                     total[there, :] += tile
 
-                shifted([-k for k in gap], add_back)
-
-        return carry
-
-    lax.fori_loop(0, 2, task, 0)
+                shifted(held, 0, [-k for k in gap], add_back)
+
+    for outgoing in tasks:
+        task(outgoing)
 
     if last:
         for a in range(orbs):
@@ -312,24 +300,36 @@
     box[:, n * plane // ROWS :] = row.astype(f32).astype(bf16)
 
 
-def pair_step(step, pieces, first, last, mine, own, others, table, total):
-    orbs, n, plane = own.shape
+def setup(own, table, mine):
+    orbs, n, _ = own.shape
     half = n // 2
-    slots = pieces[1]
-    pieces = pieces[0] if last else 0
+    vmem = pl.BlockSpec(memory_space=pltpu.VMEM)
+    return pl.pallas_call(
+        setup_kernel,
+        out_shape=[
+            jax.ShapeDtypeStruct((orbs * half * (n + 2 * half), LANES), f32),
+            jax.ShapeDtypeStruct((table.shape[0], 2 * LANES), bf16),
+            jax.ShapeDtypeStruct((n + half, LANES), f32),
+            jax.ShapeDtypeStruct((orbs * half * n, LANES), f32),
+        ],
+        in_specs=[vmem, vmem, pl.BlockSpec(memory_space=pltpu.SMEM)],
+        out_specs=[vmem] * 4,
+        compiler_params=pltpu.CompilerParams(vmem_limit_bytes=16 << 20),
+        name="setup",
+    )(own, table, mine)
+
+
+def pair_step(name, n, slots, pieces, tasks, last, mine, own, sines, modes, others, total):
+    orbs = len(others)
+    plane = n * n
+    half = n // 2
+    pieces = pieces if last else 0
     vmem = pl.BlockSpec(memory_space=pltpu.VMEM)
     smem = pl.BlockSpec(memory_space=pltpu.SMEM)
-    operands = [mine, own, *others, table]
-    specs = [smem] + [vmem] * (2 + orbs)
-    if not first:
-        operands.append(total)
-        specs.append(vmem)
-    held = jax.ShapeDtypeStruct((orbs * half * n, LANES), f32)
+    held = jax.ShapeDtypeStruct(total.shape, f32)
     rows = half * n
     scratch = [
         pltpu.VMEM((n, plane), bf16),
-        pltpu.VMEM((n, plane), bf16),
-        pltpu.VMEM((rows, LANES), f32),
         pltpu.VMEM((half * (n + 2 * half), LANES), f32),
         pltpu.VMEM((rows, LANES), f32),
         pltpu.VMEM((rows, LANES), f32),
@@ -338,21 +338,22 @@
     ]
     shapes = held
     if last:
-        shapes = jax.ShapeDtypeStruct(own.shape, bf16)
+        shapes = jax.ShapeDtypeStruct((orbs, n, plane), bf16)
         if pieces:
             scratch.insert(0, pltpu.VMEM((orbs * n * plane // LANES, LANES), f32))
             shapes = [jax.ShapeDtypeStruct((8, orbs * n * plane // pieces // 8), bf16)] * pieces
         scratch.insert(0, pltpu.VMEM(held.shape, f32))
     return pl.pallas_call(
-        functools.partial(pair_kernel, (n, orbs, slots), pieces, first, last),
+        functools.partial(pair_kernel, (n, orbs, slots), pieces, tasks, last),
         out_shape=shapes,
-        in_specs=specs,
+        in_specs=[smem] + [vmem] * (4 + orbs),
         out_specs=[vmem] * pieces if pieces else vmem,
         scratch_shapes=scratch,
+        input_output_aliases={} if last else {4 + orbs: 0},
         compiler_params=pltpu.CompilerParams(vmem_limit_bytes=32 << 20),
         cost_estimate=pl.CostEstimate(flops=2 * 12 * 3 * n**4, bytes_accessed=4 * n**3 * 4, transcendentals=0),
-        name=f"pairs_{step}",
-    )(*operands)
+        name=name,
+    )(mine, own, sines, modes, *others, total)
 
 
 def gather_kernel(n, orbs, member_ref, *refs):
@@ -404,22 +405,19 @@
     by_pieces = devices & (devices - 1) == 0 and n % devices == 0 and n // devices * orbs == 12
     pieces = devices if by_pieces else 0
     ring = [(g, (g + 1) % groups) for g in range(groups)]
-    total = None
+    own, sines, modes, total = setup(orbitals, table, mine)
+    early = [total] * orbs
     for step in range(1, groups):
+        last = step == groups - 1
         held = [lax.ppermute(h, "grp", ring) for h in held]
         for q in range(orbs):
-            held[q], _ = lax.optimization_barrier((held[q], total))
-        total = pair_step(
-            step,
-            (pieces, slots),
-            step == 1,
-            step == groups - 1,
-            mine,
-            orbitals,
-            held,
-            table,
-            total,
-        )
+            held[q], _ = lax.optimization_barrier((held[q], early[q]))
+        early = []
+        for tasks in [(True, False)] if last else [(True,), (False,)]:
+            name = f"pairs_{step}_{len(early)}"
+            total = pair_step(name, n, slots, pieces, tasks, last, mine, own, sines, modes, held, total)
+            early.insert(0, total)
+        early = [early[0]] * (orbs - 1) + early[-1:]
     if not pieces:
         whole = total.reshape(orbs, n * plane)
         return lax.all_to_all(whole, "dev", split_axis=1, concat_axis=0, tiled=True).astype(f32)

time: 55.4 us -> 55.2 us (level)
  starting transfers between devices: 17.1 us -> 14.2 us
  waiting for transfers between devices: 21.2 us -> 23.9 us
    ppermute x6, starting transfers between devices: 7.68 us -> 4.73 us  [body(): held = [lax.ppermute(h, 'grp', ring) for h in held]]
    ppermute x6, waiting for transfers between devices: 18.1 us -> 20.9 us  [body(): held = [lax.ppermute(h, 'grp', ring) for h in held]]
    pallas_call x3 -> x6, Pallas kernels: 10.2 us -> 10.6 us  [the longest x5 9.64 us: pair_step(): pl.pallas_call(functools.partial(pair_kernel, (n, orbs, slots), pieces, t...]
  transfers between devices with their start and end apart: 13 -> 13, of which waited for: 8 -> 9; matrix products, arithmetic and copies ran while one was open for 0% -> 0% of each run, Pallas kernels for 16% -> 12%
where the time goes in v4:
time: 55.2 us
  waiting for transfers between devices  23.9 us (43%)
  starting transfers between devices  14.2 us (26%)
  Pallas kernels  13.7 us (25%)
  local copies, waits for them, and re-layouts  2.63 us (5%)
  between operations  0.74 us (1%)
    ppermute x6, waiting for transfers between devices, body(): held = [lax.ppermute(h, 'grp', ring) for h in held]  20.9 us
    pallas_call x5, Pallas kernels, pair_step(): pl.pallas_call(functools.partial(pair_kernel, (n, orbs, slots), pieces, t...  9.64 us
    ppermute x7, starting transfers between devices, body(): lax.ppermute(total[k], 'dev', [(d, d ^ k) for d in range(devices)])  9.52 us
    ppermute x6, starting transfers between devices, body(): held = [lax.ppermute(h, 'grp', ring) for h in held]  4.73 us
    ppermute x7, waiting for transfers between devices, body(): lax.ppermute(total[k], 'dev', [(d, d ^ k) for d in range(devices)])  3.01 us
    unnamed x6, local copies, waits for them, and re-layouts  2.63 us
    pallas_call x1, Pallas kernels, body(): pl.pallas_call(functools.partial(pack_kernel, groups), out_shape=[jax.Sha...  1.82 us
    pallas_call x1, Pallas kernels, body(): pl.pallas_call(functools.partial(gather_kernel, n, orbs), out_shape=jax.S...  1.3 us
  transfers between devices with their start and end apart: 13, of which 9 were waited for; matrix products, arithmetic and copies ran while one was open for 0% of the time, Pallas kernels for 12%

profile of v4, /device:TPU:0, one launch (start us, length us, event | category | flops | bytes accessed | tf_op | source)
XLA Modules:
  0.0 55.2 jit_solution(13150311877559562780)
XLA Ops:
  0.7 1.8 %pack.1 = (bf16[48,2304]{1,0:T(8,128)(2,1)}, bf16[16,7040]{1,0:T(8,128)(2,1)}, s32[1,17]{1,0:T(1,128)}) custom-call(s32[2,3]{1,0:T(2,128)} %offsets.1, s32[1,4,8]{2,1,0:T(4,128)} %bitcast.2, s32[1,1,2]{2,1,0:T(1,128)} %pair_local.1, s32[1,1,2]{2,1,0:T(1,128)} %pair_source.1, s32[1,1,1]{2,1,0:T(1,128)S(6)} %copy.16.pair_count, bf16[2,48,2304]{2,1,0:T(8,128)(2,1)} %own.1), custom_call_target="tpu_custom_call" | custom-call | tf_op jit(solution)/shard_map/pack/pallas_call | solution.py:394
  2.5 3.1 %collective-permute-start.2 = (bf16[16,7040]{1,0:T(8,128)(2,1)}, bf16[16,7040]{1,0:T(8,128)(2,1)S(1)}, u32[]{:S(2)}, u32[]{:S(2)}) collective-permute-start(bf16[16,7040]{1,0:T(8,128)(2,1)} %get-tuple-element.33), channel_id=1, source_target_pairs={{0,8},{8,16},{16,24},{24,0},{1,9},{9,17},{17,25},{25,1},{2,10},{10... | collective-permute-start | bytes 675848 | tf_op jit(solution)/shard_map/ppermute | solution.py:412
  5.6 1.6 %collective-permute-start = (bf16[48,2304]{1,0:T(8,128)(2,1)}, bf16[48,2304]{1,0:T(8,128)(2,1)S(1)}, u32[]{:S(2)}, u32[]{:S(2)}) collective-permute-start(bf16[48,2304]{1,0:T(8,128)(2,1)} %get-tuple-element.30), channel_id=1, source_target_pairs={{0,8},{8,16},{16,24},{24,0},{1,9},{9,17},{17,25},{25,1},{2,10},{10... | collective-permute-start | bytes 663560 | tf_op jit(solution)/shard_map/ppermute | solution.py:412
  7.1 1.0 %copy-done = bf16[2,48,2304]{2,1,0:T(8,128)(2,1)S(1)} copy-done((bf16[2,48,2304]{2,1,0:T(8,128)(2,1)S(1)}, bf16[2,48,2304]{2,1,0:T(8,128)(2,1)}, u32[]{:S(2)}) %copy-start) | copy-done | bytes 442392
  8.1 1.0 %copy-done.1 = f32[304,384]{1,0:T(8,128)S(1)} copy-done((f32[304,384]{1,0:T(8,128)S(1)}, f32[304,384]{1,0:T(8,128)}, u32[]{:S(2)}) %copy-start.1) | copy-done | bytes 466968
  9.2 0.6 %copy-done.2 = s32[1,17]{1,0:T(1,128)S(1)} copy-done((s32[1,17]{1,0:T(1,128)S(1)}, s32[1,17]{1,0:T(1,128)}, u32[]{:S(2)}) %copy-start.2) | copy-done | bytes 92
  9.8 0.9 %setup.1 = (f32[4608,128]{1,0:T(8,128)S(1)}, bf16[304,256]{1,0:T(8,128)(2,1)S(1)}, f32[72,128]{1,0:T(8,128)S(1)}, f32[2304,128]{1,0:T(8,128)S(1)}) custom-call(bf16[2,48,2304]{2,1,0:T(8,128)(2,1)S(1)} %copy-done, f32[304,384]{1,0:T(8,128)S(1)} %copy-done.1, s32[1,17]{1,0:T(1,128)S(1)} %copy-done.2), custom_call_target="tpu_custom_call" | custom-call | tf_op jit(solution)/shard_map/setup/pallas_call | solution.py:307
  10.7 3.4 %collective-permute-done.2.refs_5_ = bf16[16,7040]{1,0:T(8,128)(2,1)S(1)} collective-permute-done((bf16[16,7040]{1,0:T(8,128)(2,1)}, bf16[16,7040]{1,0:T(8,128)(2,1)S(1)}, u32[]{:S(2)}, u32[]{:S(2)}) %collective-permute-start.2) | collective-permute-done | bytes 225312 | tf_op jit(solution)/shard_map/ppermute | solution.py:412
  14.1 0.0 collective-permute-start.4
  14.2 4.7 %collective-permute-done.refs_4_ = bf16[48,2304]{1,0:T(8,128)(2,1)S(1)} collective-permute-done((bf16[48,2304]{1,0:T(8,128)(2,1)}, bf16[48,2304]{1,0:T(8,128)(2,1)S(1)}, u32[]{:S(2)}, u32[]{:S(2)}) %collective-permute-start) | collective-permute-done | bytes 221216 | tf_op jit(solution)/shard_map/ppermute | solution.py:412
  18.9 0.0 collective-permute-start.1
  18.9 0.8 %pairs_1_0.1.refs_6_ = f32[2304,128]{1,0:T(8,128)S(1)} custom-call(s32[1,17]{1,0:T(1,128)S(1)} %copy-done.2, f32[4608,128]{1,0:T(8,128)S(1)} %get-tuple-element.27.refs_1_, bf16[304,256]{1,0:T(8,128)(2,1)S(1)} %get-tuple-element.28.refs_2_, f32[72,128]{1,0:T(8,128)S(1)} %get-tuple-element.29.refs_3_, ...), custom_call_target="tpu_custom_call", output_to_operand_aliasing={{}: (6, {})} | custom-call | flops 382205952 | bytes 1769472 | tf_op jit(solution)/shard_map/pairs_1_0/pallas_call | solution.py:346
  19.7 4.2 %collective-permute-done.4.refs_5_ = bf16[16,7040]{1,0:T(8,128)(2,1)S(1)} collective-permute-done((bf16[16,7040]{1,0:T(8,128)(2,1)S(1)}, bf16[16,7040]{1,0:T(8,128)(2,1)S(1)}, u32[]{:S(2)}, u32[]{:S(2)}) %collective-permute-start.4) | collective-permute-done | bytes 225312 | tf_op jit(solution)/shard_map/ppermute | solution.py:412
  24.0 0.0 collective-permute-start.5
  24.0 0.8 %pairs_1_1.1.refs_6_ = f32[2304,128]{1,0:T(8,128)S(1)} custom-call(s32[1,17]{1,0:T(1,128)S(1)} %copy-done.2, f32[4608,128]{1,0:T(8,128)S(1)} %get-tuple-element.27.refs_1_, bf16[304,256]{1,0:T(8,128)(2,1)S(1)} %get-tuple-element.28.refs_2_, f32[72,128]{1,0:T(8,128)S(1)} %get-tuple-element.29.refs_3_, ...), custom_call_target="tpu_custom_call", output_to_operand_aliasing={{}: (6, {})} | custom-call | flops 382205952 | bytes 1769472 | tf_op jit(solution)/shard_map/pairs_1_1/pallas_call | solution.py:346
  24.8 4.3 %collective-permute-done.1.refs_4_ = bf16[48,2304]{1,0:T(8,128)(2,1)S(1)} collective-permute-done((bf16[48,2304]{1,0:T(8,128)(2,1)S(1)}, bf16[48,2304]{1,0:T(8,128)(2,1)S(1)}, u32[]{:S(2)}, u32[]{:S(2)}) %collective-permute-start.1) | collective-permute-done | bytes 221216 | tf_op jit(solution)/shard_map/ppermute | solution.py:412
  29.0 0.8 %pairs_2_0.1.refs_6_ = f32[2304,128]{1,0:T(8,128)S(1)} custom-call(s32[1,17]{1,0:T(1,128)S(1)} %copy-done.2, f32[4608,128]{1,0:T(8,128)S(1)} %get-tuple-element.27.refs_1_, bf16[304,256]{1,0:T(8,128)(2,1)S(1)} %get-tuple-element.28.refs_2_, f32[72,128]{1,0:T(8,128)S(1)} %get-tuple-element.29.refs_3_, ...), custom_call_target="tpu_custom_call", output_to_operand_aliasing={{}: (6, {})} | custom-call | flops 382205952 | bytes 1769472 | tf_op jit(solution)/shard_map/pairs_2_0/pallas_call | solution.py:346
  29.9 4.3 %collective-permute-done.5.refs_5_ = bf16[16,7040]{1,0:T(8,128)(2,1)S(1)} collective-permute-done((bf16[16,7040]{1,0:T(8,128)(2,1)S(1)}, bf16[16,7040]{1,0:T(8,128)(2,1)S(1)}, u32[]{:S(2)}, u32[]{:S(2)}) %collective-permute-start.5) | collective-permute-done | bytes 225312 | tf_op jit(solution)/shard_map/ppermute | solution.py:412
  34.1 3.3 %pairs_2_1.1.refs_6_ = f32[2304,128]{1,0:T(8,128)S(1)} custom-call(s32[1,17]{1,0:T(1,128)S(1)} %copy-done.2, f32[4608,128]{1,0:T(8,128)S(1)} %get-tuple-element.27.refs_1_, bf16[304,256]{1,0:T(8,128)(2,1)S(1)} %get-tuple-element.28.refs_2_, f32[72,128]{1,0:T(8,128)S(1)} %get-tuple-element.29.refs_3_, ...), custom_call_target="tpu_custom_call", output_to_operand_aliasing={{}: (6, {})} | custom-call | flops 382205952 | bytes 1769472 | tf_op jit(solution)/shard_map/pairs_2_1/pallas_call | solution.py:346
  37.4 0.0 collective-permute-done.3.refs_4_
  37.4 3.9 %pairs_3_0.1 = (bf16[8,3456]{1,0:T(8,128)(2,1)S(1)}, bf16[8,3456]{1,0:T(8,128)(2,1)S(1)}, bf16[8,3456]{1,0:T(8,128)(2,1)S(1)}, bf16[8,3456]{1,0:T(8,128)(2,1)S(1...) custom-call(s32[1,17]{1,0:T(1,128)S(1)} %copy-done.2, ...), custom_call_target="tpu_custom_call" | custom-call | flops 382205952 | bytes 1769472 | tf_op jit(solution)/shard_map/pairs_3_0/pallas_call | solution.py:346
  41.4 0.1 collective-permute-start.10
  41.4 5.3 %collective-permute-start.11 = (bf16[8,3456]{1,0:T(8,128)(2,1)S(1)}, bf16[8,3456]{1,0:T(8,128)(2,1)S(1)}, u32[]{:S(2)}, u32[]{:S(2)}) collective-permute-start(bf16[8,3456]{1,0:T(8,128)(2,1)S(1)} %get-tuple-element.45), channel_id=1, source_target_pairs={{0,6},{1,7},{2,4},{3,5},{4,2},{5,3},{6,0},{7,1},{8,14},{9,15},{10,... | collective-permute-start | bytes 165896 | tf_op jit(solution)/shard_map/ppermute | solution.py:426
  46.8 0.8 %collective-permute-start.12 = (bf16[8,3456]{1,0:T(8,128)(2,1)S(1)}, bf16[8,3456]{1,0:T(8,128)(2,1)S(1)}, u32[]{:S(2)}, u32[]{:S(2)}) collective-permute-start(bf16[8,3456]{1,0:T(8,128)(2,1)S(1)} %get-tuple-element.46), channel_id=1, source_target_pairs={{0,7},{1,6},{2,5},{3,4},{4,3},{5,2},{6,1},{7,0},{8,15},{9,14},{10,... | collective-permute-start | bytes 165896 | tf_op jit(solution)/shard_map/ppermute | solution.py:426
  47.5 2.1 %collective-permute-start.7 = (bf16[8,3456]{1,0:T(8,128)(2,1)S(1)}, bf16[8,3456]{1,0:T(8,128)(2,1)S(1)}, u32[]{:S(2)}, u32[]{:S(2)}) collective-permute-start(bf16[8,3456]{1,0:T(8,128)(2,1)S(1)} %get-tuple-element.41), channel_id=1, source_target_pairs={{0,2},{1,3},{2,0},{3,1},{4,6},{5,7},{6,4},{7,5},{8,10},{9,11},{10,... | collective-permute-start | bytes 165896 | tf_op jit(solution)/shard_map/ppermute | solution.py:426
  49.6 0.1 collective-permute-start.8
  49.8 1.1 %collective-permute-start.9 = (bf16[8,3456]{1,0:T(8,128)(2,1)S(1)}, bf16[8,3456]{1,0:T(8,128)(2,1)S(1)}, u32[]{:S(2)}, u32[]{:S(2)}) collective-permute-start(bf16[8,3456]{1,0:T(8,128)(2,1)S(1)} %get-tuple-element.43), channel_id=1, source_target_pairs={{0,4},{1,5},{2,6},{3,7},{4,0},{5,1},{6,2},{7,3},{8,12},{9,13},{10,... | collective-permute-start | bytes 165896 | tf_op jit(solution)/shard_map/ppermute | solution.py:426
  50.9 0.3 collective-permute-done.12.refs_7_
  51.2 1.6 %collective-permute-done.7.refs_2_ = bf16[8,3456]{1,0:T(8,128)(2,1)S(1)} collective-permute-done((bf16[8,3456]{1,0:T(8,128)(2,1)S(1)}, bf16[8,3456]{1,0:T(8,128)(2,1)S(1)}, u32[]{:S(2)}, u32[]{:S(2)}) %collective-permute-start.7) | collective-permute-done | bytes 55328 | tf_op jit(solution)/shard_map/ppermute | solution.py:426
  52.8 0.8 %collective-permute-done.8.refs_3_ = bf16[8,3456]{1,0:T(8,128)(2,1)S(1)} collective-permute-done((bf16[8,3456]{1,0:T(8,128)(2,1)S(1)}, bf16[8,3456]{1,0:T(8,128)(2,1)S(1)}, u32[]{:S(2)}, u32[]{:S(2)}) %collective-permute-start.8) | collective-permute-done | bytes 55328 | tf_op jit(solution)/shard_map/ppermute | solution.py:426
  53.6 0.3 collective-permute-done.9.refs_4_
  53.9 1.3 %cells.1 = f32[16,13824]{1,0:T(8,128)} custom-call(s32[1]{0:T(128)} %bitcast.member_ref, bf16[8,3456]{1,0:T(8,128)(2,1)S(1)} %get-tuple-element.39.refs_0_, bf16[8,3456]{1,0:T(8,128)(2,1)S(1)} %collective-permute-done.6.refs_1_, bf16[8,3456]{1,0:T(8,128)(2,1)S(1)} %collective-permute-done.7.refs_2_, bf16[8,3456]{1,0:T(8,128)(2,1)S(1)} %collective-permute-done.8.refs_3_, ...), custom_call_target="tpu_custom_call" | custom-call | tf_op jit(solution)/shard_map/cells/pallas_call | solution.py:427
  (8 shorter events, 0.0 us)
Async XLA Ops:
  2.5 11.7 %collective-permute-start.2 = (bf16[16,7040]{1,0:T(8,128)(2,1)}, bf16[16,7040]{1,0:T(8,128)(2,1)S(1)}, u32[]{:S(2)}, u32[]{:S(2)}) collective-permute-start(bf16[16,7040]{1,0:T(8,128)(2,1)} %get-tuple-element.33), channel_id=1, source_target_pairs={{0,8},{8,16},{16,24},{24,0},{1,9},{9,17},{17,25},{25,1},{2,10},{10... | collective-permute-start | bytes 675848 | tf_op jit(solution)/shard_map/ppermute | solution.py:412
  5.6 13.3 %collective-permute-start = (bf16[48,2304]{1,0:T(8,128)(2,1)}, bf16[48,2304]{1,0:T(8,128)(2,1)S(1)}, u32[]{:S(2)}, u32[]{:S(2)}) collective-permute-start(bf16[48,2304]{1,0:T(8,128)(2,1)} %get-tuple-element.30), channel_id=1, source_target_pairs={{0,8},{8,16},{16,24},{24,0},{1,9},{9,17},{17,25},{25,1},{2,10},{10... | collective-permute-start | bytes 663560 | tf_op jit(solution)/shard_map/ppermute | solution.py:412
  7.1 1.0 %copy-start = (bf16[2,48,2304]{2,1,0:T(8,128)(2,1)S(1)}, bf16[2,48,2304]{2,1,0:T(8,128)(2,1)}, u32[]{:S(2)}) copy-start(bf16[2,48,2304]{2,1,0:T(8,128)(2,1)} %own.1) | copy-start | bytes 1327108
  8.1 1.0 %copy-start.1 = (f32[304,384]{1,0:T(8,128)S(1)}, f32[304,384]{1,0:T(8,128)}, u32[]{:S(2)}) copy-start(f32[304,384]{1,0:T(8,128)} %constant.6.clone.table) | copy-start | bytes 1400836
  9.2 0.6 %copy-start.2 = (s32[1,17]{1,0:T(1,128)S(1)}, s32[1,17]{1,0:T(1,128)}, u32[]{:S(2)}) copy-start(s32[1,17]{1,0:T(1,128)} %get-tuple-element.26.mine.refs_0_) | copy-start | bytes 208
  14.1 9.8 %collective-permute-start.4 = (bf16[16,7040]{1,0:T(8,128)(2,1)S(1)}, bf16[16,7040]{1,0:T(8,128)(2,1)S(1)}, u32[]{:S(2)}, u32[]{:S(2)}) collective-permute-start(bf16[16,7040]{1,0:T(8,128)(2,1)S(1)} %collective-permute-done.2.refs_5_), channel_id=1, source_target_pairs={{0,8},{8,16},{16,24},{24,0},{1,9},{9,17},{17,25},{25,1},{2,10},{10... | collective-permute-start | bytes 675848 | tf_op jit(solution)/shard_map/ppermute | solution.py:412
  18.9 10.2 %collective-permute-start.1 = (bf16[48,2304]{1,0:T(8,128)(2,1)S(1)}, bf16[48,2304]{1,0:T(8,128)(2,1)S(1)}, u32[]{:S(2)}, u32[]{:S(2)}) collective-permute-start(bf16[48,2304]{1,0:T(8,128)(2,1)S(1)} %collective-permute-done.refs_4_), channel_id=1, source_target_pairs={{0,8},{8,16},{16,24},{24,0},{1,9},{9,17},{17,25},{25,1},{2,10},{10... | collective-permute-start | bytes 663560 | tf_op jit(solution)/shard_map/ppermute | solution.py:412
  24.0 10.2 %collective-permute-start.5 = (bf16[16,7040]{1,0:T(8,128)(2,1)S(1)}, bf16[16,7040]{1,0:T(8,128)(2,1)S(1)}, u32[]{:S(2)}, u32[]{:S(2)}) collective-permute-start(bf16[16,7040]{1,0:T(8,128)(2,1)S(1)} %collective-permute-done.4.refs_5_), channel_id=1, source_target_pairs={{0,8},{8,16},{16,24},{24,0},{1,9},{9,17},{17,25},{25,1},{2,10},{10... | collective-permute-start | bytes 675848 | tf_op jit(solution)/shard_map/ppermute | solution.py:412
  29.0 8.4 %collective-permute-start.3 = (bf16[48,2304]{1,0:T(8,128)(2,1)S(1)}, bf16[48,2304]{1,0:T(8,128)(2,1)S(1)}, u32[]{:S(2)}, u32[]{:S(2)}) collective-permute-start(bf16[48,2304]{1,0:T(8,128)(2,1)S(1)} %collective-permute-done.1.refs_4_), channel_id=1, source_target_pairs={{0,8},{8,16},{16,24},{24,0},{1,9},{9,17},{17,25},{25,1},{2,10},{10... | collective-permute-start | bytes 663560 | tf_op jit(solution)/shard_map/ppermute | solution.py:412
  41.4 8.2 %collective-permute-start.10 = (bf16[8,3456]{1,0:T(8,128)(2,1)S(1)}, bf16[8,3456]{1,0:T(8,128)(2,1)S(1)}, u32[]{:S(2)}, u32[]{:S(2)}) collective-permute-start(bf16[8,3456]{1,0:T(8,128)(2,1)S(1)} %get-tuple-element.44), channel_id=1, source_target_pairs={{0,5},{1,4},{2,7},{3,6},{4,1},{5,0},{6,3},{7,2},{8,13},{9,12},{10,... | collective-permute-start | bytes 165896 | tf_op jit(solution)/shard_map/ppermute | solution.py:426
  41.4 8.3 %collective-permute-start.11 = (bf16[8,3456]{1,0:T(8,128)(2,1)S(1)}, bf16[8,3456]{1,0:T(8,128)(2,1)S(1)}, u32[]{:S(2)}, u32[]{:S(2)}) collective-permute-start(bf16[8,3456]{1,0:T(8,128)(2,1)S(1)} %get-tuple-element.45), channel_id=1, source_target_pairs={{0,6},{1,7},{2,4},{3,5},{4,2},{5,3},{6,0},{7,1},{8,14},{9,15},{10,... | collective-permute-start | bytes 165896 | tf_op jit(solution)/shard_map/ppermute | solution.py:426
  46.8 4.5 %collective-permute-start.12 = (bf16[8,3456]{1,0:T(8,128)(2,1)S(1)}, bf16[8,3456]{1,0:T(8,128)(2,1)S(1)}, u32[]{:S(2)}, u32[]{:S(2)}) collective-permute-start(bf16[8,3456]{1,0:T(8,128)(2,1)S(1)} %get-tuple-element.46), channel_id=1, source_target_pairs={{0,7},{1,6},{2,5},{3,4},{4,3},{5,2},{6,1},{7,0},{8,15},{9,14},{10,... | collective-permute-start | bytes 165896 | tf_op jit(solution)/shard_map/ppermute | solution.py:426
  47.5 3.7 %collective-permute-start.6 = (bf16[8,3456]{1,0:T(8,128)(2,1)S(1)}, bf16[8,3456]{1,0:T(8,128)(2,1)S(1)}, u32[]{:S(2)}, u32[]{:S(2)}) collective-permute-start(bf16[8,3456]{1,0:T(8,128)(2,1)S(1)} %get-tuple-element.40), channel_id=1, source_target_pairs={{0,1},{1,0},{2,3},{3,2},{4,5},{5,4},{6,7},{7,6},{8,9},{9,8},{10,11... | collective-permute-start | bytes 165896 | tf_op jit(solution)/shard_map/ppermute | solution.py:426
  47.5 5.3 %collective-permute-start.7 = (bf16[8,3456]{1,0:T(8,128)(2,1)S(1)}, bf16[8,3456]{1,0:T(8,128)(2,1)S(1)}, u32[]{:S(2)}, u32[]{:S(2)}) collective-permute-start(bf16[8,3456]{1,0:T(8,128)(2,1)S(1)} %get-tuple-element.41), channel_id=1, source_target_pairs={{0,2},{1,3},{2,0},{3,1},{4,6},{5,7},{6,4},{7,5},{8,10},{9,11},{10,... | collective-permute-start | bytes 165896 | tf_op jit(solution)/shard_map/ppermute | solution.py:426
  49.6 4.0 %collective-permute-start.8 = (bf16[8,3456]{1,0:T(8,128)(2,1)S(1)}, bf16[8,3456]{1,0:T(8,128)(2,1)S(1)}, u32[]{:S(2)}, u32[]{:S(2)}) collective-permute-start(bf16[8,3456]{1,0:T(8,128)(2,1)S(1)} %get-tuple-element.42), channel_id=1, source_target_pairs={{0,3},{1,2},{2,1},{3,0},{4,7},{5,6},{6,5},{7,4},{8,11},{9,10},{10,... | collective-permute-start | bytes 165896 | tf_op jit(solution)/shard_map/ppermute | solution.py:426
  49.8 4.2 %collective-permute-start.9 = (bf16[8,3456]{1,0:T(8,128)(2,1)S(1)}, bf16[8,3456]{1,0:T(8,128)(2,1)S(1)}, u32[]{:S(2)}, u32[]{:S(2)}) collective-permute-start(bf16[8,3456]{1,0:T(8,128)(2,1)S(1)} %get-tuple-element.43), channel_id=1, source_target_pairs={{0,4},{1,5},{2,6},{3,7},{4,0},{5,1},{6,2},{7,3},{8,12},{9,13},{10,... | collective-permute-start | bytes 165896 | tf_op jit(solution)/shard_map/ppermute | solution.py:426

commit v5 on v4

--- a/solution.py
+++ b/solution.py
@@ -64,7 +64,7 @@
         high, low = split(tile)
         columns.append(jnp.concatenate([high, low, high], axis=0))
     out = jnp.dot(row_side, jnp.concatenate(columns, axis=1), preferred_element_type=f32)
-    return out[:, :LANES], out[:, LANES:]
+    return [out[:, k * LANES : (k + 1) * LANES] for k in range(len(tiles))]
 
 
 def unpack(dense, put):
@@ -211,20 +211,17 @@
             lane_side = sines[: 2 * LANES, :]
             row_side = sines[2 * LANES :, : 3 * n]
             other[...] = lane_turn(field[...], lane_side)
-            for at in range(0, half, 2):
-                pair = row_turn([rows_of(other, at + k) for k in range(2)], row_side)
-                for k in range(2):
-                    field[(at + k) * n : (at + k + 1) * n, :] = pair[k]
-            for at in range(0, half, 2):
-                pair = row_turn([swapped(field, at + k) for k in range(2)], row_side)
-                pair = [pair[k] / (modes[:n, :] + modes[n + at + k : n + at + k + 1, :]) for k in range(2)]
-                pair = row_turn(pair, row_side)
-                for k in range(2):
-                    other[(at + k) * n : (at + k + 1) * n, :] = pair[k]
-            for at in range(0, half, 2):
-                pair = row_turn([swapped(other, at + k) for k in range(2)], row_side)
-                for k in range(2):
-                    field[(at + k) * n : (at + k + 1) * n, :] = pair[k]
+            tiles = row_turn([rows_of(other, at) for at in range(half)], row_side)
+            for at in range(half):
+                field[at * n : (at + 1) * n, :] = tiles[at]
+            tiles = row_turn([swapped(field, at) for at in range(half)], row_side)
+            tiles = [tiles[at] / (modes[:n, :] + modes[n + at : n + at + 1, :]) for at in range(half)]
+            tiles = row_turn(tiles, row_side)
+            for at in range(half):
+                other[at * n : (at + 1) * n, :] = tiles[at]
+            tiles = row_turn([swapped(other, at) for at in range(half)], row_side)
+            for at in range(half):
+                field[at * n : (at + 1) * n, :] = tiles[at]
             field[...] = lane_turn(field[...], lane_side)
 
             if outgoing:

time: 55.2 us -> 54 us (0.978)
  starting transfers between devices: 14.2 us -> 13.1 us
  Pallas kernels: 13.7 us -> 12.8 us
  waiting for transfers between devices: 23.9 us -> 24.5 us
    ppermute x7, starting transfers between devices: 9.52 us -> 8.34 us  [body(): lax.ppermute(total[k], 'dev', [(d, d ^ k) for d in range(devices)])]
    pallas_call x5, Pallas kernels: 9.64 us -> 8.71 us  [pair_step(): pl.pallas_call(functools.partial(pair_kernel, (n, orbs, slots), pieces, t...]
  transfers between devices with their start and end apart: 13 -> 13, of which waited for: 9 -> 10; matrix products, arithmetic and copies ran while one was open for 0% -> 0% of each run, Pallas kernels for 12% -> 12%
where the time goes in v5:
time: 54 us; the launch traced here: 53.7 us
  waiting for transfers between devices  24.5 us (45%)
  starting transfers between devices  13.1 us (24%)
  Pallas kernels  12.8 us (24%)
  local copies, waits for them, and re-layouts  2.63 us (5%)
  between operations  0.73 us (1%)
    ppermute x6, waiting for transfers between devices, body(): held = [lax.ppermute(h, 'grp', ring) for h in held]  21.1 us
    pallas_call x5, Pallas kernels, pair_step(): pl.pallas_call(functools.partial(pair_kernel, (n, orbs, slots), pieces, t...  8.71 us
    ppermute x7, starting transfers between devices, body(): lax.ppermute(total[k], 'dev', [(d, d ^ k) for d in range(devices)])  8.34 us
    ppermute x6, starting transfers between devices, body(): held = [lax.ppermute(h, 'grp', ring) for h in held]  4.73 us
    ppermute x7, waiting for transfers between devices, body(): lax.ppermute(total[k], 'dev', [(d, d ^ k) for d in range(devices)])  3.47 us
    unnamed x6, local copies, waits for them, and re-layouts  2.63 us
    pallas_call x1, Pallas kernels, body(): pl.pallas_call(functools.partial(pack_kernel, groups), out_shape=[jax.Sha...  1.82 us
    pallas_call x1, Pallas kernels, body(): pl.pallas_call(functools.partial(gather_kernel, n, orbs), out_shape=jax.S...  1.3 us
  transfers between devices with their start and end apart: 13, of which 10 were waited for; matrix products, arithmetic and copies ran while one was open for 0% of the time, Pallas kernels for 12%

profile of v5, /device:TPU:0, one launch (start us, length us, event | category | flops | bytes accessed | tf_op | source)
XLA Modules:
  0.0 53.7 jit_solution(8110840445809484913)
XLA Ops:
  0.7 1.8 %pack.1 = (bf16[48,2304]{1,0:T(8,128)(2,1)}, bf16[16,7040]{1,0:T(8,128)(2,1)}, s32[1,17]{1,0:T(1,128)}) custom-call(s32[2,3]{1,0:T(2,128)} %offsets.1, s32[1,4,8]{2,1,0:T(4,128)} %bitcast.2, s32[1,1,2]{2,1,0:T(1,128)} %pair_local.1, s32[1,1,2]{2,1,0:T(1,128)} %pair_source.1, s32[1,1,1]{2,1,0:T(1,128)S(6)} %copy.16.pair_count, bf16[2,48,2304]{2,1,0:T(8,128)(2,1)} %own.1), custom_call_target="tpu_custom_call" | custom-call | tf_op jit(solution)/shard_map/pack/pallas_call | solution.py:391
  2.5 3.1 %collective-permute-start.2 = (bf16[16,7040]{1,0:T(8,128)(2,1)}, bf16[16,7040]{1,0:T(8,128)(2,1)S(1)}, u32[]{:S(2)}, u32[]{:S(2)}) collective-permute-start(bf16[16,7040]{1,0:T(8,128)(2,1)} %get-tuple-element.33), channel_id=1, source_target_pairs={{0,8},{8,16},{16,24},{24,0},{1,9},{9,17},{17,25},{25,1},{2,10},{10... | collective-permute-start | bytes 675848 | tf_op jit(solution)/shard_map/ppermute | solution.py:409
  5.6 1.6 %collective-permute-start = (bf16[48,2304]{1,0:T(8,128)(2,1)}, bf16[48,2304]{1,0:T(8,128)(2,1)S(1)}, u32[]{:S(2)}, u32[]{:S(2)}) collective-permute-start(bf16[48,2304]{1,0:T(8,128)(2,1)} %get-tuple-element.30), channel_id=1, source_target_pairs={{0,8},{8,16},{16,24},{24,0},{1,9},{9,17},{17,25},{25,1},{2,10},{10... | collective-permute-start | bytes 663560 | tf_op jit(solution)/shard_map/ppermute | solution.py:409
  7.1 1.0 %copy-done = bf16[2,48,2304]{2,1,0:T(8,128)(2,1)S(1)} copy-done((bf16[2,48,2304]{2,1,0:T(8,128)(2,1)S(1)}, bf16[2,48,2304]{2,1,0:T(8,128)(2,1)}, u32[]{:S(2)}) %copy-start) | copy-done | bytes 442392
  8.1 1.0 %copy-done.1 = f32[304,384]{1,0:T(8,128)S(1)} copy-done((f32[304,384]{1,0:T(8,128)S(1)}, f32[304,384]{1,0:T(8,128)}, u32[]{:S(2)}) %copy-start.1) | copy-done | bytes 466968
  9.2 0.6 %copy-done.2 = s32[1,17]{1,0:T(1,128)S(1)} copy-done((s32[1,17]{1,0:T(1,128)S(1)}, s32[1,17]{1,0:T(1,128)}, u32[]{:S(2)}) %copy-start.2) | copy-done | bytes 92
  9.8 0.9 %setup.1 = (f32[4608,128]{1,0:T(8,128)S(1)}, bf16[304,256]{1,0:T(8,128)(2,1)S(1)}, f32[72,128]{1,0:T(8,128)S(1)}, f32[2304,128]{1,0:T(8,128)S(1)}) custom-call(bf16[2,48,2304]{2,1,0:T(8,128)(2,1)S(1)} %copy-done, f32[304,384]{1,0:T(8,128)S(1)} %copy-done.1, s32[1,17]{1,0:T(1,128)S(1)} %copy-done.2), custom_call_target="tpu_custom_call" | custom-call | tf_op jit(solution)/shard_map/setup/pallas_call | solution.py:304
  10.7 3.4 %collective-permute-done.2.refs_5_ = bf16[16,7040]{1,0:T(8,128)(2,1)S(1)} collective-permute-done((bf16[16,7040]{1,0:T(8,128)(2,1)}, bf16[16,7040]{1,0:T(8,128)(2,1)S(1)}, u32[]{:S(2)}, u32[]{:S(2)}) %collective-permute-start.2) | collective-permute-done | bytes 225312 | tf_op jit(solution)/shard_map/ppermute | solution.py:409
  14.1 0.0 collective-permute-start.4
  14.2 4.7 %collective-permute-done.refs_4_ = bf16[48,2304]{1,0:T(8,128)(2,1)S(1)} collective-permute-done((bf16[48,2304]{1,0:T(8,128)(2,1)}, bf16[48,2304]{1,0:T(8,128)(2,1)S(1)}, u32[]{:S(2)}, u32[]{:S(2)}) %collective-permute-start) | collective-permute-done | bytes 221216 | tf_op jit(solution)/shard_map/ppermute | solution.py:409
  18.9 0.0 collective-permute-start.1
  18.9 0.8 %pairs_1_0.1.refs_6_ = f32[2304,128]{1,0:T(8,128)S(1)} custom-call(s32[1,17]{1,0:T(1,128)S(1)} %copy-done.2, f32[4608,128]{1,0:T(8,128)S(1)} %get-tuple-element.27.refs_1_, bf16[304,256]{1,0:T(8,128)(2,1)S(1)} %get-tuple-element.28.refs_2_, f32[72,128]{1,0:T(8,128)S(1)} %get-tuple-element.29.refs_3_, ...), custom_call_target="tpu_custom_call", output_to_operand_aliasing={{}: (6, {})} | custom-call | flops 382205952 | bytes 1769472 | tf_op jit(solution)/shard_map/pairs_1_0/pallas_call | solution.py:343
  19.7 4.2 %collective-permute-done.4.refs_5_ = bf16[16,7040]{1,0:T(8,128)(2,1)S(1)} collective-permute-done((bf16[16,7040]{1,0:T(8,128)(2,1)S(1)}, bf16[16,7040]{1,0:T(8,128)(2,1)S(1)}, u32[]{:S(2)}, u32[]{:S(2)}) %collective-permute-start.4) | collective-permute-done | bytes 225312 | tf_op jit(solution)/shard_map/ppermute | solution.py:409
  24.0 0.0 collective-permute-start.5
  24.0 2.9 %pairs_1_1.1.refs_6_ = f32[2304,128]{1,0:T(8,128)S(1)} custom-call(s32[1,17]{1,0:T(1,128)S(1)} %copy-done.2, f32[4608,128]{1,0:T(8,128)S(1)} %get-tuple-element.27.refs_1_, bf16[304,256]{1,0:T(8,128)(2,1)S(1)} %get-tuple-element.28.refs_2_, f32[72,128]{1,0:T(8,128)S(1)} %get-tuple-element.29.refs_3_, ...), custom_call_target="tpu_custom_call", output_to_operand_aliasing={{}: (6, {})} | custom-call | flops 382205952 | bytes 1769472 | tf_op jit(solution)/shard_map/pairs_1_1/pallas_call | solution.py:343
  26.8 2.2 %collective-permute-done.1.refs_4_ = bf16[48,2304]{1,0:T(8,128)(2,1)S(1)} collective-permute-done((bf16[48,2304]{1,0:T(8,128)(2,1)S(1)}, bf16[48,2304]{1,0:T(8,128)(2,1)S(1)}, u32[]{:S(2)}, u32[]{:S(2)}) %collective-permute-start.1) | collective-permute-done | bytes 221216 | tf_op jit(solution)/shard_map/ppermute | solution.py:409
  29.0 0.8 %pairs_2_0.1.refs_6_ = f32[2304,128]{1,0:T(8,128)S(1)} custom-call(s32[1,17]{1,0:T(1,128)S(1)} %copy-done.2, f32[4608,128]{1,0:T(8,128)S(1)} %get-tuple-element.27.refs_1_, bf16[304,256]{1,0:T(8,128)(2,1)S(1)} %get-tuple-element.28.refs_2_, f32[72,128]{1,0:T(8,128)S(1)} %get-tuple-element.29.refs_3_, ...), custom_call_target="tpu_custom_call", output_to_operand_aliasing={{}: (6, {})} | custom-call | flops 382205952 | bytes 1769472 | tf_op jit(solution)/shard_map/pairs_2_0/pallas_call | solution.py:343
  29.9 4.3 %collective-permute-done.5.refs_5_ = bf16[16,7040]{1,0:T(8,128)(2,1)S(1)} collective-permute-done((bf16[16,7040]{1,0:T(8,128)(2,1)S(1)}, bf16[16,7040]{1,0:T(8,128)(2,1)S(1)}, u32[]{:S(2)}, u32[]{:S(2)}) %collective-permute-start.5) | collective-permute-done | bytes 225312 | tf_op jit(solution)/shard_map/ppermute | solution.py:409
  34.1 0.8 %pairs_2_1.1.refs_6_ = f32[2304,128]{1,0:T(8,128)S(1)} custom-call(s32[1,17]{1,0:T(1,128)S(1)} %copy-done.2, f32[4608,128]{1,0:T(8,128)S(1)} %get-tuple-element.27.refs_1_, bf16[304,256]{1,0:T(8,128)(2,1)S(1)} %get-tuple-element.28.refs_2_, f32[72,128]{1,0:T(8,128)S(1)} %get-tuple-element.29.refs_3_, ...), custom_call_target="tpu_custom_call", output_to_operand_aliasing={{}: (6, {})} | custom-call | flops 382205952 | bytes 1769472 | tf_op jit(solution)/shard_map/pairs_2_1/pallas_call | solution.py:343
  35.0 2.2 %collective-permute-done.3.refs_4_ = bf16[48,2304]{1,0:T(8,128)(2,1)S(1)} collective-permute-done((bf16[48,2304]{1,0:T(8,128)(2,1)S(1)}, bf16[48,2304]{1,0:T(8,128)(2,1)S(1)}, u32[]{:S(2)}, u32[]{:S(2)}) %collective-permute-start.3) | collective-permute-done | bytes 221216 | tf_op jit(solution)/shard_map/ppermute | solution.py:409
  37.2 3.4 %pairs_3_0.1 = (bf16[8,3456]{1,0:T(8,128)(2,1)S(1)}, bf16[8,3456]{1,0:T(8,128)(2,1)S(1)}, bf16[8,3456]{1,0:T(8,128)(2,1)S(1)}, bf16[8,3456]{1,0:T(8,128)(2,1)S(1...) custom-call(s32[1,17]{1,0:T(1,128)S(1)} %copy-done.2, ...), custom_call_target="tpu_custom_call" | custom-call | flops 382205952 | bytes 1769472 | tf_op jit(solution)/shard_map/pairs_3_0/pallas_call | solution.py:343
  40.6 0.1 collective-permute-start.10
  40.7 4.6 %collective-permute-start.11 = (bf16[8,3456]{1,0:T(8,128)(2,1)S(1)}, bf16[8,3456]{1,0:T(8,128)(2,1)S(1)}, u32[]{:S(2)}, u32[]{:S(2)}) collective-permute-start(bf16[8,3456]{1,0:T(8,128)(2,1)S(1)} %get-tuple-element.45), channel_id=1, source_target_pairs={{0,6},{1,7},{2,4},{3,5},{4,2},{5,3},{6,0},{7,1},{8,14},{9,15},{10,... | collective-permute-start | bytes 165896 | tf_op jit(solution)/shard_map/ppermute | solution.py:423
  45.2 0.2 collective-permute-start.6
  45.4 2.7 %collective-permute-start.7 = (bf16[8,3456]{1,0:T(8,128)(2,1)S(1)}, bf16[8,3456]{1,0:T(8,128)(2,1)S(1)}, u32[]{:S(2)}, u32[]{:S(2)}) collective-permute-start(bf16[8,3456]{1,0:T(8,128)(2,1)S(1)} %get-tuple-element.41), channel_id=1, source_target_pairs={{0,2},{1,3},{2,0},{3,1},{4,6},{5,7},{6,4},{7,5},{8,10},{9,11},{10,... | collective-permute-start | bytes 165896 | tf_op jit(solution)/shard_map/ppermute | solution.py:423
  48.1 0.1 collective-permute-start.8
  48.2 0.7 %collective-permute-start.9 = (bf16[8,3456]{1,0:T(8,128)(2,1)S(1)}, bf16[8,3456]{1,0:T(8,128)(2,1)S(1)}, u32[]{:S(2)}, u32[]{:S(2)}) collective-permute-start(bf16[8,3456]{1,0:T(8,128)(2,1)S(1)} %get-tuple-element.43), channel_id=1, source_target_pairs={{0,4},{1,5},{2,6},{3,7},{4,0},{5,1},{6,2},{7,3},{8,12},{9,13},{10,... | collective-permute-start | bytes 165896 | tf_op jit(solution)/shard_map/ppermute | solution.py:423
  48.9 0.8 %collective-permute-done.12.refs_7_ = bf16[8,3456]{1,0:T(8,128)(2,1)S(1)} collective-permute-done((bf16[8,3456]{1,0:T(8,128)(2,1)S(1)}, bf16[8,3456]{1,0:T(8,128)(2,1)S(1)}, u32[]{:S(2)}, u32[]{:S(2)}) %collective-permute-start.12) | collective-permute-done | bytes 55328 | tf_op jit(solution)/shard_map/ppermute | solution.py:423
  49.7 1.6 %collective-permute-done.7.refs_2_ = bf16[8,3456]{1,0:T(8,128)(2,1)S(1)} collective-permute-done((bf16[8,3456]{1,0:T(8,128)(2,1)S(1)}, bf16[8,3456]{1,0:T(8,128)(2,1)S(1)}, u32[]{:S(2)}, u32[]{:S(2)}) %collective-permute-start.7) | collective-permute-done | bytes 55328 | tf_op jit(solution)/shard_map/ppermute | solution.py:423
  51.3 0.8 %collective-permute-done.8.refs_3_ = bf16[8,3456]{1,0:T(8,128)(2,1)S(1)} collective-permute-done((bf16[8,3456]{1,0:T(8,128)(2,1)S(1)}, bf16[8,3456]{1,0:T(8,128)(2,1)S(1)}, u32[]{:S(2)}, u32[]{:S(2)}) %collective-permute-start.8) | collective-permute-done | bytes 55328 | tf_op jit(solution)/shard_map/ppermute | solution.py:423
  52.1 0.3 collective-permute-done.9.refs_4_
  52.4 1.3 %cells.1 = f32[16,13824]{1,0:T(8,128)} custom-call(s32[1]{0:T(128)} %bitcast.member_ref, bf16[8,3456]{1,0:T(8,128)(2,1)S(1)} %get-tuple-element.39.refs_0_, bf16[8,3456]{1,0:T(8,128)(2,1)S(1)} %collective-permute-done.6.refs_1_, bf16[8,3456]{1,0:T(8,128)(2,1)S(1)} %collective-permute-done.7.refs_2_, bf16[8,3456]{1,0:T(8,128)(2,1)S(1)} %collective-permute-done.8.refs_3_, ...), custom_call_target="tpu_custom_call" | custom-call | tf_op jit(solution)/shard_map/cells/pallas_call | solution.py:424
  (8 shorter events, 0.0 us)
Async XLA Ops:
  2.5 11.7 %collective-permute-start.2 = (bf16[16,7040]{1,0:T(8,128)(2,1)}, bf16[16,7040]{1,0:T(8,128)(2,1)S(1)}, u32[]{:S(2)}, u32[]{:S(2)}) collective-permute-start(bf16[16,7040]{1,0:T(8,128)(2,1)} %get-tuple-element.33), channel_id=1, source_target_pairs={{0,8},{8,16},{16,24},{24,0},{1,9},{9,17},{17,25},{25,1},{2,10},{10... | collective-permute-start | bytes 675848 | tf_op jit(solution)/shard_map/ppermute | solution.py:409
  5.6 13.3 %collective-permute-start = (bf16[48,2304]{1,0:T(8,128)(2,1)}, bf16[48,2304]{1,0:T(8,128)(2,1)S(1)}, u32[]{:S(2)}, u32[]{:S(2)}) collective-permute-start(bf16[48,2304]{1,0:T(8,128)(2,1)} %get-tuple-element.30), channel_id=1, source_target_pairs={{0,8},{8,16},{16,24},{24,0},{1,9},{9,17},{17,25},{25,1},{2,10},{10... | collective-permute-start | bytes 663560 | tf_op jit(solution)/shard_map/ppermute | solution.py:409
  7.1 1.0 %copy-start = (bf16[2,48,2304]{2,1,0:T(8,128)(2,1)S(1)}, bf16[2,48,2304]{2,1,0:T(8,128)(2,1)}, u32[]{:S(2)}) copy-start(bf16[2,48,2304]{2,1,0:T(8,128)(2,1)} %own.1) | copy-start | bytes 1327108
  8.1 1.0 %copy-start.1 = (f32[304,384]{1,0:T(8,128)S(1)}, f32[304,384]{1,0:T(8,128)}, u32[]{:S(2)}) copy-start(f32[304,384]{1,0:T(8,128)} %constant.6.clone.table) | copy-start | bytes 1400836
  9.2 0.6 %copy-start.2 = (s32[1,17]{1,0:T(1,128)S(1)}, s32[1,17]{1,0:T(1,128)}, u32[]{:S(2)}) copy-start(s32[1,17]{1,0:T(1,128)} %get-tuple-element.26.mine.refs_0_) | copy-start | bytes 208
  14.1 9.8 %collective-permute-start.4 = (bf16[16,7040]{1,0:T(8,128)(2,1)S(1)}, bf16[16,7040]{1,0:T(8,128)(2,1)S(1)}, u32[]{:S(2)}, u32[]{:S(2)}) collective-permute-start(bf16[16,7040]{1,0:T(8,128)(2,1)S(1)} %collective-permute-done.2.refs_5_), channel_id=1, source_target_pairs={{0,8},{8,16},{16,24},{24,0},{1,9},{9,17},{17,25},{25,1},{2,10},{10... | collective-permute-start | bytes 675848 | tf_op jit(solution)/shard_map/ppermute | solution.py:409
  18.9 10.2 %collective-permute-start.1 = (bf16[48,2304]{1,0:T(8,128)(2,1)S(1)}, bf16[48,2304]{1,0:T(8,128)(2,1)S(1)}, u32[]{:S(2)}, u32[]{:S(2)}) collective-permute-start(bf16[48,2304]{1,0:T(8,128)(2,1)S(1)} %collective-permute-done.refs_4_), channel_id=1, source_target_pairs={{0,8},{8,16},{16,24},{24,0},{1,9},{9,17},{17,25},{25,1},{2,10},{10... | collective-permute-start | bytes 663560 | tf_op jit(solution)/shard_map/ppermute | solution.py:409
  24.0 10.2 %collective-permute-start.5 = (bf16[16,7040]{1,0:T(8,128)(2,1)S(1)}, bf16[16,7040]{1,0:T(8,128)(2,1)S(1)}, u32[]{:S(2)}, u32[]{:S(2)}) collective-permute-start(bf16[16,7040]{1,0:T(8,128)(2,1)S(1)} %collective-permute-done.4.refs_5_), channel_id=1, source_target_pairs={{0,8},{8,16},{16,24},{24,0},{1,9},{9,17},{17,25},{25,1},{2,10},{10... | collective-permute-start | bytes 675848 | tf_op jit(solution)/shard_map/ppermute | solution.py:409
  29.0 8.1 %collective-permute-start.3 = (bf16[48,2304]{1,0:T(8,128)(2,1)S(1)}, bf16[48,2304]{1,0:T(8,128)(2,1)S(1)}, u32[]{:S(2)}, u32[]{:S(2)}) collective-permute-start(bf16[48,2304]{1,0:T(8,128)(2,1)S(1)} %collective-permute-done.1.refs_4_), channel_id=1, source_target_pairs={{0,8},{8,16},{16,24},{24,0},{1,9},{9,17},{17,25},{25,1},{2,10},{10... | collective-permute-start | bytes 663560 | tf_op jit(solution)/shard_map/ppermute | solution.py:409
  40.6 7.5 %collective-permute-start.10 = (bf16[8,3456]{1,0:T(8,128)(2,1)S(1)}, bf16[8,3456]{1,0:T(8,128)(2,1)S(1)}, u32[]{:S(2)}, u32[]{:S(2)}) collective-permute-start(bf16[8,3456]{1,0:T(8,128)(2,1)S(1)} %get-tuple-element.44), channel_id=1, source_target_pairs={{0,5},{1,4},{2,7},{3,6},{4,1},{5,0},{6,3},{7,2},{8,13},{9,12},{10,... | collective-permute-start | bytes 165896 | tf_op jit(solution)/shard_map/ppermute | solution.py:423
  40.7 7.6 %collective-permute-start.11 = (bf16[8,3456]{1,0:T(8,128)(2,1)S(1)}, bf16[8,3456]{1,0:T(8,128)(2,1)S(1)}, u32[]{:S(2)}, u32[]{:S(2)}) collective-permute-start(bf16[8,3456]{1,0:T(8,128)(2,1)S(1)} %get-tuple-element.45), channel_id=1, source_target_pairs={{0,6},{1,7},{2,4},{3,5},{4,2},{5,3},{6,0},{7,1},{8,14},{9,15},{10,... | collective-permute-start | bytes 165896 | tf_op jit(solution)/shard_map/ppermute | solution.py:423
  45.2 4.5 %collective-permute-start.12 = (bf16[8,3456]{1,0:T(8,128)(2,1)S(1)}, bf16[8,3456]{1,0:T(8,128)(2,1)S(1)}, u32[]{:S(2)}, u32[]{:S(2)}) collective-permute-start(bf16[8,3456]{1,0:T(8,128)(2,1)S(1)} %get-tuple-element.46), channel_id=1, source_target_pairs={{0,7},{1,6},{2,5},{3,4},{4,3},{5,2},{6,1},{7,0},{8,15},{9,14},{10,... | collective-permute-start | bytes 165896 | tf_op jit(solution)/shard_map/ppermute | solution.py:423
  45.2 4.5 %collective-permute-start.6 = (bf16[8,3456]{1,0:T(8,128)(2,1)S(1)}, bf16[8,3456]{1,0:T(8,128)(2,1)S(1)}, u32[]{:S(2)}, u32[]{:S(2)}) collective-permute-start(bf16[8,3456]{1,0:T(8,128)(2,1)S(1)} %get-tuple-element.40), channel_id=1, source_target_pairs={{0,1},{1,0},{2,3},{3,2},{4,5},{5,4},{6,7},{7,6},{8,9},{9,8},{10,11... | collective-permute-start | bytes 165896 | tf_op jit(solution)/shard_map/ppermute | solution.py:423
  45.4 5.9 %collective-permute-start.7 = (bf16[8,3456]{1,0:T(8,128)(2,1)S(1)}, bf16[8,3456]{1,0:T(8,128)(2,1)S(1)}, u32[]{:S(2)}, u32[]{:S(2)}) collective-permute-start(bf16[8,3456]{1,0:T(8,128)(2,1)S(1)} %get-tuple-element.41), channel_id=1, source_target_pairs={{0,2},{1,3},{2,0},{3,1},{4,6},{5,7},{6,4},{7,5},{8,10},{9,11},{10,... | collective-permute-start | bytes 165896 | tf_op jit(solution)/shard_map/ppermute | solution.py:423
  48.1 4.0 %collective-permute-start.8 = (bf16[8,3456]{1,0:T(8,128)(2,1)S(1)}, bf16[8,3456]{1,0:T(8,128)(2,1)S(1)}, u32[]{:S(2)}, u32[]{:S(2)}) collective-permute-start(bf16[8,3456]{1,0:T(8,128)(2,1)S(1)} %get-tuple-element.42), channel_id=1, source_target_pairs={{0,3},{1,2},{2,1},{3,0},{4,7},{5,6},{6,5},{7,4},{8,11},{9,10},{10,... | collective-permute-start | bytes 165896 | tf_op jit(solution)/shard_map/ppermute | solution.py:423
  48.2 4.2 %collective-permute-start.9 = (bf16[8,3456]{1,0:T(8,128)(2,1)S(1)}, bf16[8,3456]{1,0:T(8,128)(2,1)S(1)}, u32[]{:S(2)}, u32[]{:S(2)}) collective-permute-start(bf16[8,3456]{1,0:T(8,128)(2,1)S(1)} %get-tuple-element.43), channel_id=1, source_target_pairs={{0,4},{1,5},{2,6},{3,7},{4,0},{5,1},{6,2},{7,3},{8,12},{9,13},{10,... | collective-permute-start | bytes 165896 | tf_op jit(solution)/shard_map/ppermute | solution.py:423
